TPU v7x, 512 devices: a whole 4x8x8 slice. The times are simulated.
512 devices in a mesh: section: 16 (over x, y_lo, core), dp: 32 (over z, y_hi).
Axes of the slice: x: 4, y: 8 (y_hi: 4, y_lo: 2; y = y_hi * 2 + y_lo), z: 8, core: 2. Of those that a mesh axis runs over, the one named last changes fastest.
Arguments:
- feedforward_entry_states: bfloat16 [16, 512, 32, 1152], P('section', 'dp'), may hold values from -6 to 6
- stored_hidden_preacts: bfloat16 [16, 512, 32, 2176], P('section', 'dp'), may hold values from -6 to 6
- layernorm_multiplier: float32 [16, 1152], P('section'), may hold values from 0.1 to 1.9
- expanding_projector: bfloat16 [16, 1152, 2176], P('section', 'dp'), may hold values from -0.1875 to 0.1875
- contracting_projector: bfloat16 [16, 2176, 1152], P('section', 'dp'), may hold values from -0.125 to 0.125
- caption_tower_outputs: bfloat16 [16, 512, 1152], P('section', 'dp'), may hold values from -6 to 6
- similarity_sharpness: float32 [1], replicated, may hold values from 4 to 12
- similarity_shift_term: float32 [1], replicated, may hold values from -3 to -1
- objective_upstream_grad: float32 [1], replicated, may hold values from 8 to 48
Outputs:
- prev_grad: bfloat16 [16, 512, 32, 1152], P('section', 'dp')
- text_grad: bfloat16 [16, 512, 1152], P('section', 'dp')
All inputs are finite; a program needn't handle non-finite values.
Results may differ from a plain program's by a relative error of at most 0.013.
Values may be sent and summed in bfloat16 or wider, within the bound.
No kernel may reach another device: no remote copies, remote signals or barrier semaphores. Data moves between devices by JAX's collectives and lax.ppermute only.
A program may use at most 128 MiB of HBM per device.

v0:
```python
import jax
import jax.numpy as jnp
from jax import lax
from jax.sharding import PartitionSpec as P

EPSILON = 1e-06
TANH_SCALE = 0.7978845608028654
CUBIC_TERM = 0.044715


def from_behind(array, axis, by):
    peers = lax.axis_size(axis)
    return lax.ppermute(array, axis, [(i, (i + by) % peers) for i in range(peers)])


def gelu_slope(preact):
    inner = TANH_SCALE * (preact + CUBIC_TERM * preact * preact * preact)
    tangent = jnp.tanh(inner)
    return 0.5 * (1.0 + tangent) + 0.5 * preact * (1.0 - tangent * tangent) * TANH_SCALE * (
        1.0 + 3.0 * CUBIC_TERM * preact * preact
    )


def unit_rows(values):
    inverse = lax.rsqrt(jnp.sum(values * values, axis=-1, keepdims=True) + EPSILON)
    return (values * inverse, inverse)


def pairwise_weight(
    image_normalized,
    text_normalized,
    image_index,
    text_index,
    smoothing_coefficient,
    logit_offset,
    weight_factor,
):
    pair_logits = (
        smoothing_coefficient
        * lax.dot_general(
            image_normalized,
            text_normalized,
            (((1,), (1,)), ((), ())),
            preferred_element_type=jnp.float32,
        )
        + logit_offset
    )
    signs = jnp.where(image_index[:, None] == text_index[None, :], 1.0, -1.0).astype(jnp.float32)
    return (weight_factor * -signs * jax.nn.sigmoid(-signs * pair_logits)).astype(jnp.bfloat16)


def norm_backward(tokens, normed_grad, layernorm_multiplier):
    centered = tokens - jnp.mean(tokens, axis=-1, keepdims=True)
    inverse = lax.rsqrt(jnp.mean(centered * centered, axis=-1, keepdims=True) + EPSILON)
    normal = centered * inverse
    scaled = normed_grad * layernorm_multiplier
    return inverse * (
        scaled
        - jnp.mean(scaled, axis=-1, keepdims=True)
        - normal * jnp.mean(scaled * normal, axis=-1, keepdims=True)
    )


def per_device(
    feedforward_entry_states,
    stored_hidden_preacts,
    layernorm_multiplier,
    expanding_projector,
    contracting_projector,
    caption_tower_outputs,
    similarity_sharpness,
    similarity_shift_term,
    objective_upstream_grad,
):
    images, patches, model_width = feedforward_entry_states.shape[1:]
    hidden = stored_hidden_preacts.shape[-1]
    tokens = feedforward_entry_states[0].reshape(images * patches, model_width).astype(jnp.float32)
    preact = stored_hidden_preacts[0].reshape(images * patches, hidden).astype(jnp.float32)
    activated = jax.nn.gelu(preact, approximate=True).astype(jnp.bfloat16)
    up_gathered, down_gathered = (
        lax.all_gather(expanding_projector, "dp", axis=1, tiled=True),
        lax.all_gather(contracting_projector, "dp", axis=1, tiled=True),
    )
    up_whole = up_gathered[0]
    down_whole = down_gathered[0]
    mlp_out = jnp.dot(activated, down_whole, preferred_element_type=jnp.float32)
    pooled = jnp.mean((tokens + mlp_out).reshape(images, patches, model_width), axis=1)
    image_dir, image_inverse = unit_rows(pooled)
    image_normalized = image_dir.astype(jnp.bfloat16)
    text_dir, text_inverse = unit_rows(caption_tower_outputs[0].astype(jnp.float32))
    text_normalized = text_dir.astype(jnp.bfloat16)
    position = lax.axis_index("dp")
    cycle_size = lax.axis_size("dp")
    image_index = position * images + lax.iota(jnp.int32, images)
    smoothing_coefficient = similarity_sharpness[0]
    logit_offset = similarity_shift_term[0]
    weight_factor = objective_upstream_grad[0] * smoothing_coefficient

    def weigh_block(present_value, text_index):
        return pairwise_weight(
            image_normalized,
            present_value,
            image_index,
            text_index,
            smoothing_coefficient,
            logit_offset,
            weight_factor,
        )

    def transposed(weight_array):
        return lax.dot_general(
            weight_array,
            image_normalized,
            (((0,), (0,)), ((), ())),
            preferred_element_type=jnp.float32,
        )

    zero_rows = jnp.zeros((images, model_width), jnp.float32)

    def pass_block(values):
        return from_behind(values, "dp", 1)

    def pass_partial(values):
        return from_behind(values, "dp", 1)

    def visit_block(rotation, carried):
        present_value, partial_value, image_sum = carried
        source = (position - rotation + cycle_size) % cycle_size
        weight_array = weigh_block(present_value, source * images + lax.iota(jnp.int32, images))
        image_sum = image_sum + jnp.dot(
            weight_array, present_value, preferred_element_type=jnp.float32
        )
        return (present_value, partial_value + transposed(weight_array), image_sum)

    def advance(rotation, carried):
        present_value, partial_value, image_sum = visit_block(rotation, carried)
        return (pass_block(present_value), pass_partial(partial_value), image_sum)

    carried = lax.fori_loop(0, cycle_size - 1, advance, (text_normalized, zero_rows, zero_rows))
    present_value, partial_value, image_sum = visit_block(cycle_size - 1, carried)
    text_sum = pass_partial(partial_value)
    text_grad = (
        (text_sum - text_dir * jnp.sum(text_dir * text_sum, axis=-1, keepdims=True)) * text_inverse
    ).astype(jnp.bfloat16)
    pooled_grad = (
        image_sum - image_dir * jnp.sum(image_dir * image_sum, axis=-1, keepdims=True)
    ) * image_inverse
    share = pooled_grad / patches
    token_grad = share.astype(jnp.bfloat16)
    hidden_grad = lax.dot_general(
        token_grad, down_whole, (((1,), (1,)), ((), ())), preferred_element_type=jnp.float32
    )
    slope = gelu_slope(preact).reshape(images, patches, hidden)
    preact_grad = (
        (hidden_grad[:, None, :] * slope).astype(jnp.bfloat16).reshape(images * patches, hidden)
    )
    normed_grad = lax.dot_general(
        preact_grad, up_whole, (((1,), (1,)), ((), ())), preferred_element_type=jnp.float32
    )
    inner_grad = norm_backward(tokens, normed_grad, layernorm_multiplier[0]).reshape(
        images, patches, model_width
    )
    span_grad = (share[:, None, :] + inner_grad).astype(jnp.bfloat16)
    prev_grad = from_behind(span_grad[None], "section", -1)
    return (prev_grad, text_grad[None])


def solution(mesh):
    placed = (
        P("section", "dp", None, None),
        P("section", "dp", None, None),
        P("section", None),
        P("section", "dp", None),
        P("section", "dp", None),
        P("section", "dp", None),
        P(),
        P(),
        P(),
    )
    return jax.shard_map(
        per_device,
        mesh=mesh,
        in_specs=placed,
        out_specs=(P("section", "dp", None, None), P("section", "dp", None)),
        check_vma=False,
    )
```

profile of v0, /device:TPU:6, one launch (start us, length us, event | category | flops | bytes accessed | tf_op | source)
XLA Modules:
  0.0 789.8 jit_solution(16796920198239645043)
XLA Ops:
  19.6 151.4 %all-gather.3.cloned.1.call-done = bf16[1,2176,1152]{2,0,1:T(2,128)(2,1)} async-done(((bf16[1,68,1152]{2,0,1:T(2,128)(2,1)}), bf16[1,2176,1152]{2,0,1:T(2,128)(2,1)}) %all-gather.3.cloned.1.call-update) | async-done | bytes 5013520 | tf_op jit(solution)/shard_map/all_gather | solution.py:82
  171.1 7.7 bitcast_reduce_fusion
  180.2 559.1 %while.20 = (s32[]{:T(128)}, bf16[16,1152]{1,0:T(8,128)(2,1)S(1)}, f32[16,1152]{1,0:T(8,128)S(1)}, f32[16,1152]{1,0:T(8,128)}, f32[]{:T(128)}, /*index=5*/s32[]{...) while((s32[]{:T(128)}, bf16[16,1152]{1,0:T(8,128)(2,1)S(1)}, ...), condition=%wide.region_4.5_spmd.clone, body=%wide.region_3.4_spmd.clone.sunk | while | flops 1827889 | bytes 962728 | solution.py:139
  180.4 4.5 collective-permute-start
  193.1 10.5 %collective-permute-done.1 = f32[16,1152]{1,0:T(8,128)S(1)} collective-permute-done((f32[16,1152]{1,0:T(8,128)}, f32[16,1152]{1,0:T(8,128)S(1)}, u32[]{:S(2)}, u32[]{:S(2)}) %collective-permute-start.1) | collective-permute-done | bytes 73760 | tf_op jit(solution)/shard_map/while/body/eval_jaxpr/ppermute | solution.py:13
  213.7 6.3 collective-permute-done.1
  230.5 6.1 collective-permute-done.1
  249.1 6.9 collective-permute-done.1
  265.4 3.1 collective-permute-done
  268.5 7.5 collective-permute-done.1
  285.3 3.4 collective-permute-done
  288.7 7.8 collective-permute-done.1
  305.8 3.2 collective-permute-done
  309.0 8.1 %collective-permute-done.1 = f32[16,1152]{1,0:T(8,128)S(1)} collective-permute-done((f32[16,1152]{1,0:T(8,128)}, f32[16,1152]{1,0:T(8,128)S(1)}, u32[]{:S(2)}, u32[]{:S(2)}) %collective-permute-start.1) | collective-permute-done | bytes 73760 | tf_op jit(solution)/shard_map/while/body/eval_jaxpr/ppermute | solution.py:13
  326.5 8.1 %collective-permute-done = bf16[16,1152]{1,0:T(8,128)(2,1)S(1)} collective-permute-done((bf16[16,1152]{1,0:T(8,128)(2,1)S(1)}, bf16[16,1152]{1,0:T(8,128)(2,1)S(1)}, u32[]{:S(2)}, u32[]{:S(2)}) %collective-permute-start) | collective-permute-done | bytes 36896 | tf_op jit(solution)/shard_map/while/body/eval_jaxpr/ppermute | solution.py:13
  334.6 3.2 collective-permute-done.1
  337.8 4.2 collective-permute-start
  345.8 3.1 collective-permute-start.1
  350.6 5.9 collective-permute-done.1
  362.2 3.4 collective-permute-start.1
  367.3 5.7 collective-permute-done.1
  378.7 3.7 collective-permute-start.1
  384.1 5.3 collective-permute-done.1
  399.9 6.0 collective-permute-done.1
  411.7 5.7 collective-permute-start.1
  419.0 3.3 collective-permute-done.1
  422.3 3.1 collective-permute-start
  429.3 7.3 collective-permute-start.1
  440.1 4.0 collective-permute-start
  448.0 6.3 collective-permute-start.1
  455.9 4.7 collective-permute-done.1
  466.4 5.8 collective-permute-start.1
  473.9 3.2 collective-permute-done.1
  484.0 6.2 collective-permute-start.1
  491.9 3.1 collective-permute-done.1
  495.0 3.1 collective-permute-start
  502.0 6.9 collective-permute-start.1
  512.8 4.3 collective-permute-start
  520.9 7.2 collective-permute-start.1
  531.6 4.0 collective-permute-start
  539.4 6.3 collective-permute-start.1
  556.9 5.3 collective-permute-start.1
  563.9 3.7 collective-permute-done.1
  573.4 4.3 collective-permute-start.1
  579.4 5.2 collective-permute-done.1
  590.4 3.3 collective-permute-start.1
  595.4 5.7 collective-permute-done.1
  611.2 6.4 collective-permute-done.1
  623.4 4.8 collective-permute-start.1
  629.9 4.3 collective-permute-done.1
  634.2 3.9 collective-permute-start
  641.9 6.6 collective-permute-start.1
  653.2 3.4 collective-permute-start
  660.5 6.3 collective-permute-start.1
  671.2 4.2 collective-permute-start
  679.2 3.4 collective-permute-start.1
  684.3 5.7 collective-permute-done.1
  700.0 6.4 collective-permute-done.1
  716.5 6.4 collective-permute-done.1
  732.9 6.4 collective-permute-done.1
  742.3 5.3 fusion.20
  747.6 4.0 fusion.31
  751.6 7.9 %fusion.68 = (f32[512]{0:T(512)S(1)}, f32[512]{0:T(512)S(1)}, f32[512,1152]{1,0:T(8,128)S(1)}) fusion(f32[512]{0:T(512)} %rsqrt.30, f32[512]{0:T(512)} %div.39, bf16[1,16,32,1152]{3,2,1,0:T(8,128)(2,1)S(1)} %copy-done, f32[1152]{0:T(1024)} %reduce.2, bf16[512,2176]{1,0:T(8,128)(2,1)} %bitcast.120, bf16[1,1152,2176]{2,0,1:T(2,128)(2,1)} %all-gather.5.cloned.1.call-done), kind=kOutput, calls=%fused_computation.96 | convolution fusion | flops 2571041792 | bytes 10793472 | tf_op jit(solution)/shard_map/dot_general | solution.py:157
  764.5 16.5 %collective-permute-done.3 = f32[16,1152]{1,0:T(8,128)S(1)} collective-permute-done((f32[16,1152]{1,0:T(8,128)S(1)}, f32[16,1152]{1,0:T(8,128)S(1)}, u32[]{:S(2)}, u32[]{:S(2)}) %collective-permute-start.3) | collective-permute-done | bytes 73760 | tf_op jit(solution)/shard_map/ppermute | solution.py:13
  (381 shorter events, 281.9 us)
Async XLA Ops:
  7.2 163.9 %all-gather.3.cloned.1.call-start = ((), (), s32[]{:S(2)}) async-start(), calls=%async_computation | async-start | bytes 10340352 | tf_op jit(solution)/shard_map/all_gather | solution.py:82
  9.3 742.3 %all-gather.5.cloned.1.call-start = ((), (), s32[]{:S(2)}) async-start(), calls=%async_computation.1 | async-start | bytes 10340352 | tf_op jit(solution)/shard_map/all_gather | solution.py:81
  180.4 12.7 %collective-permute-start = (bf16[16,1152]{1,0:T(8,128)(2,1)S(1)}, bf16[16,1152]{1,0:T(8,128)(2,1)S(1)}, u32[]{:S(2)}, u32[]{:S(2)}) collective-permute-start(bf16[16,1152]{1,0:T(8,128)(2,1)S(1)} %copy.40), channel_id=1, source_target_pairs={{0,1},{1,2},{2,3},{3,4},{4,5},{5,6},{6,7},{7,8},{8,9},{9,10},{10,1... | collective-permute-start | bytes 110600 | tf_op jit(solution)/shard_map/while/body/eval_jaxpr/ppermute | solution.py:13
  188.8 14.9 %collective-permute-start.1 = (f32[16,1152]{1,0:T(8,128)}, f32[16,1152]{1,0:T(8,128)S(1)}, u32[]{:S(2)}, u32[]{:S(2)}) collective-permute-start(f32[16,1152]{1,0:T(8,128)} %convolution_add_fusion.6), channel_id=1, source_target_pairs={{0,1},{1,2},{2,3},{3,4},{4,5},{5,6},{6,7},{7,8},{8,9},{9,10},{10,1... | collective-permute-start | bytes 221192 | tf_op jit(solution)/shard_map/while/body/eval_jaxpr/ppermute | solution.py:13
  203.6 10.1 %collective-permute-start = (bf16[16,1152]{1,0:T(8,128)(2,1)S(1)}, bf16[16,1152]{1,0:T(8,128)(2,1)S(1)}, u32[]{:S(2)}, u32[]{:S(2)}) collective-permute-start(bf16[16,1152]{1,0:T(8,128)(2,1)S(1)} %copy.40), channel_id=1, source_target_pairs={{0,1},{1,2},{2,3},{3,4},{4,5},{5,6},{6,7},{7,8},{8,9},{9,10},{10,1... | collective-permute-start | bytes 110600 | tf_op jit(solution)/shard_map/while/body/eval_jaxpr/ppermute | solution.py:13
  209.4 10.7 %collective-permute-start.1 = (f32[16,1152]{1,0:T(8,128)}, f32[16,1152]{1,0:T(8,128)S(1)}, u32[]{:S(2)}, u32[]{:S(2)}) collective-permute-start(f32[16,1152]{1,0:T(8,128)} %convolution_add_fusion.6), channel_id=1, source_target_pairs={{0,1},{1,2},{2,3},{3,4},{4,5},{5,6},{6,7},{7,8},{8,9},{9,10},{10,1... | collective-permute-start | bytes 221192 | tf_op jit(solution)/shard_map/while/body/eval_jaxpr/ppermute | solution.py:13
  220.1 10.5 %collective-permute-start = (bf16[16,1152]{1,0:T(8,128)(2,1)S(1)}, bf16[16,1152]{1,0:T(8,128)(2,1)S(1)}, u32[]{:S(2)}, u32[]{:S(2)}) collective-permute-start(bf16[16,1152]{1,0:T(8,128)(2,1)S(1)} %copy.40), channel_id=1, source_target_pairs={{0,1},{1,2},{2,3},{3,4},{4,5},{5,6},{6,7},{7,8},{8,9},{9,10},{10,1... | collective-permute-start | bytes 110600 | tf_op jit(solution)/shard_map/while/body/eval_jaxpr/ppermute | solution.py:13
  225.8 10.8 %collective-permute-start.1 = (f32[16,1152]{1,0:T(8,128)}, f32[16,1152]{1,0:T(8,128)S(1)}, u32[]{:S(2)}, u32[]{:S(2)}) collective-permute-start(f32[16,1152]{1,0:T(8,128)} %convolution_add_fusion.6), channel_id=1, source_target_pairs={{0,1},{1,2},{2,3},{3,4},{4,5},{5,6},{6,7},{7,8},{8,9},{9,10},{10,1... | collective-permute-start | bytes 221192 | tf_op jit(solution)/shard_map/while/body/eval_jaxpr/ppermute | solution.py:13
  236.6 12.5 %collective-permute-start = (bf16[16,1152]{1,0:T(8,128)(2,1)S(1)}, bf16[16,1152]{1,0:T(8,128)(2,1)S(1)}, u32[]{:S(2)}, u32[]{:S(2)}) collective-permute-start(bf16[16,1152]{1,0:T(8,128)(2,1)S(1)} %copy.40), channel_id=1, source_target_pairs={{0,1},{1,2},{2,3},{3,4},{4,5},{5,6},{6,7},{7,8},{8,9},{9,10},{10,1... | collective-permute-start | bytes 110600 | tf_op jit(solution)/shard_map/while/body/eval_jaxpr/ppermute | solution.py:13
  242.4 13.6 %collective-permute-start.1 = (f32[16,1152]{1,0:T(8,128)}, f32[16,1152]{1,0:T(8,128)S(1)}, u32[]{:S(2)}, u32[]{:S(2)}) collective-permute-start(f32[16,1152]{1,0:T(8,128)} %convolution_add_fusion.6), channel_id=1, source_target_pairs={{0,1},{1,2},{2,3},{3,4},{4,5},{5,6},{6,7},{7,8},{8,9},{9,10},{10,1... | collective-permute-start | bytes 221192 | tf_op jit(solution)/shard_map/while/body/eval_jaxpr/ppermute | solution.py:13
  256.0 12.5 %collective-permute-start = (bf16[16,1152]{1,0:T(8,128)(2,1)S(1)}, bf16[16,1152]{1,0:T(8,128)(2,1)S(1)}, u32[]{:S(2)}, u32[]{:S(2)}) collective-permute-start(bf16[16,1152]{1,0:T(8,128)(2,1)S(1)} %copy.40), channel_id=1, source_target_pairs={{0,1},{1,2},{2,3},{3,4},{4,5},{5,6},{6,7},{7,8},{8,9},{9,10},{10,1... | collective-permute-start | bytes 110600 | tf_op jit(solution)/shard_map/while/body/eval_jaxpr/ppermute | solution.py:13
  261.8 14.2 %collective-permute-start.1 = (f32[16,1152]{1,0:T(8,128)}, f32[16,1152]{1,0:T(8,128)S(1)}, u32[]{:S(2)}, u32[]{:S(2)}) collective-permute-start(f32[16,1152]{1,0:T(8,128)} %convolution_add_fusion.6), channel_id=1, source_target_pairs={{0,1},{1,2},{2,3},{3,4},{4,5},{5,6},{6,7},{7,8},{8,9},{9,10},{10,1... | collective-permute-start | bytes 221192 | tf_op jit(solution)/shard_map/while/body/eval_jaxpr/ppermute | solution.py:13
  275.9 12.7 %collective-permute-start = (bf16[16,1152]{1,0:T(8,128)(2,1)S(1)}, bf16[16,1152]{1,0:T(8,128)(2,1)S(1)}, u32[]{:S(2)}, u32[]{:S(2)}) collective-permute-start(bf16[16,1152]{1,0:T(8,128)(2,1)S(1)} %copy.40), channel_id=1, source_target_pairs={{0,1},{1,2},{2,3},{3,4},{4,5},{5,6},{6,7},{7,8},{8,9},{9,10},{10,1... | collective-permute-start | bytes 110600 | tf_op jit(solution)/shard_map/while/body/eval_jaxpr/ppermute | solution.py:13
  281.7 14.8 %collective-permute-start.1 = (f32[16,1152]{1,0:T(8,128)}, f32[16,1152]{1,0:T(8,128)S(1)}, u32[]{:S(2)}, u32[]{:S(2)}) collective-permute-start(f32[16,1152]{1,0:T(8,128)} %convolution_add_fusion.6), channel_id=1, source_target_pairs={{0,1},{1,2},{2,3},{3,4},{4,5},{5,6},{6,7},{7,8},{8,9},{9,10},{10,1... | collective-permute-start | bytes 221192 | tf_op jit(solution)/shard_map/while/body/eval_jaxpr/ppermute | solution.py:13
  296.5 12.6 %collective-permute-start = (bf16[16,1152]{1,0:T(8,128)(2,1)S(1)}, bf16[16,1152]{1,0:T(8,128)(2,1)S(1)}, u32[]{:S(2)}, u32[]{:S(2)}) collective-permute-start(bf16[16,1152]{1,0:T(8,128)(2,1)S(1)} %copy.40), channel_id=1, source_target_pairs={{0,1},{1,2},{2,3},{3,4},{4,5},{5,6},{6,7},{7,8},{8,9},{9,10},{10,1... | collective-permute-start | bytes 110600 | tf_op jit(solution)/shard_map/while/body/eval_jaxpr/ppermute | solution.py:13
  302.2 14.9 %collective-permute-start.1 = (f32[16,1152]{1,0:T(8,128)}, f32[16,1152]{1,0:T(8,128)S(1)}, u32[]{:S(2)}, u32[]{:S(2)}) collective-permute-start(f32[16,1152]{1,0:T(8,128)} %convolution_add_fusion.6), channel_id=1, source_target_pairs={{0,1},{1,2},{2,3},{3,4},{4,5},{5,6},{6,7},{7,8},{8,9},{9,10},{10,1... | collective-permute-start | bytes 221192 | tf_op jit(solution)/shard_map/while/body/eval_jaxpr/ppermute | solution.py:13
  317.1 17.4 %collective-permute-start = (bf16[16,1152]{1,0:T(8,128)(2,1)S(1)}, bf16[16,1152]{1,0:T(8,128)(2,1)S(1)}, u32[]{:S(2)}, u32[]{:S(2)}) collective-permute-start(bf16[16,1152]{1,0:T(8,128)(2,1)S(1)} %copy.40), channel_id=1, source_target_pairs={{0,1},{1,2},{2,3},{3,4},{4,5},{5,6},{6,7},{7,8},{8,9},{9,10},{10,1... | collective-permute-start | bytes 110600 | tf_op jit(solution)/shard_map/while/body/eval_jaxpr/ppermute | solution.py:13
  322.9 14.9 %collective-permute-start.1 = (f32[16,1152]{1,0:T(8,128)}, f32[16,1152]{1,0:T(8,128)S(1)}, u32[]{:S(2)}, u32[]{:S(2)}) collective-permute-start(f32[16,1152]{1,0:T(8,128)} %convolution_add_fusion.6), channel_id=1, source_target_pairs={{0,1},{1,2},{2,3},{3,4},{4,5},{5,6},{6,7},{7,8},{8,9},{9,10},{10,1... | collective-permute-start | bytes 221192 | tf_op jit(solution)/shard_map/while/body/eval_jaxpr/ppermute | solution.py:13
  337.8 12.8 %collective-permute-start = (bf16[16,1152]{1,0:T(8,128)(2,1)S(1)}, bf16[16,1152]{1,0:T(8,128)(2,1)S(1)}, u32[]{:S(2)}, u32[]{:S(2)}) collective-permute-start(bf16[16,1152]{1,0:T(8,128)(2,1)S(1)} %copy.40), channel_id=1, source_target_pairs={{0,1},{1,2},{2,3},{3,4},{4,5},{5,6},{6,7},{7,8},{8,9},{9,10},{10,1... | collective-permute-start | bytes 110600 | tf_op jit(solution)/shard_map/while/body/eval_jaxpr/ppermute | solution.py:13
  345.8 10.7 %collective-permute-start.1 = (f32[16,1152]{1,0:T(8,128)}, f32[16,1152]{1,0:T(8,128)S(1)}, u32[]{:S(2)}, u32[]{:S(2)}) collective-permute-start(f32[16,1152]{1,0:T(8,128)} %convolution_add_fusion.6), channel_id=1, source_target_pairs={{0,1},{1,2},{2,3},{3,4},{4,5},{5,6},{6,7},{7,8},{8,9},{9,10},{10,1... | collective-permute-start | bytes 221192 | tf_op jit(solution)/shard_map/while/body/eval_jaxpr/ppermute | solution.py:13
  356.5 10.8 %collective-permute-start = (bf16[16,1152]{1,0:T(8,128)(2,1)S(1)}, bf16[16,1152]{1,0:T(8,128)(2,1)S(1)}, u32[]{:S(2)}, u32[]{:S(2)}) collective-permute-start(bf16[16,1152]{1,0:T(8,128)(2,1)S(1)} %copy.40), channel_id=1, source_target_pairs={{0,1},{1,2},{2,3},{3,4},{4,5},{5,6},{6,7},{7,8},{8,9},{9,10},{10,1... | collective-permute-start | bytes 110600 | tf_op jit(solution)/shard_map/while/body/eval_jaxpr/ppermute | solution.py:13
  362.2 10.8 %collective-permute-start.1 = (f32[16,1152]{1,0:T(8,128)}, f32[16,1152]{1,0:T(8,128)S(1)}, u32[]{:S(2)}, u32[]{:S(2)}) collective-permute-start(f32[16,1152]{1,0:T(8,128)} %convolution_add_fusion.6), channel_id=1, source_target_pairs={{0,1},{1,2},{2,3},{3,4},{4,5},{5,6},{6,7},{7,8},{8,9},{9,10},{10,1... | collective-permute-start | bytes 221192 | tf_op jit(solution)/shard_map/while/body/eval_jaxpr/ppermute | solution.py:13
  373.0 11.1 %collective-permute-start = (bf16[16,1152]{1,0:T(8,128)(2,1)S(1)}, bf16[16,1152]{1,0:T(8,128)(2,1)S(1)}, u32[]{:S(2)}, u32[]{:S(2)}) collective-permute-start(bf16[16,1152]{1,0:T(8,128)(2,1)S(1)} %copy.40), channel_id=1, source_target_pairs={{0,1},{1,2},{2,3},{3,4},{4,5},{5,6},{6,7},{7,8},{8,9},{9,10},{10,1... | collective-permute-start | bytes 110600 | tf_op jit(solution)/shard_map/while/body/eval_jaxpr/ppermute | solution.py:13
  378.7 10.7 %collective-permute-start.1 = (f32[16,1152]{1,0:T(8,128)}, f32[16,1152]{1,0:T(8,128)S(1)}, u32[]{:S(2)}, u32[]{:S(2)}) collective-permute-start(f32[16,1152]{1,0:T(8,128)} %convolution_add_fusion.6), channel_id=1, source_target_pairs={{0,1},{1,2},{2,3},{3,4},{4,5},{5,6},{6,7},{7,8},{8,9},{9,10},{10,1... | collective-permute-start | bytes 221192 | tf_op jit(solution)/shard_map/while/body/eval_jaxpr/ppermute | solution.py:13
  389.5 10.4 %collective-permute-start = (bf16[16,1152]{1,0:T(8,128)(2,1)S(1)}, bf16[16,1152]{1,0:T(8,128)(2,1)S(1)}, u32[]{:S(2)}, u32[]{:S(2)}) collective-permute-start(bf16[16,1152]{1,0:T(8,128)(2,1)S(1)} %copy.40), channel_id=1, source_target_pairs={{0,1},{1,2},{2,3},{3,4},{4,5},{5,6},{6,7},{7,8},{8,9},{9,10},{10,1... | collective-permute-start | bytes 110600 | tf_op jit(solution)/shard_map/while/body/eval_jaxpr/ppermute | solution.py:13
  395.2 10.7 %collective-permute-start.1 = (f32[16,1152]{1,0:T(8,128)}, f32[16,1152]{1,0:T(8,128)S(1)}, u32[]{:S(2)}, u32[]{:S(2)}) collective-permute-start(f32[16,1152]{1,0:T(8,128)} %convolution_add_fusion.6), channel_id=1, source_target_pairs={{0,1},{1,2},{2,3},{3,4},{4,5},{5,6},{6,7},{7,8},{8,9},{9,10},{10,1... | collective-permute-start | bytes 221192 | tf_op jit(solution)/shard_map/while/body/eval_jaxpr/ppermute | solution.py:13
  405.9 13.1 %collective-permute-start = (bf16[16,1152]{1,0:T(8,128)(2,1)S(1)}, bf16[16,1152]{1,0:T(8,128)(2,1)S(1)}, u32[]{:S(2)}, u32[]{:S(2)}) collective-permute-start(bf16[16,1152]{1,0:T(8,128)(2,1)S(1)} %copy.40), channel_id=1, source_target_pairs={{0,1},{1,2},{2,3},{3,4},{4,5},{5,6},{6,7},{7,8},{8,9},{9,10},{10,1... | collective-permute-start | bytes 110600 | tf_op jit(solution)/shard_map/while/body/eval_jaxpr/ppermute | solution.py:13
  411.7 10.7 %collective-permute-start.1 = (f32[16,1152]{1,0:T(8,128)}, f32[16,1152]{1,0:T(8,128)S(1)}, u32[]{:S(2)}, u32[]{:S(2)}) collective-permute-start(f32[16,1152]{1,0:T(8,128)} %convolution_add_fusion.6), channel_id=1, source_target_pairs={{0,1},{1,2},{2,3},{3,4},{4,5},{5,6},{6,7},{7,8},{8,9},{9,10},{10,1... | collective-permute-start | bytes 221192 | tf_op jit(solution)/shard_map/while/body/eval_jaxpr/ppermute | solution.py:13
  422.3 16.0 %collective-permute-start = (bf16[16,1152]{1,0:T(8,128)(2,1)S(1)}, bf16[16,1152]{1,0:T(8,128)(2,1)S(1)}, u32[]{:S(2)}, u32[]{:S(2)}) collective-permute-start(bf16[16,1152]{1,0:T(8,128)(2,1)S(1)} %copy.40), channel_id=1, source_target_pairs={{0,1},{1,2},{2,3},{3,4},{4,5},{5,6},{6,7},{7,8},{8,9},{9,10},{10,1... | collective-permute-start | bytes 110600 | tf_op jit(solution)/shard_map/while/body/eval_jaxpr/ppermute | solution.py:13
  429.3 10.8 %collective-permute-start.1 = (f32[16,1152]{1,0:T(8,128)}, f32[16,1152]{1,0:T(8,128)S(1)}, u32[]{:S(2)}, u32[]{:S(2)}) collective-permute-start(f32[16,1152]{1,0:T(8,128)} %convolution_add_fusion.6), channel_id=1, source_target_pairs={{0,1},{1,2},{2,3},{3,4},{4,5},{5,6},{6,7},{7,8},{8,9},{9,10},{10,1... | collective-permute-start | bytes 221192 | tf_op jit(solution)/shard_map/while/body/eval_jaxpr/ppermute | solution.py:13
  440.1 15.8 %collective-permute-start = (bf16[16,1152]{1,0:T(8,128)(2,1)S(1)}, bf16[16,1152]{1,0:T(8,128)(2,1)S(1)}, u32[]{:S(2)}, u32[]{:S(2)}) collective-permute-start(bf16[16,1152]{1,0:T(8,128)(2,1)S(1)} %copy.40), channel_id=1, source_target_pairs={{0,1},{1,2},{2,3},{3,4},{4,5},{5,6},{6,7},{7,8},{8,9},{9,10},{10,1... | collective-permute-start | bytes 110600 | tf_op jit(solution)/shard_map/while/body/eval_jaxpr/ppermute | solution.py:13
  448.0 12.6 %collective-permute-start.1 = (f32[16,1152]{1,0:T(8,128)}, f32[16,1152]{1,0:T(8,128)S(1)}, u32[]{:S(2)}, u32[]{:S(2)}) collective-permute-start(f32[16,1152]{1,0:T(8,128)} %convolution_add_fusion.6), channel_id=1, source_target_pairs={{0,1},{1,2},{2,3},{3,4},{4,5},{5,6},{6,7},{7,8},{8,9},{9,10},{10,1... | collective-permute-start | bytes 221192 | tf_op jit(solution)/shard_map/while/body/eval_jaxpr/ppermute | solution.py:13
  460.6 13.3 %collective-permute-start = (bf16[16,1152]{1,0:T(8,128)(2,1)S(1)}, bf16[16,1152]{1,0:T(8,128)(2,1)S(1)}, u32[]{:S(2)}, u32[]{:S(2)}) collective-permute-start(bf16[16,1152]{1,0:T(8,128)(2,1)S(1)} %copy.40), channel_id=1, source_target_pairs={{0,1},{1,2},{2,3},{3,4},{4,5},{5,6},{6,7},{7,8},{8,9},{9,10},{10,1... | collective-permute-start | bytes 110600 | tf_op jit(solution)/shard_map/while/body/eval_jaxpr/ppermute | solution.py:13
  466.4 10.7 %collective-permute-start.1 = (f32[16,1152]{1,0:T(8,128)}, f32[16,1152]{1,0:T(8,128)S(1)}, u32[]{:S(2)}, u32[]{:S(2)}) collective-permute-start(f32[16,1152]{1,0:T(8,128)} %convolution_add_fusion.6), channel_id=1, source_target_pairs={{0,1},{1,2},{2,3},{3,4},{4,5},{5,6},{6,7},{7,8},{8,9},{9,10},{10,1... | collective-permute-start | bytes 221192 | tf_op jit(solution)/shard_map/while/body/eval_jaxpr/ppermute | solution.py:13
  477.0 14.9 %collective-permute-start = (bf16[16,1152]{1,0:T(8,128)(2,1)S(1)}, bf16[16,1152]{1,0:T(8,128)(2,1)S(1)}, u32[]{:S(2)}, u32[]{:S(2)}) collective-permute-start(bf16[16,1152]{1,0:T(8,128)(2,1)S(1)} %copy.40), channel_id=1, source_target_pairs={{0,1},{1,2},{2,3},{3,4},{4,5},{5,6},{6,7},{7,8},{8,9},{9,10},{10,1... | collective-permute-start | bytes 110600 | tf_op jit(solution)/shard_map/while/body/eval_jaxpr/ppermute | solution.py:13
  484.0 11.1 %collective-permute-start.1 = (f32[16,1152]{1,0:T(8,128)}, f32[16,1152]{1,0:T(8,128)S(1)}, u32[]{:S(2)}, u32[]{:S(2)}) collective-permute-start(f32[16,1152]{1,0:T(8,128)} %convolution_add_fusion.6), channel_id=1, source_target_pairs={{0,1},{1,2},{2,3},{3,4},{4,5},{5,6},{6,7},{7,8},{8,9},{9,10},{10,1... | collective-permute-start | bytes 221192 | tf_op jit(solution)/shard_map/while/body/eval_jaxpr/ppermute | solution.py:13
  495.0 15.5 %collective-permute-start = (bf16[16,1152]{1,0:T(8,128)(2,1)S(1)}, bf16[16,1152]{1,0:T(8,128)(2,1)S(1)}, u32[]{:S(2)}, u32[]{:S(2)}) collective-permute-start(bf16[16,1152]{1,0:T(8,128)(2,1)S(1)} %copy.40), channel_id=1, source_target_pairs={{0,1},{1,2},{2,3},{3,4},{4,5},{5,6},{6,7},{7,8},{8,9},{9,10},{10,1... | collective-permute-start | bytes 110600 | tf_op jit(solution)/shard_map/while/body/eval_jaxpr/ppermute | solution.py:13
  502.0 10.8 %collective-permute-start.1 = (f32[16,1152]{1,0:T(8,128)}, f32[16,1152]{1,0:T(8,128)S(1)}, u32[]{:S(2)}, u32[]{:S(2)}) collective-permute-start(f32[16,1152]{1,0:T(8,128)} %convolution_add_fusion.6), channel_id=1, source_target_pairs={{0,1},{1,2},{2,3},{3,4},{4,5},{5,6},{6,7},{7,8},{8,9},{9,10},{10,1... | collective-permute-start | bytes 221192 | tf_op jit(solution)/shard_map/while/body/eval_jaxpr/ppermute | solution.py:13
  512.8 17.0 %collective-permute-start = (bf16[16,1152]{1,0:T(8,128)(2,1)S(1)}, bf16[16,1152]{1,0:T(8,128)(2,1)S(1)}, u32[]{:S(2)}, u32[]{:S(2)}) collective-permute-start(bf16[16,1152]{1,0:T(8,128)(2,1)S(1)} %copy.40), channel_id=1, source_target_pairs={{0,1},{1,2},{2,3},{3,4},{4,5},{5,6},{6,7},{7,8},{8,9},{9,10},{10,1... | collective-permute-start | bytes 110600 | tf_op jit(solution)/shard_map/while/body/eval_jaxpr/ppermute | solution.py:13
  520.9 10.7 %collective-permute-start.1 = (f32[16,1152]{1,0:T(8,128)}, f32[16,1152]{1,0:T(8,128)S(1)}, u32[]{:S(2)}, u32[]{:S(2)}) collective-permute-start(f32[16,1152]{1,0:T(8,128)} %convolution_add_fusion.6), channel_id=1, source_target_pairs={{0,1},{1,2},{2,3},{3,4},{4,5},{5,6},{6,7},{7,8},{8,9},{9,10},{10,1... | collective-permute-start | bytes 221192 | tf_op jit(solution)/shard_map/while/body/eval_jaxpr/ppermute | solution.py:13
  531.6 15.8 %collective-permute-start = (bf16[16,1152]{1,0:T(8,128)(2,1)S(1)}, bf16[16,1152]{1,0:T(8,128)(2,1)S(1)}, u32[]{:S(2)}, u32[]{:S(2)}) collective-permute-start(bf16[16,1152]{1,0:T(8,128)(2,1)S(1)} %copy.40), channel_id=1, source_target_pairs={{0,1},{1,2},{2,3},{3,4},{4,5},{5,6},{6,7},{7,8},{8,9},{9,10},{10,1... | collective-permute-start | bytes 110600 | tf_op jit(solution)/shard_map/while/body/eval_jaxpr/ppermute | solution.py:13
  539.4 10.8 %collective-permute-start.1 = (f32[16,1152]{1,0:T(8,128)}, f32[16,1152]{1,0:T(8,128)S(1)}, u32[]{:S(2)}, u32[]{:S(2)}) collective-permute-start(f32[16,1152]{1,0:T(8,128)} %convolution_add_fusion.6), channel_id=1, source_target_pairs={{0,1},{1,2},{2,3},{3,4},{4,5},{5,6},{6,7},{7,8},{8,9},{9,10},{10,1... | collective-permute-start | bytes 221192 | tf_op jit(solution)/shard_map/while/body/eval_jaxpr/ppermute | solution.py:13
  550.2 13.7 %collective-permute-start = (bf16[16,1152]{1,0:T(8,128)(2,1)S(1)}, bf16[16,1152]{1,0:T(8,128)(2,1)S(1)}, u32[]{:S(2)}, u32[]{:S(2)}) collective-permute-start(bf16[16,1152]{1,0:T(8,128)(2,1)S(1)} %copy.40), channel_id=1, source_target_pairs={{0,1},{1,2},{2,3},{3,4},{4,5},{5,6},{6,7},{7,8},{8,9},{9,10},{10,1... | collective-permute-start | bytes 110600 | tf_op jit(solution)/shard_map/while/body/eval_jaxpr/ppermute | solution.py:13
  556.9 10.7 %collective-permute-start.1 = (f32[16,1152]{1,0:T(8,128)}, f32[16,1152]{1,0:T(8,128)S(1)}, u32[]{:S(2)}, u32[]{:S(2)}) collective-permute-start(f32[16,1152]{1,0:T(8,128)} %convolution_add_fusion.6), channel_id=1, source_target_pairs={{0,1},{1,2},{2,3},{3,4},{4,5},{5,6},{6,7},{7,8},{8,9},{9,10},{10,1... | collective-permute-start | bytes 221192 | tf_op jit(solution)/shard_map/while/body/eval_jaxpr/ppermute | solution.py:13
  567.6 11.9 %collective-permute-start = (bf16[16,1152]{1,0:T(8,128)(2,1)S(1)}, bf16[16,1152]{1,0:T(8,128)(2,1)S(1)}, u32[]{:S(2)}, u32[]{:S(2)}) collective-permute-start(bf16[16,1152]{1,0:T(8,128)(2,1)S(1)} %copy.40), channel_id=1, source_target_pairs={{0,1},{1,2},{2,3},{3,4},{4,5},{5,6},{6,7},{7,8},{8,9},{9,10},{10,1... | collective-permute-start | bytes 110600 | tf_op jit(solution)/shard_map/while/body/eval_jaxpr/ppermute | solution.py:13
  573.4 11.2 %collective-permute-start.1 = (f32[16,1152]{1,0:T(8,128)}, f32[16,1152]{1,0:T(8,128)S(1)}, u32[]{:S(2)}, u32[]{:S(2)}) collective-permute-start(f32[16,1152]{1,0:T(8,128)} %convolution_add_fusion.6), channel_id=1, source_target_pairs={{0,1},{1,2},{2,3},{3,4},{4,5},{5,6},{6,7},{7,8},{8,9},{9,10},{10,1... | collective-permute-start | bytes 221192 | tf_op jit(solution)/shard_map/while/body/eval_jaxpr/ppermute | solution.py:13
  584.7 10.7 %collective-permute-start = (bf16[16,1152]{1,0:T(8,128)(2,1)S(1)}, bf16[16,1152]{1,0:T(8,128)(2,1)S(1)}, u32[]{:S(2)}, u32[]{:S(2)}) collective-permute-start(bf16[16,1152]{1,0:T(8,128)(2,1)S(1)} %copy.40), channel_id=1, source_target_pairs={{0,1},{1,2},{2,3},{3,4},{4,5},{5,6},{6,7},{7,8},{8,9},{9,10},{10,1... | collective-permute-start | bytes 110600 | tf_op jit(solution)/shard_map/while/body/eval_jaxpr/ppermute | solution.py:13
  590.4 10.7 %collective-permute-start.1 = (f32[16,1152]{1,0:T(8,128)}, f32[16,1152]{1,0:T(8,128)S(1)}, u32[]{:S(2)}, u32[]{:S(2)}) collective-permute-start(f32[16,1152]{1,0:T(8,128)} %convolution_add_fusion.6), channel_id=1, source_target_pairs={{0,1},{1,2},{2,3},{3,4},{4,5},{5,6},{6,7},{7,8},{8,9},{9,10},{10,1... | collective-permute-start | bytes 221192 | tf_op jit(solution)/shard_map/while/body/eval_jaxpr/ppermute | solution.py:13
  601.1 10.1 %collective-permute-start = (bf16[16,1152]{1,0:T(8,128)(2,1)S(1)}, bf16[16,1152]{1,0:T(8,128)(2,1)S(1)}, u32[]{:S(2)}, u32[]{:S(2)}) collective-permute-start(bf16[16,1152]{1,0:T(8,128)(2,1)S(1)} %copy.40), channel_id=1, source_target_pairs={{0,1},{1,2},{2,3},{3,4},{4,5},{5,6},{6,7},{7,8},{8,9},{9,10},{10,1... | collective-permute-start | bytes 110600 | tf_op jit(solution)/shard_map/while/body/eval_jaxpr/ppermute | solution.py:13
  606.9 10.8 %collective-permute-start.1 = (f32[16,1152]{1,0:T(8,128)}, f32[16,1152]{1,0:T(8,128)S(1)}, u32[]{:S(2)}, u32[]{:S(2)}) collective-permute-start(f32[16,1152]{1,0:T(8,128)} %convolution_add_fusion.6), channel_id=1, source_target_pairs={{0,1},{1,2},{2,3},{3,4},{4,5},{5,6},{6,7},{7,8},{8,9},{9,10},{10,1... | collective-permute-start | bytes 221192 | tf_op jit(solution)/shard_map/while/body/eval_jaxpr/ppermute | solution.py:13
  617.6 12.3 %collective-permute-start = (bf16[16,1152]{1,0:T(8,128)(2,1)S(1)}, bf16[16,1152]{1,0:T(8,128)(2,1)S(1)}, u32[]{:S(2)}, u32[]{:S(2)}) collective-permute-start(bf16[16,1152]{1,0:T(8,128)(2,1)S(1)} %copy.40), channel_id=1, source_target_pairs={{0,1},{1,2},{2,3},{3,4},{4,5},{5,6},{6,7},{7,8},{8,9},{9,10},{10,1... | collective-permute-start | bytes 110600 | tf_op jit(solution)/shard_map/while/body/eval_jaxpr/ppermute | solution.py:13
  623.4 10.8 %collective-permute-start.1 = (f32[16,1152]{1,0:T(8,128)}, f32[16,1152]{1,0:T(8,128)S(1)}, u32[]{:S(2)}, u32[]{:S(2)}) collective-permute-start(f32[16,1152]{1,0:T(8,128)} %convolution_add_fusion.6), channel_id=1, source_target_pairs={{0,1},{1,2},{2,3},{3,4},{4,5},{5,6},{6,7},{7,8},{8,9},{9,10},{10,1... | collective-permute-start | bytes 221192 | tf_op jit(solution)/shard_map/while/body/eval_jaxpr/ppermute | solution.py:13
  634.2 16.0 %collective-permute-start = (bf16[16,1152]{1,0:T(8,128)(2,1)S(1)}, bf16[16,1152]{1,0:T(8,128)(2,1)S(1)}, u32[]{:S(2)}, u32[]{:S(2)}) collective-permute-start(bf16[16,1152]{1,0:T(8,128)(2,1)S(1)} %copy.40), channel_id=1, source_target_pairs={{0,1},{1,2},{2,3},{3,4},{4,5},{5,6},{6,7},{7,8},{8,9},{9,10},{10,1... | collective-permute-start | bytes 110600 | tf_op jit(solution)/shard_map/while/body/eval_jaxpr/ppermute | solution.py:13
  641.9 11.3 %collective-permute-start.1 = (f32[16,1152]{1,0:T(8,128)}, f32[16,1152]{1,0:T(8,128)S(1)}, u32[]{:S(2)}, u32[]{:S(2)}) collective-permute-start(f32[16,1152]{1,0:T(8,128)} %convolution_add_fusion.6), channel_id=1, source_target_pairs={{0,1},{1,2},{2,3},{3,4},{4,5},{5,6},{6,7},{7,8},{8,9},{9,10},{10,1... | collective-permute-start | bytes 221192 | tf_op jit(solution)/shard_map/while/body/eval_jaxpr/ppermute | solution.py:13
  653.2 15.3 %collective-permute-start = (bf16[16,1152]{1,0:T(8,128)(2,1)S(1)}, bf16[16,1152]{1,0:T(8,128)(2,1)S(1)}, u32[]{:S(2)}, u32[]{:S(2)}) collective-permute-start(bf16[16,1152]{1,0:T(8,128)(2,1)S(1)} %copy.40), channel_id=1, source_target_pairs={{0,1},{1,2},{2,3},{3,4},{4,5},{5,6},{6,7},{7,8},{8,9},{9,10},{10,1... | collective-permute-start | bytes 110600 | tf_op jit(solution)/shard_map/while/body/eval_jaxpr/ppermute | solution.py:13
  660.5 10.7 %collective-permute-start.1 = (f32[16,1152]{1,0:T(8,128)}, f32[16,1152]{1,0:T(8,128)S(1)}, u32[]{:S(2)}, u32[]{:S(2)}) collective-permute-start(f32[16,1152]{1,0:T(8,128)} %convolution_add_fusion.6), channel_id=1, source_target_pairs={{0,1},{1,2},{2,3},{3,4},{4,5},{5,6},{6,7},{7,8},{8,9},{9,10},{10,1... | collective-permute-start | bytes 221192 | tf_op jit(solution)/shard_map/while/body/eval_jaxpr/ppermute | solution.py:13
  671.2 13.1 %collective-permute-start = (bf16[16,1152]{1,0:T(8,128)(2,1)S(1)}, bf16[16,1152]{1,0:T(8,128)(2,1)S(1)}, u32[]{:S(2)}, u32[]{:S(2)}) collective-permute-start(bf16[16,1152]{1,0:T(8,128)(2,1)S(1)} %copy.40), channel_id=1, source_target_pairs={{0,1},{1,2},{2,3},{3,4},{4,5},{5,6},{6,7},{7,8},{8,9},{9,10},{10,1... | collective-permute-start | bytes 110600 | tf_op jit(solution)/shard_map/while/body/eval_jaxpr/ppermute | solution.py:13
  679.2 10.8 %collective-permute-start.1 = (f32[16,1152]{1,0:T(8,128)}, f32[16,1152]{1,0:T(8,128)S(1)}, u32[]{:S(2)}, u32[]{:S(2)}) collective-permute-start(f32[16,1152]{1,0:T(8,128)} %convolution_add_fusion.6), channel_id=1, source_target_pairs={{0,1},{1,2},{2,3},{3,4},{4,5},{5,6},{6,7},{7,8},{8,9},{9,10},{10,1... | collective-permute-start | bytes 221192 | tf_op jit(solution)/shard_map/while/body/eval_jaxpr/ppermute | solution.py:13
  695.7 10.7 %collective-permute-start.1 = (f32[16,1152]{1,0:T(8,128)}, f32[16,1152]{1,0:T(8,128)S(1)}, u32[]{:S(2)}, u32[]{:S(2)}) collective-permute-start(f32[16,1152]{1,0:T(8,128)} %convolution_add_fusion.6), channel_id=1, source_target_pairs={{0,1},{1,2},{2,3},{3,4},{4,5},{5,6},{6,7},{7,8},{8,9},{9,10},{10,1... | collective-permute-start | bytes 221192 | tf_op jit(solution)/shard_map/while/body/eval_jaxpr/ppermute | solution.py:13
  712.2 10.7 %collective-permute-start.1 = (f32[16,1152]{1,0:T(8,128)}, f32[16,1152]{1,0:T(8,128)S(1)}, u32[]{:S(2)}, u32[]{:S(2)}) collective-permute-start(f32[16,1152]{1,0:T(8,128)} %convolution_add_fusion.6), channel_id=1, source_target_pairs={{0,1},{1,2},{2,3},{3,4},{4,5},{5,6},{6,7},{7,8},{8,9},{9,10},{10,1... | collective-permute-start | bytes 221192 | tf_op jit(solution)/shard_map/while/body/eval_jaxpr/ppermute | solution.py:13
  722.8 10.1 %collective-permute-start = (bf16[16,1152]{1,0:T(8,128)(2,1)S(1)}, bf16[16,1152]{1,0:T(8,128)(2,1)S(1)}, u32[]{:S(2)}, u32[]{:S(2)}) collective-permute-start(bf16[16,1152]{1,0:T(8,128)(2,1)S(1)} %copy.40), channel_id=1, source_target_pairs={{0,1},{1,2},{2,3},{3,4},{4,5},{5,6},{6,7},{7,8},{8,9},{9,10},{10,1... | collective-permute-start | bytes 110600 | tf_op jit(solution)/shard_map/while/body/eval_jaxpr/ppermute | solution.py:13
  728.6 10.7 %collective-permute-start.1 = (f32[16,1152]{1,0:T(8,128)}, f32[16,1152]{1,0:T(8,128)S(1)}, u32[]{:S(2)}, u32[]{:S(2)}) collective-permute-start(f32[16,1152]{1,0:T(8,128)} %convolution_add_fusion.6), channel_id=1, source_target_pairs={{0,1},{1,2},{2,3},{3,4},{4,5},{5,6},{6,7},{7,8},{8,9},{9,10},{10,1... | collective-permute-start | bytes 221192 | tf_op jit(solution)/shard_map/while/body/eval_jaxpr/ppermute | solution.py:13
  760.5 21.5 %collective-permute-start.2 = (bf16[1,16,32,1152]{3,2,1,0:T(8,128)(2,1)S(1)}, bf16[1,16,32,1152]{3,2,1,0:T(8,128)(2,1)S(1)}, u32[]{:S(2)}, u32[]{:S(2)}) collective-permute-start(bf16[1,16,32,1152]{3,2,1,0:T(8,128)(2,1)S(1)} %add_convert_fusion), channel_id=1, source_target_pairs={{0,480},{32,0},{64,32},{96,64},{128,96},{160,128},{192,160},{224,1... | collective-permute-start | bytes 3538952 | tf_op jit(solution)/shard_map/ppermute | solution.py:13
  762.6 18.4 %collective-permute-start.3 = (f32[16,1152]{1,0:T(8,128)S(1)}, f32[16,1152]{1,0:T(8,128)S(1)}, u32[]{:S(2)}, u32[]{:S(2)}) collective-permute-start(f32[16,1152]{1,0:T(8,128)S(1)} %convolution_add_fusion.2), channel_id=1, source_target_pairs={{0,1},{1,2},{2,3},{3,4},{4,5},{5,6},{6,7},{7,8},{8,9},{9,10},{10,1... | collective-permute-start | bytes 221192 | tf_op jit(solution)/shard_map/ppermute | solution.py:13
  (47 other events, 317.8 us)
Sparse Core Ops, SparseCore 0:
  11.8 159.2 all-gather.2
  174.2 175.7 all-gather.4
where the time goes:
time: 798 us; the launch traced here: 790 us
  waiting for transfers between devices  349 us (44%)
  starting transfers between devices  210 us (26%)
  matrix products  191 us (24%)
  between operations  16.2 us (2%)
  other arithmetic  13.5 us (2%)
    ppermute x64, starting transfers between devices, from_behind(): lax.ppermute(array, axis, [(i, (i + by) % peers) for i in range(peers)])  210 us
    ppermute x64, waiting for transfers between devices, from_behind(): lax.ppermute(array, axis, [(i, (i + by) % peers) for i in range(peers)])  198 us
    all_gather x1, waiting for transfers between devices, per_device(): lax.all_gather(contracting_projector, 'dp', axis=1, tiled=True)  151 us
    dot_general x32, matrix products, pairwise_weight(): lax.dot_general(image_normalized, text_normalized, (((1,), (1,)), ((), ()...  69.1 us
    dot_general x32, matrix products, visit_block(): jnp.dot(weight_array, present_value, preferred_element_type=jnp.float32)  52.3 us
    dot_general x32, matrix products, transposed(): lax.dot_general(weight_array, image_normalized, (((0,), (0,)), ((), ())),...  49 us
  transfers between devices with their start and end apart: 66, of which 43 were waited for; matrix products, arithmetic and copies ran while one was open for 25% of the time, Pallas kernels for 0%

commit v1 on v0

v1 whole, which is shorter than its diff:
```python
import jax
import jax.numpy as jnp
from jax import lax
from jax.sharding import Mesh, PartitionSpec as P

EPSILON = 1e-06
TANH_SCALE = 0.7978845608028654
CUBIC_TERM = 0.044715
Y_SHARDS = 4


def from_ahead(array, axis, by):
    peers = lax.axis_size(axis)
    return lax.ppermute(array, axis, [((i + by) % peers, i) for i in range(peers)])


def gelu_slope(preact):
    inner = TANH_SCALE * (preact + CUBIC_TERM * preact * preact * preact)
    tangent = jnp.tanh(inner)
    return 0.5 * (1.0 + tangent) + 0.5 * preact * (1.0 - tangent * tangent) * TANH_SCALE * (
        1.0 + 3.0 * CUBIC_TERM * preact * preact
    )


def unit_rows(values):
    inverse = lax.rsqrt(jnp.sum(values * values, axis=-1, keepdims=True) + EPSILON)
    return (values * inverse, inverse)


def pair_weights(image_unit, text_unit, image_index, text_index, sharpness, shift, factor):
    logits = (
        sharpness
        * lax.dot_general(
            image_unit, text_unit, (((1,), (1,)), ((), ())), preferred_element_type=jnp.float32
        )
        + shift
    )
    signs = jnp.where(image_index[:, None] == text_index[None, :], 1.0, -1.0).astype(jnp.float32)
    return (factor * -signs * jax.nn.sigmoid(-signs * logits)).astype(jnp.bfloat16)


def norm_backward(tokens, normed_grad, layernorm_multiplier):
    centered = tokens - jnp.mean(tokens, axis=-1, keepdims=True)
    inverse = lax.rsqrt(jnp.mean(centered * centered, axis=-1, keepdims=True) + EPSILON)
    normal = centered * inverse
    scaled = normed_grad * layernorm_multiplier
    return inverse * (
        scaled
        - jnp.mean(scaled, axis=-1, keepdims=True)
        - normal * jnp.mean(scaled * normal, axis=-1, keepdims=True)
    )


def exchange_z(blocks):
    return lax.all_to_all(blocks, "z", 0, 0)


def gather_y(shard, y):
    ahead = [shard] + [from_ahead(shard, "y", k) for k in range(1, Y_SHARDS)]
    placed = [
        lax.select_n(y, *[ahead[(a - own) % Y_SHARDS] for own in range(Y_SHARDS)])
        for a in range(Y_SHARDS)
    ]
    return jnp.concatenate(placed, axis=0)


def per_device(
    feedforward_entry_states,
    stored_hidden_preacts,
    layernorm_multiplier,
    expanding_projector,
    contracting_projector,
    caption_tower_outputs,
    similarity_sharpness,
    similarity_shift_term,
    objective_upstream_grad,
):
    images, patches, model_width = feedforward_entry_states.shape[1:]
    hidden = stored_hidden_preacts.shape[-1]
    z, y = lax.axis_index("z"), lax.axis_index("y")
    z_size = lax.axis_size("z")
    part = hidden // z_size
    column = images * z_size
    sharpness = similarity_sharpness[0]
    shift = similarity_shift_term[0]
    factor = objective_upstream_grad[0] * sharpness

    up_y = gather_y(expanding_projector[0], y)
    up_whole = lax.all_gather(up_y, "z", axis=0, tiled=True)
    down_y = gather_y(contracting_projector[0], y)

    tokens = feedforward_entry_states[0].reshape(images * patches, model_width).astype(jnp.float32)
    preact = stored_hidden_preacts[0].astype(jnp.float32)
    activated = jax.nn.gelu(preact, approximate=True).astype(jnp.bfloat16).astype(jnp.float32)
    mean_activated = jnp.mean(activated, axis=1)
    mean_high = mean_activated.astype(jnp.bfloat16)
    mean_low = (mean_activated - mean_high.astype(jnp.float32)).astype(jnp.bfloat16)
    mean_tokens = jnp.mean(tokens.reshape(images, patches, model_width), axis=1)

    text_dir, text_inverse = unit_rows(caption_tower_outputs[0].astype(jnp.float32))
    text_unit = text_dir.astype(jnp.bfloat16)

    def by_z(values):
        return values.reshape(images, z_size, part).transpose(1, 0, 2).reshape(z_size, images * part)

    first = exchange_z(
        jnp.concatenate(
            [
                by_z(mean_high),
                by_z(mean_low),
                jnp.broadcast_to(text_unit.reshape(1, -1), (z_size, images * model_width)),
            ],
            axis=1,
        )
    )
    cut = images * part
    column_high = first[:, :cut].reshape(column, part)
    column_low = first[:, cut : 2 * cut].reshape(column, part)
    column_text = first[:, 2 * cut :].reshape(column, model_width)
    text_all = jnp.concatenate(
        [column_text] + [from_ahead(column_text, "y", k) for k in range(1, Y_SHARDS)], axis=0
    )

    partial = jnp.dot(column_high, down_y, preferred_element_type=jnp.float32) + jnp.dot(
        column_low, down_y, preferred_element_type=jnp.float32
    )
    partials = exchange_z(partial.astype(jnp.bfloat16).reshape(z_size, images, model_width))
    pooled = mean_tokens + jnp.sum(partials.astype(jnp.float32), axis=0)
    image_dir, image_inverse = unit_rows(pooled)
    image_unit = image_dir.astype(jnp.bfloat16)

    def index_of(z_index, y_index):
        start = (z_index * Y_SHARDS + y_index % Y_SHARDS) * images
        return start[..., None] + lax.iota(jnp.int32, images)

    text_index = index_of(
        lax.broadcasted_iota(jnp.int32, (Y_SHARDS, z_size), 1),
        y + lax.broadcasted_iota(jnp.int32, (Y_SHARDS, z_size), 0),
    ).reshape(-1)
    weights = pair_weights(
        image_unit, text_all, index_of(z, y).reshape(-1), text_index, sharpness, shift, factor
    )
    image_sum = jnp.dot(weights, text_all, preferred_element_type=jnp.float32)
    pooled_grad = (
        image_sum - image_dir * jnp.sum(image_dir * image_sum, axis=-1, keepdims=True)
    ) * image_inverse
    share = pooled_grad / patches
    token_grad = share.astype(jnp.bfloat16)

    column_grad = exchange_z(jnp.broadcast_to(token_grad[None], (z_size, images, model_width)))
    column_hidden = lax.dot_general(
        column_grad.reshape(column, model_width),
        down_y,
        (((1,), (1,)), ((), ())),
        preferred_element_type=jnp.float32,
    )
    hidden_grad = (
        exchange_z(column_hidden.reshape(z_size, images, part))
        .transpose(1, 0, 2)
        .reshape(images, hidden)
    )

    unit_late, _ = lax.optimization_barrier((image_unit, hidden_grad))
    column_unit = exchange_z(
        jnp.broadcast_to(unit_late[None], (z_size, images, model_width))
    ).reshape(column, model_width)
    row_text = lax.dynamic_index_in_dim(
        text_all.reshape(Y_SHARDS, z_size, images, model_width), z, axis=1, keepdims=False
    ).reshape(Y_SHARDS * images, model_width)
    row_weights = pair_weights(
        column_unit,
        row_text,
        index_of(jnp.arange(z_size, dtype=jnp.int32), y).reshape(-1),
        index_of(z, y + jnp.arange(Y_SHARDS, dtype=jnp.int32)).reshape(-1),
        sharpness,
        shift,
        factor,
    )
    row_sums = lax.dot_general(
        row_weights, column_unit, (((0,), (0,)), ((), ())), preferred_element_type=jnp.float32
    ).reshape(Y_SHARDS, images, model_width)
    text_sum = row_sums[0]
    for k in range(1, Y_SHARDS):
        text_sum = text_sum + from_ahead(row_sums[k], "y", -k)
    text_grad = (
        (text_sum - text_dir * jnp.sum(text_dir * text_sum, axis=-1, keepdims=True)) * text_inverse
    ).astype(jnp.bfloat16)

    preact_grad = (hidden_grad[:, None, :] * gelu_slope(preact)).astype(jnp.bfloat16)
    normed_grad = lax.dot_general(
        preact_grad.reshape(images * patches, hidden),
        up_whole,
        (((1,), (1,)), ((), ())),
        preferred_element_type=jnp.float32,
    )
    inner_grad = norm_backward(tokens, normed_grad, layernorm_multiplier[0]).reshape(
        images, patches, model_width
    )
    span_grad = (share[:, None, :] + inner_grad).astype(jnp.bfloat16)
    prev_grad = from_ahead(span_grad[None], "section", 1)
    return (prev_grad, text_grad[None])


def solution(mesh):
    sections, shards = mesh.devices.shape
    folded = Mesh(
        mesh.devices.reshape(sections, shards // Y_SHARDS, Y_SHARDS), ("section", "z", "y")
    )
    dp = ("z", "y")
    placed = (
        P("section", dp, None, None),
        P("section", dp, None, None),
        P("section", None),
        P("section", dp, None),
        P("section", dp, None),
        P("section", dp, None),
        P(),
        P(),
        P(),
    )
    return jax.shard_map(
        per_device,
        mesh=folded,
        in_specs=placed,
        out_specs=(P("section", dp, None, None), P("section", dp, None)),
        check_vma=False,
    )
```

time: 798 us -> 212 us (0.27)
  waiting for transfers between devices: 349 us -> 72.3 us
  matrix products: 191 us -> 14.3 us
  starting transfers between devices: 210 us -> 76.9 us
  local copies, waits for them, and re-layouts: 6.59 us -> 14.6 us
    dot_general x99 -> x6, matrix products: 191 us -> 14.3 us  [the longest x1 6.54 us: per_device(): lax.dot_general(preact_grad.reshape(images * patches, hidden), up_whole,...]
    ppermute x64 -> x13, waiting for transfers between devices: 198 us -> 24.7 us  [from_ahead(): lax.ppermute(array, axis, [((i + by) % peers, i) for i in range(peers)])]
    ppermute x64 -> x13, starting transfers between devices: 210 us -> 51.4 us  [from_ahead(): lax.ppermute(array, axis, [((i + by) % peers, i) for i in range(peers)])]
    all_gather x2 -> x1, waiting for transfers between devices: 151 us -> 0.01 us  [per_device(): up_whole = lax.all_gather(up_y, 'z', axis=0, tiled=True)]
    all_to_all x0 -> x5, waiting for transfers between devices: none -> 47.6 us  [exchange_z(): return lax.all_to_all(blocks, 'z', 0, 0)]
    all_to_all x0 -> x5, starting transfers between devices: none -> 25.4 us  [exchange_z(): return lax.all_to_all(blocks, 'z', 0, 0)]
  transfers between devices with their start and end apart: 66 -> 19, of which waited for: 43 -> 9; matrix products, arithmetic and copies ran while one was open for 25% -> 17% of each run, Pallas kernels for 0% -> 0%
where the time goes in v1:
time: 212 us; the launch traced here: 211 us
  starting transfers between devices  76.9 us (36%)
  waiting for transfers between devices  72.3 us (34%)
  between operations  16.6 us (8%)
  other arithmetic  16.5 us (8%)
  local copies, waits for them, and re-layouts  14.6 us (7%)
  matrix products  14.3 us (7%)
    ppermute x13, starting transfers between devices, from_ahead(): lax.ppermute(array, axis, [((i + by) % peers, i) for i in range(peers)])  51.4 us
    all_to_all x5, waiting for transfers between devices, exchange_z(): return lax.all_to_all(blocks, 'z', 0, 0)  47.6 us
    all_to_all x5, starting transfers between devices, exchange_z(): return lax.all_to_all(blocks, 'z', 0, 0)  25.4 us
    ppermute x13, waiting for transfers between devices, from_ahead(): lax.ppermute(array, axis, [((i + by) % peers, i) for i in range(peers)])  24.7 us
    dot_general x1, matrix products, per_device(): lax.dot_general(preact_grad.reshape(images * patches, hidden), up_whole,...  6.54 us
    unnamed x43, local copies, waits for them, and re-layouts  5.08 us
  transfers between devices with their start and end apart: 19, of which 9 were waited for; matrix products, arithmetic and copies ran while one was open for 17% of the time, Pallas kernels for 0%

profile of v1, /device:TPU:6, one launch (start us, length us, event | category | flops | bytes accessed | tf_op | source)
XLA Modules:
  0.0 211.1 jit_solution(12850292554272661550)
XLA Ops:
  7.2 7.7 %collective-permute-start.1 = (bf16[68,1152]{1,0:T(8,128)(2,1)}, bf16[68,1152]{1,0:T(8,128)(2,1)S(1)}, u32[]{:S(2)}, u32[]{:S(2)}) collective-permute-start(bf16[68,1152]{1,0:T(8,128)(2,1)} %bitcast.97), channel_id=1, source_target_pairs={{2,0},{3,1},{0,2},{1,3},{6,4},{7,5},{4,6},{5,7},{10,8},{11,9},{8,1... | collective-permute-start | bytes 470024 | tf_op jit(solution)/shard_map/ppermute | solution.py:14
  15.0 2.2 %collective-permute-start.2 = (bf16[68,1152]{1,0:T(8,128)(2,1)}, bf16[68,1152]{1,0:T(8,128)(2,1)S(1)}, u32[]{:S(2)}, u32[]{:S(2)}) collective-permute-start(bf16[68,1152]{1,0:T(8,128)(2,1)} %bitcast.98), channel_id=1, source_target_pairs={{1,0},{2,1},{3,2},{0,3},{5,4},{6,5},{7,6},{4,7},{9,8},{10,9},{11,1... | collective-permute-start | bytes 470024 | tf_op jit(solution)/shard_map/ppermute | solution.py:14
  17.2 5.9 %collective-permute-start.7 = (bf16[36,2176]{1,0:T(8,128)(2,1)}, bf16[36,2176]{1,0:T(8,128)(2,1)S(1)}, u32[]{:S(2)}, u32[]{:S(2)}) collective-permute-start(bf16[36,2176]{1,0:T(8,128)(2,1)} %bitcast.94), channel_id=1, source_target_pairs={{2,0},{3,1},{0,2},{1,3},{6,4},{7,5},{4,6},{5,7},{10,8},{11,9},{8,1... | collective-permute-start | bytes 470024 | tf_op jit(solution)/shard_map/ppermute | solution.py:14
  23.2 4.0 %collective-permute-start.8 = (bf16[36,2176]{1,0:T(8,128)(2,1)}, bf16[36,2176]{1,0:T(8,128)(2,1)S(1)}, u32[]{:S(2)}, u32[]{:S(2)}) collective-permute-start(bf16[36,2176]{1,0:T(8,128)(2,1)} %bitcast.95), channel_id=1, source_target_pairs={{1,0},{2,1},{3,2},{0,3},{5,4},{6,5},{7,6},{4,7},{9,8},{10,9},{11,1... | collective-permute-start | bytes 470024 | tf_op jit(solution)/shard_map/ppermute | solution.py:14
  27.2 2.7 %collective-permute-start.6 = (bf16[36,2176]{1,0:T(8,128)(2,1)}, bf16[36,2176]{1,0:T(8,128)(2,1)S(1)}, u32[]{:S(2)}, u32[]{:S(2)}) collective-permute-start(bf16[36,2176]{1,0:T(8,128)(2,1)} %bitcast.96), channel_id=1, source_target_pairs={{3,0},{0,1},{1,2},{2,3},{7,4},{4,5},{5,6},{6,7},{11,8},{8,9},{9,10... | collective-permute-start | bytes 470024 | tf_op jit(solution)/shard_map/ppermute | solution.py:14
  29.9 0.9 fusion.42
  30.8 0.9 reshape.282
  31.7 0.5 copy-done.14
  32.3 3.4 %convert_reduce_fusion = f32[16,2176]{1,0:T(8,128)S(1)} fusion(bf16[1,16,32,2176]{3,2,1,0:T(8,128)(2,1)} %param.10), kind=kLoop, calls=%fused_computation.22 | loop fusion | flops 13334528 | bytes 2367488 | tf_op jit(solution)/shard_map/reduce_sum | solution.py:95
  36.4 1.9 collective-permute-start
  38.3 7.3 %collective-permute-done.8 = bf16[36,2176]{1,0:T(8,128)(2,1)S(1)} collective-permute-done((bf16[36,2176]{1,0:T(8,128)(2,1)}, bf16[36,2176]{1,0:T(8,128)(2,1)S(1)}, u32[]{:S(2)}, u32[]{:S(2)}) %collective-permute-start.8) | collective-permute-done | bytes 156704 | tf_op jit(solution)/shard_map/ppermute | solution.py:14
  45.8 0.9 pad_maximum_fusion.1
  46.8 0.5 broadcast.292
  47.3 0.9 reduce.4
  48.3 0.9 reshape.289
  49.2 10.3 %all-to-all-start = ((bf16[8,2,13568]{2,1,0:T(2,128)(2,1)}), bf16[8,2,13568]{2,1,0:T(2,128)(2,1)S(1)}, u32[]{:S(2)}, u32[]{:S(2)}) async-start(bf16[8,2,13568]{2,1,0:T(2,128)(2,1)} %reshape.289), calls=%async_computation | async-start | bytes 868352 | tf_op jit(solution)/shard_map/all_to_all | solution.py:55
  59.6 0.2 convert_reduce_fusion.1
  59.8 0.7 multiply_reduce_fusion.1
  60.7 0.6 add_multiply_fusion.2
  63.3 0.8 select_select_fusion.7
  64.1 14.1 %all-to-all-done = bf16[8,2,13568]{2,1,0:T(2,128)(2,1)S(1)} async-done(((bf16[8,2,13568]{2,1,0:T(2,128)(2,1)}), bf16[8,2,13568]{2,1,0:T(2,128)(2,1)S(1)}, u32[]{:S(2)}, u32[]{:S(2)}) %all-to-all-start) | async-done | bytes 434208 | tf_op jit(solution)/shard_map/all_to_all | solution.py:55
  78.2 0.4 reshape.290
  78.8 1.9 collective-permute-start.5
  80.8 7.2 %collective-permute-start.4 = (bf16[128,1152]{1,0:T(8,128)(2,1)S(1)}, bf16[128,1152]{1,0:T(8,128)(2,1)}, u32[]{:S(2)}, u32[]{:S(2)}) collective-permute-start(bf16[128,1152]{1,0:T(8,128)(2,1)S(1)} %reshape.276), channel_id=1, source_target_pairs={{2,0},{3,1},{0,2},{1,3},{6,4},{7,5},{4,6},{5,7},{10,8},{11,9},{8,1... | collective-permute-start | bytes 884744 | tf_op jit(solution)/shard_map/ppermute | solution.py:14
  88.0 1.9 collective-permute-start.3
  90.3 1.2 fusion.71
  91.6 1.0 fusion.17
  92.6 3.4 %all-to-all-start.1 = ((bf16[8,16,1152]{2,1,0:T(8,128)(2,1)}), bf16[8,16,1152]{2,1,0:T(8,128)(2,1)S(1)}, u32[]{:S(2)}, u32[]{:S(2)}) async-start(bf16[8,16,1152]{2,1,0:T(8,128)(2,1)} %bitcast.93), calls=%async_computation.1 | async-start | bytes 589824 | tf_op jit(solution)/shard_map/all_to_all | solution.py:55
  96.1 8.4 %collective-permute-done.3 = bf16[128,1152]{1,0:T(8,128)(2,1)} collective-permute-done((bf16[128,1152]{1,0:T(8,128)(2,1)S(1)}, bf16[128,1152]{1,0:T(8,128)(2,1)}, u32[]{:S(2)}, u32[]{:S(2)}) %collective-permute-start.3) | collective-permute-done | bytes 294944 | tf_op jit(solution)/shard_map/ppermute | solution.py:14
  104.5 1.0 constant_dynamic-update-slice_fusion.2
  105.5 1.0 constant_dynamic-update-slice_fusion.1
  106.5 5.4 %all-to-all-done.1 = bf16[8,16,1152]{2,1,0:T(8,128)(2,1)S(1)} async-done(((bf16[8,16,1152]{2,1,0:T(8,128)(2,1)}), bf16[8,16,1152]{2,1,0:T(8,128)(2,1)S(1)}, u32[]{:S(2)}, u32[]{:S(2)}) %all-to-all-start.1) | async-done | bytes 294944 | tf_op jit(solution)/shard_map/all_to_all | solution.py:55
  112.2 0.8 multiply_reduce_fusion.3
  112.9 0.7 fusion.74
  113.7 0.7 broadcast_in_dim.25
  114.4 3.4 %all-to-all-start.2 = ((bf16[8,16,1152]{2,1,0:T(8,128)(2,1)}), bf16[8,16,1152]{2,1,0:T(8,128)(2,1)S(1)}, u32[]{:S(2)}, u32[]{:S(2)}) async-start(bf16[8,16,1152]{2,1,0:T(8,128)(2,1)} %broadcast_in_dim.25), calls=%async_computation.2 | async-start | bytes 589824 | tf_op jit(solution)/shard_map/all_to_all | solution.py:55
  118.0 15.5 %all-to-all-done.2 = bf16[8,16,1152]{2,1,0:T(8,128)(2,1)S(1)} async-done(((bf16[8,16,1152]{2,1,0:T(8,128)(2,1)}), bf16[8,16,1152]{2,1,0:T(8,128)(2,1)S(1)}, u32[]{:S(2)}, u32[]{:S(2)}) %all-to-all-start.2) | async-done | bytes 294944 | tf_op jit(solution)/shard_map/all_to_all | solution.py:55
  133.5 0.8 broadcast_in_dim.30
  134.3 4.0 %all-to-all-start.4 = ((bf16[8,16,1152]{2,1,0:T(8,128)(2,1)}), bf16[8,16,1152]{2,1,0:T(8,128)(2,1)}, u32[]{:S(2)}, u32[]{:S(2)}) async-start(bf16[8,16,1152]{2,1,0:T(8,128)(2,1)} %broadcast_in_dim.30), calls=%async_computation.4 | async-start | bytes 589824 | tf_op jit(solution)/shard_map/all_to_all | solution.py:55
  138.4 0.7 div.43
  139.1 0.7 add.278
  139.7 0.7 add.272
  140.4 0.7 rsqrt.30
  141.1 0.6 reduce.3
  141.7 2.4 %fusion.37 = f32[8,16,272]{2,1,0:T(8,128)} fusion(bf16[8,16,1152]{2,1,0:T(8,128)(2,1)} %copy-done.4, bf16[68,1152]{1,0:T(8,128)(2,1)} %copy-done.9, bf16[68,1152]{1,0:T(8,128)(2,1)} %copy-done.10, bf16[68,1152]{1,0:T(8,128)(2,1)} %get-tuple-element.19, bf16[68,1152]{1,0:T(8,128)(2,1)} %copy-done.8), kind=kOutput, calls=%fused_computation.56 | convolution fusion | flops 82722816 | bytes 1060864 | tf_op jit(solution)/shard_map/dot_general | solution.py:151
  144.1 5.2 %all-to-all-done.4 = bf16[8,16,1152]{2,1,0:T(8,128)(2,1)} async-done(((bf16[8,16,1152]{2,1,0:T(8,128)(2,1)}), bf16[8,16,1152]{2,1,0:T(8,128)(2,1)}, u32[]{:S(2)}, u32[]{:S(2)}) %all-to-all-start.4) | async-done | bytes 294944 | tf_op jit(solution)/shard_map/all_to_all | solution.py:55
  149.3 4.2 %all-to-all-start.3 = ((f32[8,16,272]{2,1,0:T(8,128)}), f32[8,16,272]{2,1,0:T(8,128)}, u32[]{:S(2)}, u32[]{:S(2)}) async-start(f32[8,16,272]{2,1,0:T(8,128)} %fusion.37), calls=%async_computation.3 | async-start | bytes 393216 | tf_op jit(solution)/shard_map/all_to_all | solution.py:55
  153.5 2.2 %fusion.35 = f32[64,1152]{1,0:T(8,128)} fusion(bf16[128,1152]{1,0:T(8,128)(2,1)} %bitcast.17, bf16[64,1152]{1,0:T(8,128)(2,1)S(1)} %bitcast.92, f32[]{:T(128)} %bitcast.86, f32[]{:T(128)} %bitcast.84, s32[128]{0:T(128)} %add.272, f32[]{:T(128)S(6)} %mul.263, s32[64]{0:T(128)} %add.278), kind=kOutput, calls=%fused_computation.52 | convolution fusion | flops 37847040 | bytes 738060 | tf_op jit(solution)/shard_map/dot_general | solution.py:179
  155.7 7.4 %all-to-all-done.3 = f32[8,16,272]{2,1,0:T(8,128)} async-done(((f32[8,16,272]{2,1,0:T(8,128)}), f32[8,16,272]{2,1,0:T(8,128)}, u32[]{:S(2)}, u32[]{:S(2)}) %all-to-all-start.3) | async-done | bytes 139296 | tf_op jit(solution)/shard_map/all_to_all | solution.py:55
  163.1 1.7 copy.21
  164.7 1.0 mul.293
  165.8 4.0 %fusion.14 = bf16[512,2176]{1,0:T(8,128)(2,1)} fusion(bf16[1,16,32,2176]{3,2,1,0:T(8,128)(2,1)S(1)} %copy-done.1, f32[16,2176]{1,0:T(8,128)S(1)} %mul.293), kind=kLoop, calls=%fused_computation.17 | loop fusion | flops 22282240 | bytes 4595712 | tf_op jit(solution)/shard_map/convert_element_type | solution.py:189
  169.8 6.5 %fusion.72 = (f32[512]{0:T(512)S(1)}, f32[512]{0:T(512)S(1)}, f32[512,1152]{1,0:T(8,128)S(1)}) fusion(f32[512]{0:T(512)S(1)} %copy-done.13, f32[512]{0:T(512)S(1)} %copy-done.12, bf16[1,16,32,1152]{3,2,1,0:T(8,128)(2,1)S(1)} %copy-done, f32[1152]{0:T(1024)} %reduce.3, bf16[512,2176]{1,0:T(8,128)(2,1)} %fusion.14, ...), kind=kOutput, calls=%fused_computation.139 | convolution fusion | flops 2571041792 | bytes 10793472 | tf_op jit(solution)/shard_map/dot_general | solution.py:190
  176.4 0.7 subtract_multiply_fusion
  177.3 0.2 add_convert_fusion
  177.5 1.9 collective-permute-start.9
  179.5 4.1 %collective-permute-start.10 = (f32[16,1152]{1,0:T(8,128)S(1)}, f32[16,1152]{1,0:T(8,128)S(1)}, u32[]{:S(2)}, u32[]{:S(2)}) collective-permute-start(f32[16,1152]{1,0:T(8,128)S(1)} %get-tuple-element.22), channel_id=1, source_target_pairs={{3,0},{0,1},{1,2},{2,3},{7,4},{4,5},{5,6},{6,7},{11,8},{8,9},{9,10... | collective-permute-start | bytes 221192 | tf_op jit(solution)/shard_map/ppermute | solution.py:14
  183.6 3.9 %collective-permute-start.12 = (f32[16,1152]{1,0:T(8,128)S(1)}, f32[16,1152]{1,0:T(8,128)S(1)}, u32[]{:S(2)}, u32[]{:S(2)}) collective-permute-start(f32[16,1152]{1,0:T(8,128)S(1)} %get-tuple-element.23), channel_id=1, source_target_pairs={{1,0},{2,1},{3,2},{0,3},{5,4},{6,5},{7,6},{4,7},{9,8},{10,9},{11,1... | collective-permute-start | bytes 221192 | tf_op jit(solution)/shard_map/ppermute | solution.py:14
  187.4 5.9 %collective-permute-start.11 = (f32[16,1152]{1,0:T(8,128)S(1)}, f32[16,1152]{1,0:T(8,128)S(1)}, u32[]{:S(2)}, u32[]{:S(2)}) collective-permute-start(f32[16,1152]{1,0:T(8,128)S(1)} %get-tuple-element.24), channel_id=1, source_target_pairs={{2,0},{3,1},{0,2},{1,3},{6,4},{7,5},{4,6},{5,7},{10,8},{11,9},{8,1... | collective-permute-start | bytes 221192 | tf_op jit(solution)/shard_map/ppermute | solution.py:14
  193.4 5.4 %collective-permute-done.10 = f32[16,1152]{1,0:T(8,128)S(1)} collective-permute-done((f32[16,1152]{1,0:T(8,128)S(1)}, f32[16,1152]{1,0:T(8,128)S(1)}, u32[]{:S(2)}, u32[]{:S(2)}) %collective-permute-start.10) | collective-permute-done | bytes 73760 | tf_op jit(solution)/shard_map/ppermute | solution.py:14
  198.8 3.6 %collective-permute-done.11 = f32[16,1152]{1,0:T(8,128)S(1)} collective-permute-done((f32[16,1152]{1,0:T(8,128)S(1)}, f32[16,1152]{1,0:T(8,128)S(1)}, u32[]{:S(2)}, u32[]{:S(2)}) %collective-permute-start.11) | collective-permute-done | bytes 73760 | tf_op jit(solution)/shard_map/ppermute | solution.py:14
  202.4 0.2 multiply_reduce_fusion.2
  202.6 0.7 fusion.43
  203.3 1.0 copy.33
  (89 shorter events, 2.4 us)
Async XLA Ops:
  7.2 162.7 %all-gather.2.cloned.1.call-start = ((), (), s32[]{:S(2)}) async-start(), calls=%async_computation.5 | async-start | bytes 5640192 | tf_op jit(solution)/shard_map/all_gather | solution.py:89
  7.2 56.1 %collective-permute-start.1 = (bf16[68,1152]{1,0:T(8,128)(2,1)}, bf16[68,1152]{1,0:T(8,128)(2,1)S(1)}, u32[]{:S(2)}, u32[]{:S(2)}) collective-permute-start(bf16[68,1152]{1,0:T(8,128)(2,1)} %bitcast.97), channel_id=1, source_target_pairs={{2,0},{3,1},{0,2},{1,3},{6,4},{7,5},{4,6},{5,7},{10,8},{11,9},{8,1... | collective-permute-start | bytes 470024 | tf_op jit(solution)/shard_map/ppermute | solution.py:14
  15.0 48.4 %collective-permute-start.2 = (bf16[68,1152]{1,0:T(8,128)(2,1)}, bf16[68,1152]{1,0:T(8,128)(2,1)S(1)}, u32[]{:S(2)}, u32[]{:S(2)}) collective-permute-start(bf16[68,1152]{1,0:T(8,128)(2,1)} %bitcast.98), channel_id=1, source_target_pairs={{1,0},{2,1},{3,2},{0,3},{5,4},{6,5},{7,6},{4,7},{9,8},{10,9},{11,1... | collective-permute-start | bytes 470024 | tf_op jit(solution)/shard_map/ppermute | solution.py:14
  17.2 19.2 %collective-permute-start.7 = (bf16[36,2176]{1,0:T(8,128)(2,1)}, bf16[36,2176]{1,0:T(8,128)(2,1)S(1)}, u32[]{:S(2)}, u32[]{:S(2)}) collective-permute-start(bf16[36,2176]{1,0:T(8,128)(2,1)} %bitcast.94), channel_id=1, source_target_pairs={{2,0},{3,1},{0,2},{1,3},{6,4},{7,5},{4,6},{5,7},{10,8},{11,9},{8,1... | collective-permute-start | bytes 470024 | tf_op jit(solution)/shard_map/ppermute | solution.py:14
  23.2 22.5 %collective-permute-start.8 = (bf16[36,2176]{1,0:T(8,128)(2,1)}, bf16[36,2176]{1,0:T(8,128)(2,1)S(1)}, u32[]{:S(2)}, u32[]{:S(2)}) collective-permute-start(bf16[36,2176]{1,0:T(8,128)(2,1)} %bitcast.95), channel_id=1, source_target_pairs={{1,0},{2,1},{3,2},{0,3},{5,4},{6,5},{7,6},{4,7},{9,8},{10,9},{11,1... | collective-permute-start | bytes 470024 | tf_op jit(solution)/shard_map/ppermute | solution.py:14
  27.2 18.5 %collective-permute-start.6 = (bf16[36,2176]{1,0:T(8,128)(2,1)}, bf16[36,2176]{1,0:T(8,128)(2,1)S(1)}, u32[]{:S(2)}, u32[]{:S(2)}) collective-permute-start(bf16[36,2176]{1,0:T(8,128)(2,1)} %bitcast.96), channel_id=1, source_target_pairs={{3,0},{0,1},{1,2},{2,3},{7,4},{4,5},{5,6},{6,7},{11,8},{8,9},{9,10... | collective-permute-start | bytes 470024 | tf_op jit(solution)/shard_map/ppermute | solution.py:14
  30.8 5.6 %copy-start.7 = (bf16[1,68,1152]{2,1,0:T(8,128)(2,1)S(1)}, bf16[1,68,1152]{2,1,0:T(8,128)(2,1)}, u32[]{:S(2)}) copy-start(bf16[1,68,1152]{2,1,0:T(8,128)(2,1)} %param.13) | copy-start | bytes 470020
  30.8 14.9 %copy-start.6 = (bf16[1,36,2176]{2,1,0:T(8,128)(2,1)S(1)}, bf16[1,36,2176]{2,1,0:T(8,128)(2,1)}, u32[]{:S(2)}) copy-start(bf16[1,36,2176]{2,1,0:T(8,128)(2,1)} %param.12) | copy-start | bytes 470020
  31.7 0.5 copy-start.14
  36.4 26.9 %collective-permute-start = (bf16[68,1152]{1,0:T(8,128)(2,1)S(1)}, bf16[68,1152]{1,0:T(8,128)(2,1)S(1)}, u32[]{:S(2)}, u32[]{:S(2)}) collective-permute-start(bf16[68,1152]{1,0:T(8,128)(2,1)S(1)} %bitcast.99), channel_id=1, source_target_pairs={{3,0},{0,1},{1,2},{2,3},{7,4},{4,5},{5,6},{6,7},{11,8},{8,9},{9,10... | collective-permute-start | bytes 470024 | tf_op jit(solution)/shard_map/ppermute | solution.py:14
  45.8 13.8 %copy-start = (bf16[1,16,32,1152]{3,2,1,0:T(8,128)(2,1)S(1)}, bf16[1,16,32,1152]{3,2,1,0:T(8,128)(2,1)}, u32[]{:S(2)}) copy-start(bf16[1,16,32,1152]{3,2,1,0:T(8,128)(2,1)} %param.9) | copy-start | bytes 3538948
  49.2 29.1 %all-to-all-start = ((bf16[8,2,13568]{2,1,0:T(2,128)(2,1)}), bf16[8,2,13568]{2,1,0:T(2,128)(2,1)S(1)}, u32[]{:S(2)}, u32[]{:S(2)}) async-start(bf16[8,2,13568]{2,1,0:T(2,128)(2,1)} %reshape.289), calls=%async_computation | async-start | bytes 868352 | tf_op jit(solution)/shard_map/all_to_all | solution.py:55
  64.1 27.4 %copy-start.8 = (bf16[68,1152]{1,0:T(8,128)(2,1)}, bf16[68,1152]{1,0:T(8,128)(2,1)S(1)}, u32[]{:S(2)}) copy-start(bf16[68,1152]{1,0:T(8,128)(2,1)S(1)} %get-tuple-element.16) | copy-start | bytes 470020
  64.1 27.4 %copy-start.9 = (bf16[68,1152]{1,0:T(8,128)(2,1)}, bf16[68,1152]{1,0:T(8,128)(2,1)S(1)}, u32[]{:S(2)}) copy-start(bf16[68,1152]{1,0:T(8,128)(2,1)S(1)} %get-tuple-element.17) | copy-start | bytes 470020
  64.1 27.4 %copy-start.10 = (bf16[68,1152]{1,0:T(8,128)(2,1)}, bf16[68,1152]{1,0:T(8,128)(2,1)S(1)}, u32[]{:S(2)}) copy-start(bf16[68,1152]{1,0:T(8,128)(2,1)S(1)} %get-tuple-element.18) | copy-start | bytes 470020
  78.7 12.9 %copy-start.11 = (bf16[68,1152]{1,0:T(8,128)(2,1)S(1)}, bf16[68,1152]{1,0:T(8,128)(2,1)}, u32[]{:S(2)}) copy-start(bf16[68,1152]{1,0:T(8,128)(2,1)} %get-tuple-element.19) | copy-start | bytes 470020
  78.8 27.6 %collective-permute-start.5 = (bf16[128,1152]{1,0:T(8,128)(2,1)S(1)}, bf16[128,1152]{1,0:T(8,128)(2,1)S(1)}, u32[]{:S(2)}, u32[]{:S(2)}) collective-permute-start(bf16[128,1152]{1,0:T(8,128)(2,1)S(1)} %reshape.276), channel_id=1, source_target_pairs={{3,0},{0,1},{1,2},{2,3},{7,4},{4,5},{5,6},{6,7},{11,8},{8,9},{9,10... | collective-permute-start | bytes 884744 | tf_op jit(solution)/shard_map/ppermute | solution.py:14
  80.8 24.7 %collective-permute-start.4 = (bf16[128,1152]{1,0:T(8,128)(2,1)S(1)}, bf16[128,1152]{1,0:T(8,128)(2,1)}, u32[]{:S(2)}, u32[]{:S(2)}) collective-permute-start(bf16[128,1152]{1,0:T(8,128)(2,1)S(1)} %reshape.276), channel_id=1, source_target_pairs={{2,0},{3,1},{0,2},{1,3},{6,4},{7,5},{4,6},{5,7},{10,8},{11,9},{8,1... | collective-permute-start | bytes 884744 | tf_op jit(solution)/shard_map/ppermute | solution.py:14
  88.0 16.5 %collective-permute-start.3 = (bf16[128,1152]{1,0:T(8,128)(2,1)S(1)}, bf16[128,1152]{1,0:T(8,128)(2,1)}, u32[]{:S(2)}, u32[]{:S(2)}) collective-permute-start(bf16[128,1152]{1,0:T(8,128)(2,1)S(1)} %reshape.276), channel_id=1, source_target_pairs={{1,0},{2,1},{3,2},{0,3},{5,4},{6,5},{7,6},{4,7},{9,8},{10,9},{11,1... | collective-permute-start | bytes 884744 | tf_op jit(solution)/shard_map/ppermute | solution.py:14
  92.6 19.4 %all-to-all-start.1 = ((bf16[8,16,1152]{2,1,0:T(8,128)(2,1)}), bf16[8,16,1152]{2,1,0:T(8,128)(2,1)S(1)}, u32[]{:S(2)}, u32[]{:S(2)}) async-start(bf16[8,16,1152]{2,1,0:T(8,128)(2,1)} %bitcast.93), calls=%async_computation.1 | async-start | bytes 589824 | tf_op jit(solution)/shard_map/all_to_all | solution.py:55
  106.5 11.4 %copy-start.17 = (s32[8]{0:T(128)S(1)}, s32[8]{0:T(128)}, u32[]{:S(2)}) copy-start(s32[8]{0:T(128)} %add_multiply_fusion.2) | copy-start | bytes 100
  112.2 28.9 %copy-start.16 = (f32[1,1152]{1,0:T(1,128)S(1)}, f32[1,1152]{1,0:T(1,128)}, u32[]{:S(2)}) copy-start(f32[1,1152]{1,0:T(1,128)} %param.11) | copy-start | bytes 13828
  114.4 19.1 %all-to-all-start.2 = ((bf16[8,16,1152]{2,1,0:T(8,128)(2,1)}), bf16[8,16,1152]{2,1,0:T(8,128)(2,1)S(1)}, u32[]{:S(2)}, u32[]{:S(2)}) async-start(bf16[8,16,1152]{2,1,0:T(8,128)(2,1)} %broadcast_in_dim.25), calls=%async_computation.2 | async-start | bytes 589824 | tf_op jit(solution)/shard_map/all_to_all | solution.py:55
  133.5 8.2 %copy-start.4 = (bf16[8,16,1152]{2,1,0:T(8,128)(2,1)}, bf16[8,16,1152]{2,1,0:T(8,128)(2,1)S(1)}, u32[]{:S(2)}) copy-start(bf16[8,16,1152]{2,1,0:T(8,128)(2,1)S(1)} %all-to-all-done.2) | copy-start | bytes 884740
  134.3 15.0 %all-to-all-start.4 = ((bf16[8,16,1152]{2,1,0:T(8,128)(2,1)}), bf16[8,16,1152]{2,1,0:T(8,128)(2,1)}, u32[]{:S(2)}, u32[]{:S(2)}) async-start(bf16[8,16,1152]{2,1,0:T(8,128)(2,1)} %broadcast_in_dim.30), calls=%async_computation.4 | async-start | bytes 589824 | tf_op jit(solution)/shard_map/all_to_all | solution.py:55
  141.7 24.1 %copy-start.1 = (bf16[1,16,32,2176]{3,2,1,0:T(8,128)(2,1)S(1)}, bf16[1,16,32,2176]{3,2,1,0:T(8,128)(2,1)}, u32[]{:S(2)}) copy-start(bf16[1,16,32,2176]{3,2,1,0:T(8,128)(2,1)} %param.10) | copy-start | bytes 6684676
  149.3 13.8 %all-to-all-start.3 = ((f32[8,16,272]{2,1,0:T(8,128)}), f32[8,16,272]{2,1,0:T(8,128)}, u32[]{:S(2)}, u32[]{:S(2)}) async-start(f32[8,16,272]{2,1,0:T(8,128)} %fusion.37), calls=%async_computation.3 | async-start | bytes 393216 | tf_op jit(solution)/shard_map/all_to_all | solution.py:55
  165.8 4.0 %copy-start.12 = (f32[512]{0:T(512)S(1)}, f32[512]{0:T(512)}, u32[]{:S(2)}) copy-start(f32[512]{0:T(512)} %div.43) | copy-start | bytes 6148
  165.8 4.0 %copy-start.13 = (f32[512]{0:T(512)S(1)}, f32[512]{0:T(512)}, u32[]{:S(2)}) copy-start(f32[512]{0:T(512)} %rsqrt.30) | copy-start | bytes 6148
  176.4 0.9 copy-start.5
  177.1 2.4 %copy-start.2 = (f32[64,1152]{1,0:T(8,128)S(1)}, f32[64,1152]{1,0:T(8,128)}, u32[]{:S(2)}) copy-start(f32[64,1152]{1,0:T(8,128)} %fusion.35) | copy-start | bytes 884740
  177.1 25.3 %copy-start.3 = (bf16[1,16,1152]{2,1,0:T(8,128)(2,1)S(1)}, bf16[1,16,1152]{2,1,0:T(8,128)(2,1)}, u32[]{:S(2)}) copy-start(bf16[1,16,1152]{2,1,0:T(8,128)(2,1)} %param.14) | copy-start | bytes 110596
  177.1 25.3 %copy-start.15 = (f32[16]{0:T(128)S(1)}, f32[16]{0:T(128)}, u32[]{:S(2)}) copy-start(f32[16]{0:T(128)} %copy-done.14) | copy-start | bytes 196
  177.5 25.8 %collective-permute-start.9 = (bf16[1,16,32,1152]{3,2,1,0:T(8,128)(2,1)S(1)}, bf16[1,16,32,1152]{3,2,1,0:T(8,128)(2,1)S(1)}, u32[]{:S(2)}, u32[]{:S(2)}) collective-permute-start(bf16[1,16,32,1152]{3,2,1,0:T(8,128)(2,1)S(1)} %add_convert_fusion), channel_id=1, source_target_pairs={{32,0},{64,32},{96,64},{128,96},{160,128},{192,160},{224,192},{256... | collective-permute-start | bytes 3538952 | tf_op jit(solution)/shard_map/ppermute | solution.py:14
  179.5 19.3 %collective-permute-start.10 = (f32[16,1152]{1,0:T(8,128)S(1)}, f32[16,1152]{1,0:T(8,128)S(1)}, u32[]{:S(2)}, u32[]{:S(2)}) collective-permute-start(f32[16,1152]{1,0:T(8,128)S(1)} %get-tuple-element.22), channel_id=1, source_target_pairs={{3,0},{0,1},{1,2},{2,3},{7,4},{4,5},{5,6},{6,7},{11,8},{8,9},{9,10... | collective-permute-start | bytes 221192 | tf_op jit(solution)/shard_map/ppermute | solution.py:14
  183.6 15.2 %collective-permute-start.12 = (f32[16,1152]{1,0:T(8,128)S(1)}, f32[16,1152]{1,0:T(8,128)S(1)}, u32[]{:S(2)}, u32[]{:S(2)}) collective-permute-start(f32[16,1152]{1,0:T(8,128)S(1)} %get-tuple-element.23), channel_id=1, source_target_pairs={{1,0},{2,1},{3,2},{0,3},{5,4},{6,5},{7,6},{4,7},{9,8},{10,9},{11,1... | collective-permute-start | bytes 221192 | tf_op jit(solution)/shard_map/ppermute | solution.py:14
  187.4 14.9 %collective-permute-start.11 = (f32[16,1152]{1,0:T(8,128)S(1)}, f32[16,1152]{1,0:T(8,128)S(1)}, u32[]{:S(2)}, u32[]{:S(2)}) collective-permute-start(f32[16,1152]{1,0:T(8,128)S(1)} %get-tuple-element.24), channel_id=1, source_target_pairs={{2,0},{3,1},{0,2},{1,3},{6,4},{7,5},{4,6},{5,7},{10,8},{11,9},{8,1... | collective-permute-start | bytes 221192 | tf_op jit(solution)/shard_map/ppermute | solution.py:14
Sparse Core Ops, SparseCore 0:
  46.9 85.4 all-gather.1

commit v2 on v1

--- a/solution.py
+++ b/solution.py
@@ -55,8 +55,17 @@
     return lax.all_to_all(blocks, "z", 0, 0)
 
 
-def gather_y(shard, y):
-    ahead = [shard] + [from_ahead(shard, "y", k) for k in range(1, Y_SHARDS)]
+def gather_next_section_y(shard, y):
+    sections = lax.axis_size("section")
+
+    def pairs(by):
+        return [
+            (((s + 1) % sections) * Y_SHARDS + (own + by) % Y_SHARDS, s * Y_SHARDS + own)
+            for s in range(sections)
+            for own in range(Y_SHARDS)
+        ]
+
+    ahead = [lax.ppermute(shard, ("section", "y"), pairs(k)) for k in range(Y_SHARDS)]
     placed = [
         lax.select_n(y, *[ahead[(a - own) % Y_SHARDS] for own in range(Y_SHARDS)])
         for a in range(Y_SHARDS)
@@ -85,9 +94,14 @@
     shift = similarity_shift_term[0]
     factor = objective_upstream_grad[0] * sharpness
 
-    up_y = gather_y(expanding_projector[0], y)
+    down_y = lax.all_to_all(
+        jnp.broadcast_to(contracting_projector, (Y_SHARDS,) + contracting_projector.shape[1:]),
+        "y",
+        0,
+        0,
+    ).reshape(-1, model_width)
+    up_y = gather_next_section_y(expanding_projector[0], y)
     up_whole = lax.all_gather(up_y, "z", axis=0, tiled=True)
-    down_y = gather_y(contracting_projector[0], y)
 
     tokens = feedforward_entry_states[0].reshape(images * patches, model_width).astype(jnp.float32)
     preact = stored_hidden_preacts[0].astype(jnp.float32)
@@ -117,17 +131,21 @@
     column_high = first[:, :cut].reshape(column, part)
     column_low = first[:, cut : 2 * cut].reshape(column, part)
     column_text = first[:, 2 * cut :].reshape(column, model_width)
+    partial = jnp.dot(column_high, down_y, preferred_element_type=jnp.float32) + jnp.dot(
+        column_low, down_y, preferred_element_type=jnp.float32
+    )
+    partial, column_text = lax.optimization_barrier((partial.astype(jnp.bfloat16), column_text))
     text_all = jnp.concatenate(
         [column_text] + [from_ahead(column_text, "y", k) for k in range(1, Y_SHARDS)], axis=0
     )
-
-    partial = jnp.dot(column_high, down_y, preferred_element_type=jnp.float32) + jnp.dot(
-        column_low, down_y, preferred_element_type=jnp.float32
-    )
-    partials = exchange_z(partial.astype(jnp.bfloat16).reshape(z_size, images, model_width))
+    partials = exchange_z(partial.reshape(z_size, images, model_width))
     pooled = mean_tokens + jnp.sum(partials.astype(jnp.float32), axis=0)
     image_dir, image_inverse = unit_rows(pooled)
     image_unit = image_dir.astype(jnp.bfloat16)
+
+    text_all, entry_states, preacts = lax.optimization_barrier(
+        (text_all, feedforward_entry_states, stored_hidden_preacts)
+    )
 
     def index_of(z_index, y_index):
         start = (z_index * Y_SHARDS + y_index % Y_SHARDS) * images
@@ -147,12 +165,16 @@
     share = pooled_grad / patches
     token_grad = share.astype(jnp.bfloat16)
 
-    column_grad = exchange_z(jnp.broadcast_to(token_grad[None], (z_size, images, model_width)))
+    columns = exchange_z(
+        jnp.broadcast_to(
+            jnp.concatenate([token_grad, image_unit], axis=0)[None],
+            (z_size, 2 * images, model_width),
+        )
+    )
+    column_grad = columns[:, :images].reshape(column, model_width)
+    column_unit = columns[:, images:].reshape(column, model_width)
     column_hidden = lax.dot_general(
-        column_grad.reshape(column, model_width),
-        down_y,
-        (((1,), (1,)), ((), ())),
-        preferred_element_type=jnp.float32,
+        column_grad, down_y, (((1,), (1,)), ((), ())), preferred_element_type=jnp.float32
     )
     hidden_grad = (
         exchange_z(column_hidden.reshape(z_size, images, part))
@@ -160,10 +182,6 @@
         .reshape(images, hidden)
     )
 
-    unit_late, _ = lax.optimization_barrier((image_unit, hidden_grad))
-    column_unit = exchange_z(
-        jnp.broadcast_to(unit_late[None], (z_size, images, model_width))
-    ).reshape(column, model_width)
     row_text = lax.dynamic_index_in_dim(
         text_all.reshape(Y_SHARDS, z_size, images, model_width), z, axis=1, keepdims=False
     ).reshape(Y_SHARDS * images, model_width)
@@ -186,18 +204,23 @@
         (text_sum - text_dir * jnp.sum(text_dir * text_sum, axis=-1, keepdims=True)) * text_inverse
     ).astype(jnp.bfloat16)
 
-    preact_grad = (hidden_grad[:, None, :] * gelu_slope(preact)).astype(jnp.bfloat16)
+    next_preact = from_ahead(preacts, "section", 1)[0].astype(jnp.float32)
+    next_tokens = from_ahead(entry_states, "section", 1)[0].astype(jnp.float32)
+    handed = from_ahead(jnp.concatenate([hidden_grad, share], axis=1), "section", 1)
+    next_hidden, next_share = handed[:, :hidden], handed[:, hidden:]
+    next_multiplier = from_ahead(layernorm_multiplier, "section", 1)
+
+    preact_grad = (next_hidden[:, None, :] * gelu_slope(next_preact)).astype(jnp.bfloat16)
     normed_grad = lax.dot_general(
         preact_grad.reshape(images * patches, hidden),
         up_whole,
         (((1,), (1,)), ((), ())),
         preferred_element_type=jnp.float32,
     )
-    inner_grad = norm_backward(tokens, normed_grad, layernorm_multiplier[0]).reshape(
-        images, patches, model_width
-    )
-    span_grad = (share[:, None, :] + inner_grad).astype(jnp.bfloat16)
-    prev_grad = from_ahead(span_grad[None], "section", 1)
+    inner_grad = norm_backward(
+        next_tokens.reshape(images * patches, model_width), normed_grad, next_multiplier[0]
+    ).reshape(images, patches, model_width)
+    prev_grad = (next_share[:, None, :] + inner_grad).astype(jnp.bfloat16)[None]
     return (prev_grad, text_grad[None])
 
 

time: 212 us -> 201 us (0.948)
  the two profiles are of different devices: /device:TPU:6 before, /device:TPU:9 now
where the time goes in v2:
time: 201 us; the launch traced here: 200 us
  starting transfers between devices  93.4 us (46%)
  waiting for transfers between devices  54.9 us (27%)
  between operations  16.6 us (8%)
  other arithmetic  15.3 us (8%)
  matrix products  10.5 us (5%)
  local copies, waits for them, and re-layouts  8.99 us (4%)
    ppermute x10, starting transfers between devices, from_ahead(): lax.ppermute(array, axis, [((i + by) % peers, i) for i in range(peers)])  50 us
    ppermute x10, waiting for transfers between devices, from_ahead(): lax.ppermute(array, axis, [((i + by) % peers, i) for i in range(peers)])  29.2 us
    all_to_all x4, starting transfers between devices, exchange_z(): return lax.all_to_all(blocks, 'z', 0, 0)  21.1 us
    ppermute x4, starting transfers between devices, gather_next_section_y(): lax.ppermute(shard, ('section', 'y'), pairs(k))  16.6 us
    all_to_all x1, waiting for transfers between devices, per_device(): lax.all_to_all(jnp.broadcast_to(contracting_projector, (Y_SHARDS,) + cont...  13.6 us
    all_to_all x4, waiting for transfers between devices, exchange_z(): return lax.all_to_all(blocks, 'z', 0, 0)  12 us
    dot_general x1, matrix products, per_device(): lax.dot_general(preact_grad.reshape(images * patches, hidden), up_whole,...  5.82 us
    all_to_all x1, starting transfers between devices, per_device(): lax.all_to_all(jnp.broadcast_to(contracting_projector, (Y_SHARDS,) + cont...  5.68 us
  transfers between devices with their start and end apart: 20, of which 7 were waited for; matrix products, arithmetic and copies ran while one was open for 13% of the time, Pallas kernels for 0%

profile of v2, /device:TPU:9, one launch (start us, length us, event | category | flops | bytes accessed | tf_op | source)
XLA Modules:
  0.0 199.6 jit_solution(7113870010739468415)
XLA Ops:
  7.2 5.5 %collective-permute-start.9 = (bf16[36,2176]{1,0:T(8,128)(2,1)}, bf16[36,2176]{1,0:T(8,128)(2,1)S(1)}, u32[]{:S(2)}, u32[]{:S(2)}) collective-permute-start(bf16[36,2176]{1,0:T(8,128)(2,1)} %bitcast.75), channel_id=1, source_target_pairs={{33,0},{34,1},{35,2},{32,3},{65,32},{66,33},{67,34},{64,35},{97,64... | collective-permute-start | bytes 470024 | tf_op jit(solution)/shard_map/ppermute | solution.py:68
  12.7 4.0 %collective-permute-start.8 = (bf16[36,2176]{1,0:T(8,128)(2,1)}, bf16[36,2176]{1,0:T(8,128)(2,1)S(1)}, u32[]{:S(2)}, u32[]{:S(2)}) collective-permute-start(bf16[36,2176]{1,0:T(8,128)(2,1)} %bitcast.76), channel_id=1, source_target_pairs={{34,0},{35,1},{32,2},{33,3},{66,32},{67,33},{64,34},{65,35},{98,64... | collective-permute-start | bytes 470024 | tf_op jit(solution)/shard_map/ppermute | solution.py:68
  16.8 3.9 %collective-permute-start.7 = (bf16[36,2176]{1,0:T(8,128)(2,1)}, bf16[36,2176]{1,0:T(8,128)(2,1)S(1)}, u32[]{:S(2)}, u32[]{:S(2)}) collective-permute-start(bf16[36,2176]{1,0:T(8,128)(2,1)} %bitcast.77), channel_id=1, source_target_pairs={{35,0},{32,1},{33,2},{34,3},{67,32},{64,33},{65,34},{66,35},{99,64... | collective-permute-start | bytes 470024 | tf_op jit(solution)/shard_map/ppermute | solution.py:68
  20.6 3.2 %collective-permute-start.6 = (bf16[36,2176]{1,0:T(8,128)(2,1)}, bf16[36,2176]{1,0:T(8,128)(2,1)S(1)}, u32[]{:S(2)}, u32[]{:S(2)}) collective-permute-start(bf16[36,2176]{1,0:T(8,128)(2,1)} %bitcast.78), channel_id=1, source_target_pairs={{32,0},{33,1},{34,2},{35,3},{64,32},{65,33},{66,34},{67,35},{96,64... | collective-permute-start | bytes 470024 | tf_op jit(solution)/shard_map/ppermute | solution.py:68
  23.8 3.7 %collective-permute-start.10 = (f32[1,1152]{1,0:T(1,128)}, f32[1,1152]{1,0:T(1,128)S(1)}, u32[]{:S(2)}, u32[]{:S(2)}) collective-permute-start(f32[1,1152]{1,0:T(1,128)} %param.11), channel_id=1, source_target_pairs={{32,0},{64,32},{96,64},{128,96},{160,128},{192,160},{224,192},{256... | collective-permute-start | bytes 13832 | tf_op jit(solution)/shard_map/ppermute | solution.py:14
  27.5 0.9 fusion.40
  28.4 0.8 reshape.290
  29.3 3.5 %convert_reduce_fusion = f32[16,2176]{1,0:T(8,128)S(1)} fusion(bf16[1,16,32,2176]{3,2,1,0:T(8,128)(2,1)} %param.10), kind=kLoop, calls=%fused_computation.26 | loop fusion | flops 13334528 | bytes 2367488 | tf_op jit(solution)/shard_map/reduce_sum | solution.py:109
  32.8 0.1 div.37
  33.0 0.2 reshape.277
  33.2 0.2 reshape.278
  33.4 0.5 broadcast.292
  33.9 0.9 reduce.4
  34.9 0.9 reshape.298
  35.8 10.0 %all-to-all-start = ((bf16[8,2,13568]{2,1,0:T(2,128)(2,1)}), bf16[8,2,13568]{2,1,0:T(2,128)(2,1)S(1)}, u32[]{:S(2)}, u32[]{:S(2)}) async-start(bf16[8,2,13568]{2,1,0:T(2,128)(2,1)} %reshape.298), calls=%async_computation | async-start | bytes 868352 | tf_op jit(solution)/shard_map/all_to_all | solution.py:55
  46.0 0.9 pad_maximum_fusion.1
  47.1 0.3 convert_reduce_fusion.1
  47.5 12.0 %all-to-all-done = bf16[8,2,13568]{2,1,0:T(2,128)(2,1)S(1)} async-done(((bf16[8,2,13568]{2,1,0:T(2,128)(2,1)}), bf16[8,2,13568]{2,1,0:T(2,128)(2,1)S(1)}, u32[]{:S(2)}, u32[]{:S(2)}) %all-to-all-start) | async-done | bytes 434208 | tf_op jit(solution)/shard_map/all_to_all | solution.py:55
  59.5 0.9 broadcast_in_dim.30
  60.4 5.7 %all-to-all-start.1 = ((bf16[4,68,1152]{2,1,0:T(8,128)(2,1)}), bf16[4,68,1152]{2,1,0:T(8,128)(2,1)S(1)}, u32[]{:S(2)}, u32[]{:S(2)}) async-start(bf16[4,68,1152]{2,1,0:T(8,128)(2,1)} %broadcast_in_dim.30), calls=%async_computation.1 | async-start | bytes 1327104 | tf_op jit(solution)/shard_map/all_to_all | solution.py:97
  66.1 0.4 reshape.299
  66.5 0.1 reshape.282
  66.7 0.2 reshape.281
  66.9 0.2 reshape.279
  67.0 13.6 %all-to-all-done.1 = bf16[4,68,1152]{2,1,0:T(8,128)(2,1)S(1)} async-done(((bf16[4,68,1152]{2,1,0:T(8,128)(2,1)}), bf16[4,68,1152]{2,1,0:T(8,128)(2,1)S(1)}, u32[]{:S(2)}, u32[]{:S(2)}) %all-to-all-start.1) | async-done | bytes 626720 | tf_op jit(solution)/shard_map/all_to_all | solution.py:97
  80.7 0.1 reshape.280
  80.8 0.3 fusion.73
  81.1 1.0 fusion.15
  82.1 3.0 %collective-permute-start.2 = (bf16[128,1152]{1,0:T(8,128)(2,1)S(1)}, bf16[128,1152]{1,0:T(8,128)(2,1)S(1)}, u32[]{:S(2)}, u32[]{:S(2)}) collective-permute-start(bf16[128,1152]{1,0:T(8,128)(2,1)S(1)} %reshape.282), channel_id=1, source_target_pairs={{3,0},{0,1},{1,2},{2,3},{7,4},{4,5},{5,6},{6,7},{11,8},{8,9},{9,10... | collective-permute-start | bytes 884744 | tf_op jit(solution)/shard_map/ppermute | solution.py:14
  85.1 1.9 collective-permute-start.1
  87.0 5.3 %collective-permute-start = (bf16[128,1152]{1,0:T(8,128)(2,1)S(1)}, bf16[128,1152]{1,0:T(8,128)(2,1)S(1)}, u32[]{:S(2)}, u32[]{:S(2)}) collective-permute-start(bf16[128,1152]{1,0:T(8,128)(2,1)S(1)} %reshape.282), channel_id=1, source_target_pairs={{1,0},{2,1},{3,2},{0,3},{5,4},{6,5},{7,6},{4,7},{9,8},{10,9},{11,1... | collective-permute-start | bytes 884744 | tf_op jit(solution)/shard_map/ppermute | solution.py:14
  92.4 3.4 %all-to-all-start.2 = ((bf16[8,16,1152]{2,1,0:T(8,128)(2,1)}), bf16[8,16,1152]{2,1,0:T(8,128)(2,1)S(1)}, u32[]{:S(2)}, u32[]{:S(2)}) async-start(bf16[8,16,1152]{2,1,0:T(8,128)(2,1)} %bitcast.9), calls=%async_computation.2 | async-start | bytes 589824 | tf_op jit(solution)/shard_map/all_to_all | solution.py:55
  97.9 1.9 collective-permute-done.1
  99.8 10.7 %collective-permute-done = bf16[128,1152]{1,0:T(8,128)(2,1)S(1)} collective-permute-done((bf16[128,1152]{1,0:T(8,128)(2,1)S(1)}, bf16[128,1152]{1,0:T(8,128)(2,1)S(1)}, u32[]{:S(2)}, u32[]{:S(2)}) %collective-permute-start) | collective-permute-done | bytes 294944 | tf_op jit(solution)/shard_map/ppermute | solution.py:14
  110.6 4.7 %collective-permute-start.4 = (bf16[1,16,32,1152]{3,2,1,0:T(8,128)(2,1)}, bf16[1,16,32,1152]{3,2,1,0:T(8,128)(2,1)S(1)}, u32[]{:S(2)}, u32[]{:S(2)}) collective-permute-start(bf16[1,16,32,1152]{3,2,1,0:T(8,128)(2,1)} %param.9), channel_id=1, source_target_pairs={{32,0},{64,32},{96,64},{128,96},{160,128},{192,160},{224,192},{256... | collective-permute-start | bytes 3538952 | tf_op jit(solution)/shard_map/ppermute | solution.py:14
  115.4 0.1 multiply_reduce_fusion.5
  115.6 0.8 multiply_reduce_fusion.4
  116.4 0.1 fusion.70
  116.5 0.9 broadcast_in_dim.31
  117.4 4.2 %all-to-all-start.3 = ((bf16[8,32,1152]{2,1,0:T(8,128)(2,1)}), bf16[8,32,1152]{2,1,0:T(8,128)(2,1)}, u32[]{:S(2)}, u32[]{:S(2)}) async-start(bf16[8,32,1152]{2,1,0:T(8,128)(2,1)} %broadcast_in_dim.31), calls=%async_computation.3 | async-start | bytes 1179648 | tf_op jit(solution)/shard_map/all_to_all | solution.py:55
  121.9 0.9 reshape.294
  122.8 8.4 %collective-permute-start.5 = (bf16[1,16,32,2176]{3,2,1,0:T(8,128)(2,1)}, bf16[1,16,32,2176]{3,2,1,0:T(8,128)(2,1)}, u32[]{:S(2)}, u32[]{:S(2)}) collective-permute-start(bf16[1,16,32,2176]{3,2,1,0:T(8,128)(2,1)} %param.10), channel_id=1, source_target_pairs={{32,0},{64,32},{96,64},{128,96},{160,128},{192,160},{224,192},{256... | collective-permute-start | bytes 6684680 | tf_op jit(solution)/shard_map/ppermute | solution.py:14
  131.2 5.1 %collective-permute-done.4 = bf16[1,16,32,1152]{3,2,1,0:T(8,128)(2,1)S(1)} collective-permute-done((bf16[1,16,32,1152]{3,2,1,0:T(8,128)(2,1)}, bf16[1,16,32,1152]{3,2,1,0:T(8,128)(2,1)S(1)}, u32[]{:S(2)}, u32[]{:S(2)}) %collective-permute-start.4) | collective-permute-done | bytes 1179680 | tf_op jit(solution)/shard_map/ppermute | solution.py:14
  136.3 0.2 convert_reduce_fusion.2
  136.6 0.5 multiply_reduce_fusion.1
  137.0 2.0 %fusion.35 = f32[8,16,272]{2,1,0:T(8,128)} fusion(bf16[272,1152,1]{1,0,2:T(8,128)(2,1)S(1)} %copy-done, bf16[8,32,1152]{2,1,0:T(8,128)(2,1)} %all-to-all-done.3), kind=kOutput, calls=%fused_computation.63 | convolution fusion | flops 80216064 | bytes 1060864 | tf_op jit(solution)/shard_map/dot_general | solution.py:176
  139.1 3.4 %all-to-all-start.4 = ((f32[8,16,272]{2,1,0:T(8,128)}), f32[8,16,272]{2,1,0:T(8,128)S(1)}, u32[]{:S(2)}, u32[]{:S(2)}) async-start(f32[8,16,272]{2,1,0:T(8,128)} %fusion.35), calls=%async_computation.4 | async-start | bytes 393216 | tf_op jit(solution)/shard_map/all_to_all | solution.py:55
  142.5 1.0 slice.54
  143.5 0.5 fusion.33
  144.0 12.1 %collective-permute-start.11 = (f32[16,1152]{1,0:T(8,128)S(1)}, f32[16,1152]{1,0:T(8,128)S(1)}, u32[]{:S(2)}, u32[]{:S(2)}) collective-permute-start(f32[16,1152]{1,0:T(8,128)S(1)} %get-tuple-element.26), channel_id=1, source_target_pairs={{3,0},{0,1},{1,2},{2,3},{7,4},{4,5},{5,6},{6,7},{11,8},{8,9},{9,10... | collective-permute-start | bytes 221192 | tf_op jit(solution)/shard_map/ppermute | solution.py:14
  156.1 1.9 collective-permute-start.13
  158.0 5.2 %collective-permute-start.12 = (f32[16,1152]{1,0:T(8,128)S(1)}, f32[16,1152]{1,0:T(8,128)S(1)}, u32[]{:S(2)}, u32[]{:S(2)}) collective-permute-start(f32[16,1152]{1,0:T(8,128)S(1)} %get-tuple-element.28), channel_id=1, source_target_pairs={{2,0},{3,1},{0,2},{1,3},{6,4},{7,5},{4,6},{5,7},{10,8},{11,9},{8,1... | collective-permute-start | bytes 221192 | tf_op jit(solution)/shard_map/ppermute | solution.py:14
  163.4 3.8 %collective-permute-done.12 = f32[16,1152]{1,0:T(8,128)S(1)} collective-permute-done((f32[16,1152]{1,0:T(8,128)S(1)}, f32[16,1152]{1,0:T(8,128)S(1)}, u32[]{:S(2)}, u32[]{:S(2)}) %collective-permute-start.12) | collective-permute-done | bytes 73760 | tf_op jit(solution)/shard_map/ppermute | solution.py:14
  167.1 0.2 multiply_reduce_fusion.3
  167.4 0.1 reshape.284
  167.6 3.9 %collective-permute-start.3 = (f32[16,3328]{1,0:T(8,128)S(1)}, f32[16,3328]{1,0:T(8,128)S(1)}, u32[]{:S(2)}, u32[]{:S(2)}) collective-permute-start(f32[16,3328]{1,0:T(8,128)S(1)} %pad_maximum_fusion.2), channel_id=1, source_target_pairs={{32,0},{64,32},{96,64},{128,96},{160,128},{192,160},{224,192},{256... | collective-permute-start | bytes 638984 | tf_op jit(solution)/shard_map/ppermute | solution.py:14
  171.4 0.7 fusion.41
  172.1 7.7 %collective-permute-done.3 = f32[16,3328]{1,0:T(8,128)S(1)} collective-permute-done((f32[16,3328]{1,0:T(8,128)S(1)}, f32[16,3328]{1,0:T(8,128)S(1)}, u32[]{:S(2)}, u32[]{:S(2)}) %collective-permute-start.3) | collective-permute-done | bytes 213024 | tf_op jit(solution)/shard_map/ppermute | solution.py:14
  179.8 0.7 copy-done.3
  180.5 4.2 %fusion.13 = bf16[512,2176]{1,0:T(8,128)(2,1)S(1)} fusion(bf16[1,16,32,2176]{3,2,1,0:T(8,128)(2,1)} %collective-permute-done.5, f32[16,2176]{1,0:T(8,128)S(1)} %slice.53), kind=kLoop, calls=%fused_computation.24 | loop fusion | flops 22282240 | bytes 4595712 | tf_op jit(solution)/shard_map/convert_element_type | solution.py:213
  184.8 5.8 %multiply_reduce_fusion.2 = (f32[512]{0:T(512)S(1)}, f32[512]{0:T(512)S(1)}, f32[512,1152]{1,0:T(8,128)S(1)}) fusion(f32[1152]{0:T(1024)S(1)} %reduce.3, f32[512]{0:T(512)S(1)} %rsqrt.30, f32[512]{0:T(512)S(1)} %div.43, bf16[1,16,32,1152]{3,2,1,0:T(8,128)(2,1)S(1)} %collective-permute-done.4, bf16[512,2176]{1,0:T(8,128)(2,1)S(1)} %fusion.13, ...), kind=kOutput, calls=%fused_computation.37 | convolution fusion | flops 2571041792 | bytes 10793472 | tf_op jit(solution)/shard_map/dot_general | solution.py:214
  190.6 0.8 subtract_multiply_fusion
  191.4 0.1 slice-done
  191.5 1.2 add_convert_fusion
  (69 shorter events, 1.7 us)
Async XLA Ops:
  7.2 38.7 %collective-permute-start.9 = (bf16[36,2176]{1,0:T(8,128)(2,1)}, bf16[36,2176]{1,0:T(8,128)(2,1)S(1)}, u32[]{:S(2)}, u32[]{:S(2)}) collective-permute-start(bf16[36,2176]{1,0:T(8,128)(2,1)} %bitcast.75), channel_id=1, source_target_pairs={{33,0},{34,1},{35,2},{32,3},{65,32},{66,33},{67,34},{64,35},{97,64... | collective-permute-start | bytes 470024 | tf_op jit(solution)/shard_map/ppermute | solution.py:68
  12.7 33.2 %collective-permute-start.8 = (bf16[36,2176]{1,0:T(8,128)(2,1)}, bf16[36,2176]{1,0:T(8,128)(2,1)S(1)}, u32[]{:S(2)}, u32[]{:S(2)}) collective-permute-start(bf16[36,2176]{1,0:T(8,128)(2,1)} %bitcast.76), channel_id=1, source_target_pairs={{34,0},{35,1},{32,2},{33,3},{66,32},{67,33},{64,34},{65,35},{98,64... | collective-permute-start | bytes 470024 | tf_op jit(solution)/shard_map/ppermute | solution.py:68
  16.8 29.1 %collective-permute-start.7 = (bf16[36,2176]{1,0:T(8,128)(2,1)}, bf16[36,2176]{1,0:T(8,128)(2,1)S(1)}, u32[]{:S(2)}, u32[]{:S(2)}) collective-permute-start(bf16[36,2176]{1,0:T(8,128)(2,1)} %bitcast.77), channel_id=1, source_target_pairs={{35,0},{32,1},{33,2},{34,3},{67,32},{64,33},{65,34},{66,35},{99,64... | collective-permute-start | bytes 470024 | tf_op jit(solution)/shard_map/ppermute | solution.py:68
  20.6 25.3 %collective-permute-start.6 = (bf16[36,2176]{1,0:T(8,128)(2,1)}, bf16[36,2176]{1,0:T(8,128)(2,1)S(1)}, u32[]{:S(2)}, u32[]{:S(2)}) collective-permute-start(bf16[36,2176]{1,0:T(8,128)(2,1)} %bitcast.78), channel_id=1, source_target_pairs={{32,0},{33,1},{34,2},{35,3},{64,32},{65,33},{66,34},{67,35},{96,64... | collective-permute-start | bytes 470024 | tf_op jit(solution)/shard_map/ppermute | solution.py:68
  23.8 98.0 %collective-permute-start.10 = (f32[1,1152]{1,0:T(1,128)}, f32[1,1152]{1,0:T(1,128)S(1)}, u32[]{:S(2)}, u32[]{:S(2)}) collective-permute-start(f32[1,1152]{1,0:T(1,128)} %param.11), channel_id=1, source_target_pairs={{32,0},{64,32},{96,64},{128,96},{160,128},{192,160},{224,192},{256... | collective-permute-start | bytes 13832 | tf_op jit(solution)/shard_map/ppermute | solution.py:14
  34.9 12.2 %copy-start.1 = (bf16[1,16,32,1152]{3,2,1,0:T(8,128)(2,1)S(1)}, bf16[1,16,32,1152]{3,2,1,0:T(8,128)(2,1)}, u32[]{:S(2)}) copy-start(bf16[1,16,32,1152]{3,2,1,0:T(8,128)(2,1)} %param.9) | copy-start | bytes 3538948
  35.8 23.7 %all-to-all-start = ((bf16[8,2,13568]{2,1,0:T(2,128)(2,1)}), bf16[8,2,13568]{2,1,0:T(2,128)(2,1)S(1)}, u32[]{:S(2)}, u32[]{:S(2)}) async-start(bf16[8,2,13568]{2,1,0:T(2,128)(2,1)} %reshape.298), calls=%async_computation | async-start | bytes 868352 | tf_op jit(solution)/shard_map/all_to_all | solution.py:55
  45.8 13.7 %copy-start.4 = (bf16[1,68,1152]{2,1,0:T(8,128)(2,1)S(1)}, bf16[1,68,1152]{2,1,0:T(8,128)(2,1)}, u32[]{:S(2)}) copy-start(bf16[1,68,1152]{2,1,0:T(8,128)(2,1)} %param.13) | copy-start | bytes 470020
  45.8 138.9 %all-gather.2.cloned.1.call-start = ((), (), s32[]{:S(2)}) async-start(), calls=%async_computation.5 | async-start | bytes 5640192 | tf_op jit(solution)/shard_map/all_gather | solution.py:104
  60.4 20.3 %all-to-all-start.1 = ((bf16[4,68,1152]{2,1,0:T(8,128)(2,1)}), bf16[4,68,1152]{2,1,0:T(8,128)(2,1)S(1)}, u32[]{:S(2)}, u32[]{:S(2)}) async-start(bf16[4,68,1152]{2,1,0:T(8,128)(2,1)} %broadcast_in_dim.30), calls=%async_computation.1 | async-start | bytes 1327104 | tf_op jit(solution)/shard_map/all_to_all | solution.py:97
  82.1 15.8 %collective-permute-start.2 = (bf16[128,1152]{1,0:T(8,128)(2,1)S(1)}, bf16[128,1152]{1,0:T(8,128)(2,1)S(1)}, u32[]{:S(2)}, u32[]{:S(2)}) collective-permute-start(bf16[128,1152]{1,0:T(8,128)(2,1)S(1)} %reshape.282), channel_id=1, source_target_pairs={{3,0},{0,1},{1,2},{2,3},{7,4},{4,5},{5,6},{6,7},{11,8},{8,9},{9,10... | collective-permute-start | bytes 884744 | tf_op jit(solution)/shard_map/ppermute | solution.py:14
  85.1 14.7 %collective-permute-start.1 = (bf16[128,1152]{1,0:T(8,128)(2,1)S(1)}, bf16[128,1152]{1,0:T(8,128)(2,1)S(1)}, u32[]{:S(2)}, u32[]{:S(2)}) collective-permute-start(bf16[128,1152]{1,0:T(8,128)(2,1)S(1)} %reshape.282), channel_id=1, source_target_pairs={{2,0},{3,1},{0,2},{1,3},{6,4},{7,5},{4,6},{5,7},{10,8},{11,9},{8,1... | collective-permute-start | bytes 884744 | tf_op jit(solution)/shard_map/ppermute | solution.py:14
  87.0 23.5 %collective-permute-start = (bf16[128,1152]{1,0:T(8,128)(2,1)S(1)}, bf16[128,1152]{1,0:T(8,128)(2,1)S(1)}, u32[]{:S(2)}, u32[]{:S(2)}) collective-permute-start(bf16[128,1152]{1,0:T(8,128)(2,1)S(1)} %reshape.282), channel_id=1, source_target_pairs={{1,0},{2,1},{3,2},{0,3},{5,4},{6,5},{7,6},{4,7},{9,8},{10,9},{11,1... | collective-permute-start | bytes 884744 | tf_op jit(solution)/shard_map/ppermute | solution.py:14
  92.4 23.0 %all-to-all-start.2 = ((bf16[8,16,1152]{2,1,0:T(8,128)(2,1)}), bf16[8,16,1152]{2,1,0:T(8,128)(2,1)S(1)}, u32[]{:S(2)}, u32[]{:S(2)}) async-start(bf16[8,16,1152]{2,1,0:T(8,128)(2,1)} %bitcast.9), calls=%async_computation.2 | async-start | bytes 589824 | tf_op jit(solution)/shard_map/all_to_all | solution.py:55
  110.6 25.7 %collective-permute-start.4 = (bf16[1,16,32,1152]{3,2,1,0:T(8,128)(2,1)}, bf16[1,16,32,1152]{3,2,1,0:T(8,128)(2,1)S(1)}, u32[]{:S(2)}, u32[]{:S(2)}) collective-permute-start(bf16[1,16,32,1152]{3,2,1,0:T(8,128)(2,1)} %param.9), channel_id=1, source_target_pairs={{32,0},{64,32},{96,64},{128,96},{160,128},{192,160},{224,192},{256... | collective-permute-start | bytes 3538952 | tf_op jit(solution)/shard_map/ppermute | solution.py:14
  117.4 19.6 %all-to-all-start.3 = ((bf16[8,32,1152]{2,1,0:T(8,128)(2,1)}), bf16[8,32,1152]{2,1,0:T(8,128)(2,1)}, u32[]{:S(2)}, u32[]{:S(2)}) async-start(bf16[8,32,1152]{2,1,0:T(8,128)(2,1)} %broadcast_in_dim.31), calls=%async_computation.3 | async-start | bytes 1179648 | tf_op jit(solution)/shard_map/all_to_all | solution.py:55
  122.8 14.2 %copy-start = (bf16[272,1152,1]{1,0,2:T(8,128)(2,1)S(1)}, bf16[272,1152,1]{1,0,2:T(8,128)(2,1)}, u32[]{:S(2)}) copy-start(bf16[272,1152,1]{1,0,2:T(8,128)(2,1)} %reshape.294) | copy-start | bytes 1880068
  122.8 57.7 %collective-permute-start.5 = (bf16[1,16,32,2176]{3,2,1,0:T(8,128)(2,1)}, bf16[1,16,32,2176]{3,2,1,0:T(8,128)(2,1)}, u32[]{:S(2)}, u32[]{:S(2)}) collective-permute-start(bf16[1,16,32,2176]{3,2,1,0:T(8,128)(2,1)} %param.10), channel_id=1, source_target_pairs={{32,0},{64,32},{96,64},{128,96},{160,128},{192,160},{224,192},{256... | collective-permute-start | bytes 6684680 | tf_op jit(solution)/shard_map/ppermute | solution.py:14
  136.5 30.6 %copy-start.2 = (bf16[1,16,1152]{2,1,0:T(8,128)(2,1)S(1)}, bf16[1,16,1152]{2,1,0:T(8,128)(2,1)}, u32[]{:S(2)}) copy-start(bf16[1,16,1152]{2,1,0:T(8,128)(2,1)} %param.14) | copy-start | bytes 110596
  139.1 28.3 %all-to-all-start.4 = ((f32[8,16,272]{2,1,0:T(8,128)}), f32[8,16,272]{2,1,0:T(8,128)S(1)}, u32[]{:S(2)}, u32[]{:S(2)}) async-start(f32[8,16,272]{2,1,0:T(8,128)} %fusion.35), calls=%async_computation.4 | async-start | bytes 393216 | tf_op jit(solution)/shard_map/all_to_all | solution.py:55
  144.0 19.4 %collective-permute-start.11 = (f32[16,1152]{1,0:T(8,128)S(1)}, f32[16,1152]{1,0:T(8,128)S(1)}, u32[]{:S(2)}, u32[]{:S(2)}) collective-permute-start(f32[16,1152]{1,0:T(8,128)S(1)} %get-tuple-element.26), channel_id=1, source_target_pairs={{3,0},{0,1},{1,2},{2,3},{7,4},{4,5},{5,6},{6,7},{11,8},{8,9},{9,10... | collective-permute-start | bytes 221192 | tf_op jit(solution)/shard_map/ppermute | solution.py:14
  156.1 7.3 %collective-permute-start.13 = (f32[16,1152]{1,0:T(8,128)S(1)}, f32[16,1152]{1,0:T(8,128)S(1)}, u32[]{:S(2)}, u32[]{:S(2)}) collective-permute-start(f32[16,1152]{1,0:T(8,128)S(1)} %get-tuple-element.27), channel_id=1, source_target_pairs={{1,0},{2,1},{3,2},{0,3},{5,4},{6,5},{7,6},{4,7},{9,8},{10,9},{11,1... | collective-permute-start | bytes 221192 | tf_op jit(solution)/shard_map/ppermute | solution.py:14
  158.0 9.1 %collective-permute-start.12 = (f32[16,1152]{1,0:T(8,128)S(1)}, f32[16,1152]{1,0:T(8,128)S(1)}, u32[]{:S(2)}, u32[]{:S(2)}) collective-permute-start(f32[16,1152]{1,0:T(8,128)S(1)} %get-tuple-element.28), channel_id=1, source_target_pairs={{2,0},{3,1},{0,2},{1,3},{6,4},{7,5},{4,6},{5,7},{10,8},{11,9},{8,1... | collective-permute-start | bytes 221192 | tf_op jit(solution)/shard_map/ppermute | solution.py:14
  167.6 12.3 %collective-permute-start.3 = (f32[16,3328]{1,0:T(8,128)S(1)}, f32[16,3328]{1,0:T(8,128)S(1)}, u32[]{:S(2)}, u32[]{:S(2)}) collective-permute-start(f32[16,3328]{1,0:T(8,128)S(1)} %pad_maximum_fusion.2), channel_id=1, source_target_pairs={{32,0},{64,32},{96,64},{128,96},{160,128},{192,160},{224,192},{256... | collective-permute-start | bytes 638984 | tf_op jit(solution)/shard_map/ppermute | solution.py:14
  179.8 0.7 copy-start.3
  190.6 0.9 slice-start
Sparse Core Ops, SparseCore 0:
  48.7 69.7 all-gather.1

commit v3 on v1

v3 whole, which is shorter than its diff:
```python
import functools

import jax
import jax.numpy as jnp
from jax import lax
from jax.experimental import pallas as pl
from jax.experimental.pallas import tpu as pltpu
from jax.sharding import Mesh, PartitionSpec as P

EPSILON = 1e-06
TANH_SCALE = 0.7978845608028654
CUBIC_TERM = 0.044715
Y_SHARDS = 4
ROW_TILE = 8
IMAGE_BLOCK = 8
VMEM_BYTES = 50 * 1024 * 1024


def from_ahead(array, axis, by):
    peers = lax.axis_size(axis)
    return lax.ppermute(array, axis, [((i + by) % peers, i) for i in range(peers)])


def gelu_slope(preact):
    inner = TANH_SCALE * (preact + CUBIC_TERM * preact * preact * preact)
    tangent = jnp.tanh(inner)
    return 0.5 * (1.0 + tangent) + 0.5 * preact * (1.0 - tangent * tangent) * TANH_SCALE * (
        1.0 + 3.0 * CUBIC_TERM * preact * preact
    )


def unit_rows(values):
    inverse = lax.rsqrt(jnp.sum(values * values, axis=-1, keepdims=True) + EPSILON)
    return (values * inverse, inverse)


def pair_weights(image_unit, text_unit, image_index, text_index, sharpness, shift, factor):
    logits = (
        sharpness
        * lax.dot_general(
            image_unit, text_unit, (((1,), (1,)), ((), ())), preferred_element_type=jnp.float32
        )
        + shift
    )
    signs = jnp.where(image_index[:, None] == text_index[None, :], 1.0, -1.0).astype(jnp.float32)
    return (factor * -signs * jax.nn.sigmoid(-signs * logits)).astype(jnp.bfloat16)


def norm_backward(tokens, normed_grad, layernorm_multiplier):
    centered = tokens - jnp.mean(tokens, axis=-1, keepdims=True)
    inverse = lax.rsqrt(jnp.mean(centered * centered, axis=-1, keepdims=True) + EPSILON)
    normal = centered * inverse
    scaled = normed_grad * layernorm_multiplier
    return inverse * (
        scaled
        - jnp.mean(scaled, axis=-1, keepdims=True)
        - normal * jnp.mean(scaled * normal, axis=-1, keepdims=True)
    )


def slope_kernel(preact_ref, slope_ref):
    slope_ref[...] = gelu_slope(preact_ref[...].astype(jnp.float32))


def slopes(preact):
    tokens, hidden = preact.shape
    block = tokens // 4
    spec = pl.BlockSpec((block, hidden), lambda i: (i, 0))
    return pl.pallas_call(
        slope_kernel,
        grid=(tokens // block,),
        in_specs=[spec],
        out_specs=spec,
        out_shape=jax.ShapeDtypeStruct((tokens, hidden), jnp.float32),
        compiler_params=pltpu.CompilerParams(vmem_limit_bytes=VMEM_BYTES),
        cost_estimate=pl.CostEstimate(
            flops=20 * tokens * hidden, bytes_accessed=6 * tokens * hidden, transcendentals=0
        ),
    )(preact)


def span_kernel(
    pieces, grad_ref, slope_ref, up_ref, tokens_ref, share_ref, multiplier_ref, span_ref, hidden_ref
):
    @pl.when(pl.program_id(0) == 0)
    def _():
        hidden_ref[...] = jnp.concatenate(
            [grad_ref[y, :, start:end] for y, start, end in pieces], axis=1
        ).reshape(hidden_ref.shape)

    step = pl.program_id(0)
    tokens = tokens_ref[...].astype(jnp.float32)
    rows, width = tokens.shape
    count = IMAGE_BLOCK
    patches = rows // count
    hidden = hidden_ref.shape[2]
    grads = hidden_ref[step]
    slope = slope_ref[...].reshape(count, patches, hidden)
    preact_grad = (grads[:, None, :] * slope).astype(jnp.bfloat16).reshape(rows, hidden)
    normed = lax.dot_general(
        preact_grad, up_ref[...], (((1,), (1,)), ((), ())), preferred_element_type=jnp.float32
    )
    inner = norm_backward(tokens, normed, multiplier_ref[...])
    share = share_ref[step]
    span_ref[...] = (
        (share[:, None, :] + inner.reshape(count, patches, width))
        .astype(jnp.bfloat16)
        .reshape(rows, width)
    )


def span(received, pieces, slope, up_whole, tokens, share, multiplier):
    count, width = tokens.shape
    images = share.shape[0]
    share = share.reshape(images // IMAGE_BLOCK, IMAGE_BLOCK, width)
    hidden = slope.shape[1]
    rows = IMAGE_BLOCK * (count // images)
    whole = lambda array: pl.BlockSpec(array.shape, lambda i: (0,) * array.ndim)
    block = lambda columns: pl.BlockSpec((rows, columns), lambda i: (i, 0))
    return pl.pallas_call(
        functools.partial(span_kernel, pieces),
        grid=(count // rows,),
        in_specs=[
            whole(received),
            block(hidden),
            whole(up_whole),
            block(width),
            whole(share),
            whole(multiplier),
        ],
        out_specs=block(width),
        out_shape=jax.ShapeDtypeStruct((count, width), jnp.bfloat16),
        scratch_shapes=[pltpu.VMEM((images // IMAGE_BLOCK, IMAGE_BLOCK, hidden), jnp.float32)],
        compiler_params=pltpu.CompilerParams(vmem_limit_bytes=VMEM_BYTES),
        cost_estimate=pl.CostEstimate(
            flops=2 * count * hidden * width,
            bytes_accessed=4 * count * hidden + 2 * hidden * width + 4 * count * width,
            transcendentals=0,
        ),
    )(received, slope, up_whole, tokens, share, multiplier)


def exchange_y(blocks):
    return lax.all_to_all(blocks, "y", 0, 0)


def in_order_of_y(ahead, y):
    placed = [
        lax.select_n(y, *[ahead[(a - own) % Y_SHARDS] for own in range(Y_SHARDS)])
        for a in range(Y_SHARDS)
    ]
    return jnp.concatenate(placed, axis=0)


def per_device(
    feedforward_entry_states,
    stored_hidden_preacts,
    layernorm_multiplier,
    expanding_projector,
    contracting_projector,
    caption_tower_outputs,
    similarity_sharpness,
    similarity_shift_term,
    objective_upstream_grad,
):
    images, patches, model_width = feedforward_entry_states.shape[1:]
    hidden = stored_hidden_preacts.shape[-1]
    z, y = lax.axis_index("z"), lax.axis_index("y")
    z_size = lax.axis_size("z")
    shard_rows = contracting_projector.shape[1]
    shard_end = images + shard_rows
    block_rows = -(-shard_end // ROW_TILE) * ROW_TILE
    part = z_size * block_rows
    row = images * Y_SHARDS
    sharpness = similarity_sharpness[0]
    shift = similarity_shift_term[0]
    factor = objective_upstream_grad[0] * sharpness

    block = jnp.concatenate(
        [
            caption_tower_outputs[0],
            contracting_projector[0],
            jnp.zeros((block_rows - shard_end, model_width), jnp.bfloat16),
        ],
        axis=0,
    )
    blocks = lax.all_gather(block, "z", axis=0, tiled=True)

    tokens = feedforward_entry_states[0].reshape(images * patches, model_width).astype(jnp.float32)
    preact = stored_hidden_preacts[0].astype(jnp.float32)
    activated = jax.nn.gelu(preact, approximate=True).astype(jnp.bfloat16).astype(jnp.float32)
    mean_activated = jnp.mean(activated, axis=1)
    mean_tokens = jnp.mean(tokens.reshape(images, patches, model_width), axis=1)

    mean_sent = (
        jnp.pad(
            mean_activated.reshape(images, z_size, Y_SHARDS, shard_rows),
            ((0, 0), (0, 0), (0, 0), (images, block_rows - shard_end)),
        )
        .transpose(2, 0, 1, 3)
        .reshape(Y_SHARDS, images, part)
    )

    mean_sent, up_shard = lax.optimization_barrier((mean_sent, expanding_projector[0]))
    up_y = in_order_of_y(
        [up_shard] + [from_ahead(up_shard, "y", k) for k in range(1, Y_SHARDS)], y
    )
    up_whole = lax.all_gather(up_y, "z", axis=0, tiled=True)

    row_mean = exchange_y(mean_sent).reshape(row, part)
    row_high = row_mean.astype(jnp.bfloat16)
    row_low = (row_mean - row_high.astype(jnp.float32)).astype(jnp.bfloat16)
    partial = jnp.dot(row_high, blocks, preferred_element_type=jnp.float32) + jnp.dot(
        row_low, blocks, preferred_element_type=jnp.float32
    )
    partials = exchange_y(partial.astype(jnp.bfloat16).reshape(Y_SHARDS, images, model_width))
    column_text = blocks.reshape(z_size, block_rows, model_width)[:, :images]
    column_text = unit_rows(
        column_text.reshape(z_size * images, model_width).astype(jnp.float32)
    )[0].astype(jnp.bfloat16)
    text_all = jnp.concatenate(
        [column_text] + [from_ahead(column_text, "y", k) for k in range(1, Y_SHARDS)], axis=0
    )
    pooled = mean_tokens + jnp.sum(partials.astype(jnp.float32), axis=0)
    image_dir, image_inverse = unit_rows(pooled)
    image_unit = image_dir.astype(jnp.bfloat16)

    def index_of(z_index, y_index):
        start = (z_index * Y_SHARDS + y_index) * images
        return start[..., None] + lax.iota(jnp.int32, images)

    def weigh(image_rows, image_index, text_rows, text_index):
        return pair_weights(
            image_rows, text_rows, image_index, text_index, sharpness, shift, factor
        )

    weights = weigh(
        image_unit,
        index_of(z, y).reshape(-1),
        text_all,
        index_of(
            lax.broadcasted_iota(jnp.int32, (Y_SHARDS, z_size), 1),
            (y + lax.broadcasted_iota(jnp.int32, (Y_SHARDS, z_size), 0)) % Y_SHARDS,
        ).reshape(-1),
    )
    image_sum = jnp.dot(weights, text_all, preferred_element_type=jnp.float32)
    pooled_grad = (
        image_sum - image_dir * jnp.sum(image_dir * image_sum, axis=-1, keepdims=True)
    ) * image_inverse
    share = pooled_grad / patches
    token_grad = share.astype(jnp.bfloat16)

    preacts, row_grad = lax.optimization_barrier((stored_hidden_preacts[0], token_grad))
    slope = slopes(preacts.reshape(images * patches, hidden))
    row_sent = jnp.concatenate([row_grad, image_unit], axis=0)
    rows = exchange_y(jnp.broadcast_to(row_sent[None], (Y_SHARDS,) + row_sent.shape))
    row_grad = rows[:, :images].reshape(row, model_width)
    row_unit = rows[:, images:].reshape(row, model_width)
    row_hidden = lax.dot_general(
        row_grad, blocks, (((1,), (1,)), ((), ())), preferred_element_type=jnp.float32
    )
    received = exchange_y(row_hidden.reshape(Y_SHARDS, images, part))
    column_weights = weigh(
        row_unit,
        index_of(z, jnp.arange(Y_SHARDS, dtype=jnp.int32)).reshape(-1),
        column_text,
        index_of(jnp.arange(z_size, dtype=jnp.int32), y).reshape(-1),
    )
    column_sums = lax.dot_general(
        column_weights, row_unit, (((0,), (0,)), ((), ())), preferred_element_type=jnp.float32
    ).reshape(z_size, images, model_width)
    pieces = [
        (own, at * block_rows + images, at * block_rows + shard_end)
        for at in range(z_size)
        for own in range(Y_SHARDS)
    ]
    span_grad = span(
        received,
        pieces,
        slope,
        up_whole,
        feedforward_entry_states.reshape(images * patches, model_width),
        share,
        layernorm_multiplier,
    ).reshape(images, patches, model_width)
    column_sums, span_grad = lax.optimization_barrier((column_sums, span_grad))
    text_sums = lax.all_to_all(column_sums, "z", 0, 0)
    prev_grad = from_ahead(span_grad[None], "section", 1)

    text_sum = jnp.sum(text_sums, axis=0)
    text_dir, text_inverse = unit_rows(caption_tower_outputs[0].astype(jnp.float32))
    text_grad = (
        (text_sum - text_dir * jnp.sum(text_dir * text_sum, axis=-1, keepdims=True)) * text_inverse
    ).astype(jnp.bfloat16)
    return (prev_grad, text_grad[None])


def solution(mesh):
    sections, shards = mesh.devices.shape
    folded = Mesh(
        mesh.devices.reshape(sections, shards // Y_SHARDS, Y_SHARDS), ("section", "z", "y")
    )
    dp = ("z", "y")
    placed = (
        P("section", dp, None, None),
        P("section", dp, None, None),
        P("section", None),
        P("section", dp, None),
        P("section", dp, None),
        P("section", dp, None),
        P(),
        P(),
        P(),
    )
    return jax.shard_map(
        per_device,
        mesh=folded,
        in_specs=placed,
        out_specs=(P("section", dp, None, None), P("section", dp, None)),
        check_vma=False,
    )
```

time: 212 us -> 182 us (0.86)
  starting transfers between devices: 76.9 us -> 59.1 us
  waiting for transfers between devices: 72.3 us -> 60.2 us
  Pallas kernels: 0 us -> 11.9 us
  local copies, waits for them, and re-layouts: 14.6 us -> 8.46 us
  matrix products: 14.3 us -> 10.9 us
  other arithmetic: 16.5 us -> 13.1 us
    ppermute x13 -> x7, starting transfers between devices: 51.4 us -> 32.2 us  [from_ahead(): lax.ppermute(array, axis, [((i + by) % peers, i) for i in range(peers)])]
    all_to_all x5, waiting for transfers between devices: 47.6 us -> 31 us  [the longest x4 16.5 us: exchange_y(): return lax.all_to_all(blocks, 'y', 0, 0)]
    pallas_call x0 -> x2, Pallas kernels: none -> 11.9 us  [the longest x1 7.7 us: span(): pl.pallas_call(functools.partial(span_kernel, pieces), grid=(count // row...]
    dot_general x5, matrix products: 13.5 us -> 7.16 us  [the longest x1 2.8 us: per_device(): lax.dot_general(row_grad, blocks, (((1,), (1,)), ((), ())), preferred_ele...]
    all_gather x0 -> x1, waiting for transfers between devices: none -> 4.59 us  [per_device(): blocks = lax.all_gather(block, 'z', axis=0, tiled=True)]
    dot_general x1, matrix products: 0.79 us -> 3.73 us  [per_device(): image_sum = jnp.dot(weights, text_all, preferred_element_type=jnp.float32)]
    concatenate x1 -> x3, other arithmetic: 0.94 us -> 3.43 us  [the longest x1 1.71 us: per_device(): jnp.concatenate([caption_tower_outputs[0], contracting_projector[0], jnp....]
    convert_element_type x4 -> x5, other arithmetic: 4.96 us -> 2.67 us  [the longest x2 1.91 us: per_device(): column_text = unit_rows(column_text.reshape(z_size * images, model_width)...]
  transfers between devices with their start and end apart: 19 -> 14, of which waited for: 9 -> 10; matrix products, arithmetic and copies ran while one was open for 17% -> 15% of each run, Pallas kernels for 0% -> 2%
where the time goes in v3:
time: 182 us; the launch traced here: 180 us
  waiting for transfers between devices  60.2 us (33%)
  starting transfers between devices  59.1 us (32%)
  between operations  16.3 us (9%)
  other arithmetic  13.1 us (7%)
  Pallas kernels  11.9 us (7%)
  matrix products  10.9 us (6%)
  local copies, waits for them, and re-layouts  8.46 us (5%)
    ppermute x7, starting transfers between devices, from_ahead(): lax.ppermute(array, axis, [((i + by) % peers, i) for i in range(peers)])  32.2 us
    ppermute x7, waiting for transfers between devices, from_ahead(): lax.ppermute(array, axis, [((i + by) % peers, i) for i in range(peers)])  24.6 us
    all_to_all x4, starting transfers between devices, exchange_y(): return lax.all_to_all(blocks, 'y', 0, 0)  20.6 us
    all_to_all x4, waiting for transfers between devices, exchange_y(): return lax.all_to_all(blocks, 'y', 0, 0)  16.5 us
    all_to_all x1, waiting for transfers between devices, per_device(): text_sums = lax.all_to_all(column_sums, 'z', 0, 0)  14.4 us
    pallas_call x1, Pallas kernels, span(): pl.pallas_call(functools.partial(span_kernel, pieces), grid=(count // row...  7.7 us
    all_to_all x1, starting transfers between devices, per_device(): text_sums = lax.all_to_all(column_sums, 'z', 0, 0)  6.29 us
    all_gather x1, waiting for transfers between devices, per_device(): blocks = lax.all_gather(block, 'z', axis=0, tiled=True)  4.59 us
  transfers between devices with their start and end apart: 14, of which 10 were waited for; matrix products, arithmetic and copies ran while one was open for 15% of the time, Pallas kernels for 2%

profile of v3, /device:TPU:6, one launch (start us, length us, event | category | flops | bytes accessed | tf_op | source)
XLA Modules:
  0.0 180.0 jit_solution(6925135280329882253)
XLA Ops:
  7.2 0.1 pad.17.clone
  7.3 1.7 maximum_maximum_fusion
  9.0 0.0 all-gather.5.cloned.1.call-start
  9.1 3.4 %convert_reduce_fusion = f32[16,2176]{1,0:T(8,128)S(1)} fusion(bf16[1,16,32,2176]{3,2,1,0:T(8,128)(2,1)} %param.10), kind=kLoop, calls=%fused_computation.10 | loop fusion | flops 13334528 | bytes 2367488 | tf_op jit(solution)/shard_map/reduce_sum | solution.py:192
  12.5 0.4 div.24
  13.0 0.2 pad_bitcast_fusion
  13.2 0.8 reshape.199
  14.0 7.7 %collective-permute-start.4 = (bf16[36,2176]{1,0:T(8,128)(2,1)S(1)}, bf16[36,2176]{1,0:T(8,128)(2,1)S(1)}, u32[]{:S(2)}, u32[]{:S(2)}) collective-permute-start(bf16[36,2176]{1,0:T(8,128)(2,1)S(1)} %bitcast.70), channel_id=1, source_target_pairs={{2,0},{3,1},{0,2},{1,3},{6,4},{7,5},{4,6},{5,7},{10,8},{11,9},{8,1... | collective-permute-start | bytes 470024 | tf_op jit(solution)/shard_map/ppermute | solution.py:21
  21.7 2.2 %collective-permute-start.5 = (bf16[36,2176]{1,0:T(8,128)(2,1)S(1)}, bf16[36,2176]{1,0:T(8,128)(2,1)S(1)}, u32[]{:S(2)}, u32[]{:S(2)}) collective-permute-start(bf16[36,2176]{1,0:T(8,128)(2,1)S(1)} %bitcast.71), channel_id=1, source_target_pairs={{1,0},{2,1},{3,2},{0,3},{5,4},{6,5},{7,6},{4,7},{9,8},{10,9},{11,1... | collective-permute-start | bytes 470024 | tf_op jit(solution)/shard_map/ppermute | solution.py:21
  24.0 4.5 %collective-permute-start.3 = (bf16[36,2176]{1,0:T(8,128)(2,1)S(1)}, bf16[36,2176]{1,0:T(8,128)(2,1)S(1)}, u32[]{:S(2)}, u32[]{:S(2)}) collective-permute-start(bf16[36,2176]{1,0:T(8,128)(2,1)S(1)} %bitcast.72), channel_id=1, source_target_pairs={{3,0},{0,1},{1,2},{2,3},{7,4},{4,5},{5,6},{6,7},{11,8},{8,9},{9,10... | collective-permute-start | bytes 470024 | tf_op jit(solution)/shard_map/ppermute | solution.py:21
  28.5 0.1 collective-permute-done.4
  28.6 9.4 %collective-permute-done.5 = bf16[36,2176]{1,0:T(8,128)(2,1)S(1)} collective-permute-done((bf16[36,2176]{1,0:T(8,128)(2,1)S(1)}, bf16[36,2176]{1,0:T(8,128)(2,1)S(1)}, u32[]{:S(2)}, u32[]{:S(2)}) %collective-permute-start.5) | collective-permute-done | bytes 156704 | tf_op jit(solution)/shard_map/ppermute | solution.py:21
  38.0 0.1 select_select_fusion.3
  38.1 0.9 pad_maximum_fusion.3
  39.1 4.5 %all-to-all-start = ((f32[4,16,704]{2,1,0:T(8,128)}), f32[4,16,704]{2,1,0:T(8,128)S(1)}, u32[]{:S(2)}, u32[]{:S(2)}) async-start(f32[4,16,704]{2,1,0:T(8,128)} %reshape.199), calls=%async_computation | async-start | bytes 393216 | tf_op jit(solution)/shard_map/all_to_all | solution.py:144
  45.0 0.1 add_multiply_fusion
  45.1 0.1 iota_add_fusion
  45.1 0.7 add.207
  46.5 0.1 iota_add_fusion.1
  46.6 0.6 add.194
  47.2 0.1 iota_add_fusion.2
  47.3 0.7 add.188
  47.9 0.6 iota_add_fusion.3
  48.5 0.3 convert_reduce_fusion.1
  48.8 5.0 %all-to-all-done = f32[4,16,704]{2,1,0:T(8,128)S(1)} async-done(((f32[4,16,704]{2,1,0:T(8,128)}), f32[4,16,704]{2,1,0:T(8,128)S(1)}, u32[]{:S(2)}, u32[]{:S(2)}) %all-to-all-start) | async-done | bytes 180256 | tf_op jit(solution)/shard_map/all_to_all | solution.py:144
  53.8 4.6 %all-gather.3.cloned.1.call-done = bf16[704,1152]{1,0:T(8,128)(2,1)} async-done(((bf16[88,1152]{1,0:T(8,128)(2,1)}), bf16[704,1152]{1,0:T(8,128)(2,1)}) %all-gather.3.cloned.1.call-update) | async-done | bytes 1622032 | tf_op jit(solution)/shard_map/all_gather | solution.py:187
  58.4 2.0 %fusion.52 = f32[64,1152]{1,0:T(8,128)S(1)} fusion(bf16[64,704]{1,0:T(8,128)(2,1)S(1)} %get-tuple-element.17, bf16[704,1152]{1,0:T(8,128)(2,1)} %all-gather.3.cloned.1.call-done), kind=kOutput, calls=%fused_computation.100 | convolution fusion | flops 103809024 | bytes 2007040 | tf_op jit(solution)/shard_map/dot_general | solution.py:213
  60.3 1.1 fusion.6
  61.4 6.7 %all-to-all-start.1 = ((bf16[4,16,1152]{2,1,0:T(8,128)(2,1)}), bf16[4,16,1152]{2,1,0:T(8,128)(2,1)S(1)}, u32[]{:S(2)}, u32[]{:S(2)}) async-start(bf16[4,16,1152]{2,1,0:T(8,128)(2,1)} %bitcast.10), calls=%async_computation.1 | async-start | bytes 294912 | tf_op jit(solution)/shard_map/all_to_all | solution.py:144
  68.1 0.1 multiply_reduce_fusion
  68.3 0.1 rsqrt.30
  68.4 0.1 fusion.26
  68.5 4.8 %collective-permute-start.2 = (bf16[128,1152]{1,0:T(8,128)(2,1)S(1)}, bf16[128,1152]{1,0:T(8,128)(2,1)S(1)}, u32[]{:S(2)}, u32[]{:S(2)}) collective-permute-start(bf16[128,1152]{1,0:T(8,128)(2,1)S(1)} %fusion.26), channel_id=1, source_target_pairs={{3,0},{0,1},{1,2},{2,3},{7,4},{4,5},{5,6},{6,7},{11,8},{8,9},{9,10... | collective-permute-start | bytes 884744 | tf_op jit(solution)/shard_map/ppermute | solution.py:21
  73.4 5.5 %collective-permute-start.1 = (bf16[128,1152]{1,0:T(8,128)(2,1)S(1)}, bf16[128,1152]{1,0:T(8,128)(2,1)S(1)}, u32[]{:S(2)}, u32[]{:S(2)}) collective-permute-start(bf16[128,1152]{1,0:T(8,128)(2,1)S(1)} %fusion.26), channel_id=1, source_target_pairs={{2,0},{3,1},{0,2},{1,3},{6,4},{7,5},{4,6},{5,7},{10,8},{11,9},{8,1... | collective-permute-start | bytes 884744 | tf_op jit(solution)/shard_map/ppermute | solution.py:21
  78.8 5.5 %collective-permute-start = (bf16[128,1152]{1,0:T(8,128)(2,1)S(1)}, bf16[128,1152]{1,0:T(8,128)(2,1)S(1)}, u32[]{:S(2)}, u32[]{:S(2)}) collective-permute-start(bf16[128,1152]{1,0:T(8,128)(2,1)S(1)} %fusion.26), channel_id=1, source_target_pairs={{1,0},{2,1},{3,2},{0,3},{5,4},{6,5},{7,6},{4,7},{9,8},{10,9},{11,1... | collective-permute-start | bytes 884744 | tf_op jit(solution)/shard_map/ppermute | solution.py:21
  84.4 0.1 multiply_reduce_fusion.2
  84.5 0.7 multiply_convert_fusion.1
  85.2 5.8 %collective-permute-done.2 = bf16[128,1152]{1,0:T(8,128)(2,1)S(1)} collective-permute-done((bf16[128,1152]{1,0:T(8,128)(2,1)S(1)}, bf16[128,1152]{1,0:T(8,128)(2,1)S(1)}, u32[]{:S(2)}, u32[]{:S(2)}) %collective-permute-start.2) | collective-permute-done | bytes 294944 | tf_op jit(solution)/shard_map/ppermute | solution.py:21
  91.0 4.8 %collective-permute-done.1 = bf16[128,1152]{1,0:T(8,128)(2,1)S(1)} collective-permute-done((bf16[128,1152]{1,0:T(8,128)(2,1)S(1)}, bf16[128,1152]{1,0:T(8,128)(2,1)S(1)}, u32[]{:S(2)}, u32[]{:S(2)}) %collective-permute-start.1) | collective-permute-done | bytes 294944 | tf_op jit(solution)/shard_map/ppermute | solution.py:21
  95.7 4.5 %collective-permute-done = bf16[128,1152]{1,0:T(8,128)(2,1)S(1)} collective-permute-done((bf16[128,1152]{1,0:T(8,128)(2,1)S(1)}, bf16[128,1152]{1,0:T(8,128)(2,1)S(1)}, u32[]{:S(2)}, u32[]{:S(2)}) %collective-permute-start) | collective-permute-done | bytes 294944 | tf_op jit(solution)/shard_map/ppermute | solution.py:21
  100.3 0.7 copy-done.14
  101.0 3.7 %multiply_reduce_fusion.1 = (f32[16]{0:T(128)}, f32[16,1152]{1,0:T(8,128)}) fusion(f32[16,1152]{1,0:T(8,128)S(1)} %get-tuple-element.15, f32[16]{0:T(128)S(1)} %add_rsqrt_fusion.2, bf16[128,1152]{1,0:T(8,128)(2,1)} %copy-done.12, bf16[128,1152]{1,0:T(8,128)(2,1)} %copy-done.13, bf16[128,1152]{1,0:T(8,128)(2,1)} %copy-done.14, ...), kind=kOutput, calls=%fused_computation.63 | convolution fusion | flops 47376368 | bytes 1329356 | tf_op jit(solution)/shard_map/dot_general | solution.py:246
  104.7 1.0 fusion.50
  105.7 0.8 pad_maximum_fusion.4
  106.5 0.7 broadcast_in_dim.27
  107.2 6.0 %all-to-all-start.2 = ((bf16[4,32,1152]{2,1,0:T(8,128)(2,1)}), bf16[4,32,1152]{2,1,0:T(8,128)(2,1)}, u32[]{:S(2)}, u32[]{:S(2)}) async-start(bf16[4,32,1152]{2,1,0:T(8,128)(2,1)} %broadcast_in_dim.27), calls=%async_computation.2 | async-start | bytes 589824 | tf_op jit(solution)/shard_map/all_to_all | solution.py:144
  113.2 1.8 %multiply_convert_fusion = bf16[8,16,1152]{2,1,0:T(8,128)(2,1)} fusion(f32[8,16]{1,0:T(8,128)} %copy-done.8, bf16[8,88,1152]{2,1,0:T(8,128)(2,1)} %bitcast.63), kind=kLoop, calls=%fused_computation.39 | loop fusion | flops 442368 | bytes 590336 | tf_op jit(solution)/shard_map/convert_element_type | solution.py:220
  115.0 4.2 %shard_map.104.slope_ref = f32[512,2176]{1,0:T(8,128)} custom-call(bf16[512,2176]{1,0:T(8,128)(2,1)S(1)} %bitcast.60), custom_call_target="tpu_custom_call" | custom-call | flops 22282240 | bytes 6684672 | tf_op jit(solution)/shard_map/pallas_call | solution.py:69
  119.2 5.3 %all-to-all-done.2 = bf16[4,32,1152]{2,1,0:T(8,128)(2,1)} async-done(((bf16[4,32,1152]{2,1,0:T(8,128)(2,1)}), bf16[4,32,1152]{2,1,0:T(8,128)(2,1)}, u32[]{:S(2)}, u32[]{:S(2)}) %all-to-all-start.2) | async-done | bytes 294944 | tf_op jit(solution)/shard_map/all_to_all | solution.py:144
  124.5 2.8 %fusion.7 = f32[4,16,704]{2,1,0:T(8,128)} fusion(bf16[704,1152]{1,0:T(8,128)(2,1)} %all-gather.3.cloned.1.call-done, bf16[4,32,1152]{2,1,0:T(8,128)(2,1)} %all-to-all-done.2), kind=kOutput, calls=%fused_computation.14 | convolution fusion | flops 103809024 | bytes 1949696 | tf_op jit(solution)/shard_map/dot_general | solution.py:259
  127.3 3.4 %all-to-all-start.3 = ((f32[4,16,704]{2,1,0:T(8,128)}), f32[4,16,704]{2,1,0:T(8,128)S(1)}, u32[]{:S(2)}, u32[]{:S(2)}) async-start(f32[4,16,704]{2,1,0:T(8,128)} %fusion.7), calls=%async_computation.3 | async-start | bytes 393216 | tf_op jit(solution)/shard_map/all_to_all | solution.py:144
  130.7 0.9 slice.13
  131.6 0.3 fusion.24
  131.9 0.1 copy.14
  132.0 1.0 fusion.53
  133.1 6.3 %all-to-all-done.3.grad_ref = f32[4,16,704]{2,1,0:T(8,128)S(1)} async-done(((f32[4,16,704]{2,1,0:T(8,128)}), f32[4,16,704]{2,1,0:T(8,128)S(1)}, u32[]{:S(2)}, u32[]{:S(2)}) %all-to-all-start.3) | async-done | bytes 180256 | tf_op jit(solution)/shard_map/all_to_all | solution.py:144
  139.4 7.7 %shard_map.105 = bf16[512,1152]{1,0:T(8,128)(2,1)S(1)} custom-call(f32[4,16,704]{2,1,0:T(8,128)S(1)} %all-to-all-done.3.grad_ref, f32[512,2176]{1,0:T(8,128)} %shard_map.104.slope_ref, bf16[1152,2176]{1,0:T(8,128)(2,1)} %all-gather.5.cloned.1.call-done.up_ref, bf16[512,1152]{1,0:T(8,128)(2,1)S(1)} %bitcast.61, ...), custom_call_target="tpu_custom_call" | custom-call | flops 2566914048 | bytes 11829248 | tf_op jit(solution)/shard_map/pallas_call | solution.py:120
  147.1 6.3 %all-to-all-start.4 = ((f32[8,16,1152]{2,1,0:T(8,128)}), f32[8,16,1152]{2,1,0:T(8,128)S(1)}, u32[]{:S(2)}, u32[]{:S(2)}) async-start(f32[8,16,1152]{2,1,0:T(8,128)} %fusion.53), calls=%async_computation.4 | async-start | bytes 1179648 | tf_op jit(solution)/shard_map/all_to_all | solution.py:287
  153.4 1.9 %collective-permute-start.6 = (bf16[1,16,32,1152]{3,2,1,0:T(8,128)(2,1)S(1)}, bf16[1,16,32,1152]{3,2,1,0:T(8,128)(2,1)}, u32[]{:S(2)}, u32[]{:S(2)}) collective-permute-start(bf16[1,16,32,1152]{3,2,1,0:T(8,128)(2,1)S(1)} %bitcast.62), channel_id=1, source_target_pairs={{32,0},{64,32},{96,64},{128,96},{160,128},{192,160},{224,192},{256... | collective-permute-start | bytes 3538952 | tf_op jit(solution)/shard_map/ppermute | solution.py:21
  155.3 0.1 fusion.29
  155.4 14.4 %all-to-all-done.4 = f32[8,16,1152]{2,1,0:T(8,128)S(1)} async-done(((f32[8,16,1152]{2,1,0:T(8,128)}), f32[8,16,1152]{2,1,0:T(8,128)S(1)}, u32[]{:S(2)}, u32[]{:S(2)}) %all-to-all-start.4) | async-done | bytes 589856 | tf_op jit(solution)/shard_map/all_to_all | solution.py:287
  169.9 0.2 fusion.31
  170.1 0.7 fusion.33
  170.8 2.4 %copy.19 = bf16[1,16,32,1152]{3,2,1,0:T(8,128)(2,1)} copy(bf16[1,16,32,1152]{3,2,1,0:T(8,128)(2,1)} %collective-permute-done.6) | data formatting | bytes 2359296
  (51 shorter events, 0.3 us)
Async XLA Ops:
  7.2 51.2 %all-gather.3.cloned.1.call-start = ((), (), s32[]{:S(2)}) async-start(), calls=%async_computation.5 | async-start | bytes 1824768 | tf_op jit(solution)/shard_map/all_gather | solution.py:187
  9.0 130.4 %all-gather.5.cloned.1.call-start = ((), (), s32[]{:S(2)}) async-start(), calls=%async_computation.6 | async-start | bytes 5640192 | tf_op jit(solution)/shard_map/all_gather | solution.py:208
  12.5 1.5 copy-start.7
  14.0 14.6 %collective-permute-start.4 = (bf16[36,2176]{1,0:T(8,128)(2,1)S(1)}, bf16[36,2176]{1,0:T(8,128)(2,1)S(1)}, u32[]{:S(2)}, u32[]{:S(2)}) collective-permute-start(bf16[36,2176]{1,0:T(8,128)(2,1)S(1)} %bitcast.70), channel_id=1, source_target_pairs={{2,0},{3,1},{0,2},{1,3},{6,4},{7,5},{4,6},{5,7},{10,8},{11,9},{8,1... | collective-permute-start | bytes 470024 | tf_op jit(solution)/shard_map/ppermute | solution.py:21
  21.7 16.3 %collective-permute-start.5 = (bf16[36,2176]{1,0:T(8,128)(2,1)S(1)}, bf16[36,2176]{1,0:T(8,128)(2,1)S(1)}, u32[]{:S(2)}, u32[]{:S(2)}) collective-permute-start(bf16[36,2176]{1,0:T(8,128)(2,1)S(1)} %bitcast.71), channel_id=1, source_target_pairs={{1,0},{2,1},{3,2},{0,3},{5,4},{6,5},{7,6},{4,7},{9,8},{10,9},{11,1... | collective-permute-start | bytes 470024 | tf_op jit(solution)/shard_map/ppermute | solution.py:21
  24.0 14.0 %collective-permute-start.3 = (bf16[36,2176]{1,0:T(8,128)(2,1)S(1)}, bf16[36,2176]{1,0:T(8,128)(2,1)S(1)}, u32[]{:S(2)}, u32[]{:S(2)}) collective-permute-start(bf16[36,2176]{1,0:T(8,128)(2,1)S(1)} %bitcast.72), channel_id=1, source_target_pairs={{3,0},{0,1},{1,2},{2,3},{7,4},{4,5},{5,6},{6,7},{11,8},{8,9},{9,10... | collective-permute-start | bytes 470024 | tf_op jit(solution)/shard_map/ppermute | solution.py:21
  28.5 20.0 %copy-start.1 = (bf16[1,16,32,1152]{3,2,1,0:T(8,128)(2,1)S(1)}, bf16[1,16,32,1152]{3,2,1,0:T(8,128)(2,1)}, u32[]{:S(2)}) copy-start(bf16[1,16,32,1152]{3,2,1,0:T(8,128)(2,1)} %param.9) | copy-start | bytes 3538948
  39.1 14.6 %all-to-all-start = ((f32[4,16,704]{2,1,0:T(8,128)}), f32[4,16,704]{2,1,0:T(8,128)S(1)}, u32[]{:S(2)}, u32[]{:S(2)}) async-start(f32[4,16,704]{2,1,0:T(8,128)} %reshape.199), calls=%async_computation | async-start | bytes 393216 | tf_op jit(solution)/shard_map/all_to_all | solution.py:144
  58.3 2.0 %copy-start.3 = (bf16[704,1152]{1,0:T(8,128)(2,1)S(1)}, bf16[704,1152]{1,0:T(8,128)(2,1)}, u32[]{:S(2)}) copy-start(bf16[704,1152]{1,0:T(8,128)(2,1)} %all-gather.3.cloned.1.call-done) | copy-start | bytes 4866052
  61.4 22.9 %all-to-all-start.1 = ((bf16[4,16,1152]{2,1,0:T(8,128)(2,1)}), bf16[4,16,1152]{2,1,0:T(8,128)(2,1)S(1)}, u32[]{:S(2)}, u32[]{:S(2)}) async-start(bf16[4,16,1152]{2,1,0:T(8,128)(2,1)} %bitcast.10), calls=%async_computation.1 | async-start | bytes 294912 | tf_op jit(solution)/shard_map/all_to_all | solution.py:144
  68.3 32.0 %copy-start.8 = (f32[8,16]{1,0:T(8,128)}, f32[8,16]{1,0:T(8,128)S(1)}, u32[]{:S(2)}) copy-start(f32[8,16]{1,0:T(8,128)S(1)} %add_rsqrt_fusion) | copy-start | bytes 1540
  68.5 31.8 %copy-start.5 = (bf16[128,1152]{1,0:T(8,128)(2,1)}, bf16[128,1152]{1,0:T(8,128)(2,1)S(1)}, u32[]{:S(2)}) copy-start(bf16[128,1152]{1,0:T(8,128)(2,1)S(1)} %fusion.26) | copy-start | bytes 884740
  68.5 22.4 %collective-permute-start.2 = (bf16[128,1152]{1,0:T(8,128)(2,1)S(1)}, bf16[128,1152]{1,0:T(8,128)(2,1)S(1)}, u32[]{:S(2)}, u32[]{:S(2)}) collective-permute-start(bf16[128,1152]{1,0:T(8,128)(2,1)S(1)} %fusion.26), channel_id=1, source_target_pairs={{3,0},{0,1},{1,2},{2,3},{7,4},{4,5},{5,6},{6,7},{11,8},{8,9},{9,10... | collective-permute-start | bytes 884744 | tf_op jit(solution)/shard_map/ppermute | solution.py:21
  73.4 22.4 %collective-permute-start.1 = (bf16[128,1152]{1,0:T(8,128)(2,1)S(1)}, bf16[128,1152]{1,0:T(8,128)(2,1)S(1)}, u32[]{:S(2)}, u32[]{:S(2)}) collective-permute-start(bf16[128,1152]{1,0:T(8,128)(2,1)S(1)} %fusion.26), channel_id=1, source_target_pairs={{2,0},{3,1},{0,2},{1,3},{6,4},{7,5},{4,6},{5,7},{10,8},{11,9},{8,1... | collective-permute-start | bytes 884744 | tf_op jit(solution)/shard_map/ppermute | solution.py:21
  78.8 21.4 %collective-permute-start = (bf16[128,1152]{1,0:T(8,128)(2,1)S(1)}, bf16[128,1152]{1,0:T(8,128)(2,1)S(1)}, u32[]{:S(2)}, u32[]{:S(2)}) collective-permute-start(bf16[128,1152]{1,0:T(8,128)(2,1)S(1)} %fusion.26), channel_id=1, source_target_pairs={{1,0},{2,1},{3,2},{0,3},{5,4},{6,5},{7,6},{4,7},{9,8},{10,9},{11,1... | collective-permute-start | bytes 884744 | tf_op jit(solution)/shard_map/ppermute | solution.py:21
  84.5 20.2 %copy-start.9 = (f32[16]{0:T(128)}, f32[16]{0:T(128)S(1)}, u32[]{:S(2)}) copy-start(f32[16]{0:T(128)S(1)} %add_rsqrt_fusion.2) | copy-start | bytes 196
  91.0 9.3 %copy-start.12 = (bf16[128,1152]{1,0:T(8,128)(2,1)}, bf16[128,1152]{1,0:T(8,128)(2,1)S(1)}, u32[]{:S(2)}) copy-start(bf16[128,1152]{1,0:T(8,128)(2,1)S(1)} %collective-permute-done.2) | copy-start | bytes 884740
  95.7 4.6 %copy-start.13 = (bf16[128,1152]{1,0:T(8,128)(2,1)}, bf16[128,1152]{1,0:T(8,128)(2,1)S(1)}, u32[]{:S(2)}) copy-start(bf16[128,1152]{1,0:T(8,128)(2,1)S(1)} %collective-permute-done.1) | copy-start | bytes 884740
  100.3 0.7 copy-start.14
  101.0 14.0 %copy-start = (bf16[1,16,32,2176]{3,2,1,0:T(8,128)(2,1)S(1)}, bf16[1,16,32,2176]{3,2,1,0:T(8,128)(2,1)}, u32[]{:S(2)}) copy-start(bf16[1,16,32,2176]{3,2,1,0:T(8,128)(2,1)} %param.10) | copy-start | bytes 6684676
  107.2 17.3 %all-to-all-start.2 = ((bf16[4,32,1152]{2,1,0:T(8,128)(2,1)}), bf16[4,32,1152]{2,1,0:T(8,128)(2,1)}, u32[]{:S(2)}, u32[]{:S(2)}) async-start(bf16[4,32,1152]{2,1,0:T(8,128)(2,1)} %broadcast_in_dim.27), calls=%async_computation.2 | async-start | bytes 589824 | tf_op jit(solution)/shard_map/all_to_all | solution.py:144
  119.2 12.4 %copy-start.6 = (bf16[8,16,1152]{2,1,0:T(8,128)(2,1)S(1)}, bf16[8,16,1152]{2,1,0:T(8,128)(2,1)}, u32[]{:S(2)}) copy-start(bf16[8,16,1152]{2,1,0:T(8,128)(2,1)} %multiply_convert_fusion) | copy-start | bytes 884740
  119.2 12.4 %copy-start.10 = (s32[128]{0:T(128)S(1)}, s32[128]{0:T(128)}, u32[]{:S(2)}) copy-start(s32[128]{0:T(128)} %add.194) | copy-start | bytes 1540
  119.2 12.4 %copy-start.11 = (s32[64]{0:T(128)S(1)}, s32[64]{0:T(128)}, u32[]{:S(2)}) copy-start(s32[64]{0:T(128)} %add.188) | copy-start | bytes 772
  119.2 20.2 %copy-start.2 = (f32[1,1152]{1,0:T(1,128)S(1)}, f32[1,1152]{1,0:T(1,128)}, u32[]{:S(2)}) copy-start(f32[1,1152]{1,0:T(1,128)} %multiplier_ref.1) | copy-start | bytes 13828
  127.3 12.1 %all-to-all-start.3 = ((f32[4,16,704]{2,1,0:T(8,128)}), f32[4,16,704]{2,1,0:T(8,128)S(1)}, u32[]{:S(2)}, u32[]{:S(2)}) async-start(f32[4,16,704]{2,1,0:T(8,128)} %fusion.7), calls=%async_computation.3 | async-start | bytes 393216 | tf_op jit(solution)/shard_map/all_to_all | solution.py:144
  139.4 15.9 %copy-start.4 = (bf16[1,16,1152]{2,1,0:T(8,128)(2,1)S(1)}, bf16[1,16,1152]{2,1,0:T(8,128)(2,1)}, u32[]{:S(2)}) copy-start(bf16[1,16,1152]{2,1,0:T(8,128)(2,1)} %param.14) | copy-start | bytes 110596
  147.1 22.8 %all-to-all-start.4 = ((f32[8,16,1152]{2,1,0:T(8,128)}), f32[8,16,1152]{2,1,0:T(8,128)S(1)}, u32[]{:S(2)}, u32[]{:S(2)}) async-start(f32[8,16,1152]{2,1,0:T(8,128)} %fusion.53), calls=%async_computation.4 | async-start | bytes 1179648 | tf_op jit(solution)/shard_map/all_to_all | solution.py:287
  153.4 17.4 %collective-permute-start.6 = (bf16[1,16,32,1152]{3,2,1,0:T(8,128)(2,1)S(1)}, bf16[1,16,32,1152]{3,2,1,0:T(8,128)(2,1)}, u32[]{:S(2)}, u32[]{:S(2)}) collective-permute-start(bf16[1,16,32,1152]{3,2,1,0:T(8,128)(2,1)S(1)} %bitcast.62), channel_id=1, source_target_pairs={{32,0},{64,32},{96,64},{128,96},{160,128},{192,160},{224,192},{256... | collective-permute-start | bytes 3538952 | tf_op jit(solution)/shard_map/ppermute | solution.py:21
Sparse Core Ops, SparseCore 0:
  10.1 48.2 all-gather.2
  61.0 64.0 all-gather.4

commit v4 on v3

--- a/solution.py
+++ b/solution.py
@@ -56,6 +56,36 @@
         - jnp.mean(scaled, axis=-1, keepdims=True)
         - normal * jnp.mean(scaled * normal, axis=-1, keepdims=True)
     )
+
+
+def partial_kernel(means_ref, blocks_ref, sums_ref):
+    means = means_ref[...]
+    high = means.astype(jnp.bfloat16)
+    low = (means - high.astype(jnp.float32)).astype(jnp.bfloat16)
+    blocks = blocks_ref[...]
+    sums = jnp.dot(high, blocks, preferred_element_type=jnp.float32)
+    sums = sums + jnp.dot(low, blocks, preferred_element_type=jnp.float32)
+    sums_ref[...] = sums.astype(jnp.bfloat16)
+
+
+def back_kernel(grads_ref, blocks_ref, sums_ref, sent_ref):
+    width = sums_ref.shape[1]
+    hidden = lax.dot_general(
+        grads_ref[...], blocks_ref[...], (((1,), (1,)), ((), ())), preferred_element_type=jnp.float32
+    )
+    sent_ref[:, :width] = sums_ref[...].astype(jnp.bfloat16)
+    sent_ref[:, width:] = hidden.astype(jnp.bfloat16)
+
+
+def small_call(kernel, rows, columns, operands, flops):
+    return pl.pallas_call(
+        kernel,
+        out_shape=jax.ShapeDtypeStruct((rows, columns), jnp.bfloat16),
+        in_specs=[pl.BlockSpec(memory_space=pltpu.VMEM)] * len(operands),
+        out_specs=pl.BlockSpec(memory_space=pltpu.VMEM),
+        compiler_params=pltpu.CompilerParams(vmem_limit_bytes=VMEM_BYTES),
+        cost_estimate=pl.CostEstimate(flops=flops, bytes_accessed=2000000, transcendentals=0),
+    )(*operands)
 
 
 def slope_kernel(preact_ref, slope_ref):
@@ -85,7 +115,7 @@
     @pl.when(pl.program_id(0) == 0)
     def _():
         hidden_ref[...] = jnp.concatenate(
-            [grad_ref[y, :, start:end] for y, start, end in pieces], axis=1
+            [grad_ref[y, :, start:end].astype(jnp.float32) for y, start, end in pieces], axis=1
         ).reshape(hidden_ref.shape)
 
     step = pl.program_id(0)
@@ -208,12 +238,10 @@
     up_whole = lax.all_gather(up_y, "z", axis=0, tiled=True)
 
     row_mean = exchange_y(mean_sent).reshape(row, part)
-    row_high = row_mean.astype(jnp.bfloat16)
-    row_low = (row_mean - row_high.astype(jnp.float32)).astype(jnp.bfloat16)
-    partial = jnp.dot(row_high, blocks, preferred_element_type=jnp.float32) + jnp.dot(
-        row_low, blocks, preferred_element_type=jnp.float32
-    )
-    partials = exchange_y(partial.astype(jnp.bfloat16).reshape(Y_SHARDS, images, model_width))
+    partial = small_call(
+        partial_kernel, row, model_width, (row_mean, blocks), 4 * row * part * model_width
+    )
+    partials = exchange_y(partial.reshape(Y_SHARDS, images, model_width))
     column_text = blocks.reshape(z_size, block_rows, model_width)[:, :images]
     column_text = unit_rows(
         column_text.reshape(z_size * images, model_width).astype(jnp.float32)
@@ -224,6 +252,9 @@
     pooled = mean_tokens + jnp.sum(partials.astype(jnp.float32), axis=0)
     image_dir, image_inverse = unit_rows(pooled)
     image_unit = image_dir.astype(jnp.bfloat16)
+    column_unit = lax.all_to_all(
+        jnp.broadcast_to(image_unit[None], (z_size, images, model_width)), "z", 0, 0
+    ).reshape(z_size * images, model_width)
 
     def index_of(z_index, y_index):
         start = (z_index * Y_SHARDS + y_index) * images
@@ -250,27 +281,36 @@
     share = pooled_grad / patches
     token_grad = share.astype(jnp.bfloat16)
 
-    preacts, row_grad = lax.optimization_barrier((stored_hidden_preacts[0], token_grad))
+    column_unit, token_grad = lax.optimization_barrier((column_unit, token_grad))
+    row_grad = exchange_y(
+        jnp.broadcast_to(token_grad[None], (Y_SHARDS,) + token_grad.shape)
+    ).reshape(row, model_width)
+    preacts, column_unit = lax.optimization_barrier((stored_hidden_preacts[0], column_unit))
     slope = slopes(preacts.reshape(images * patches, hidden))
-    row_sent = jnp.concatenate([row_grad, image_unit], axis=0)
-    rows = exchange_y(jnp.broadcast_to(row_sent[None], (Y_SHARDS,) + row_sent.shape))
-    row_grad = rows[:, :images].reshape(row, model_width)
-    row_unit = rows[:, images:].reshape(row, model_width)
-    row_hidden = lax.dot_general(
-        row_grad, blocks, (((1,), (1,)), ((), ())), preferred_element_type=jnp.float32
-    )
-    received = exchange_y(row_hidden.reshape(Y_SHARDS, images, part))
-    column_weights = weigh(
-        row_unit,
+    row_text = lax.dynamic_index_in_dim(
+        text_all.reshape(Y_SHARDS, z_size, images, model_width), z, axis=1, keepdims=False
+    )
+    row_text = in_order_of_y([row_text[k] for k in range(Y_SHARDS)], y)
+    row_weights = weigh(
+        column_unit,
+        index_of(jnp.arange(z_size, dtype=jnp.int32), y).reshape(-1),
+        row_text,
         index_of(z, jnp.arange(Y_SHARDS, dtype=jnp.int32)).reshape(-1),
-        column_text,
-        index_of(jnp.arange(z_size, dtype=jnp.int32), y).reshape(-1),
-    )
-    column_sums = lax.dot_general(
-        column_weights, row_unit, (((0,), (0,)), ((), ())), preferred_element_type=jnp.float32
-    ).reshape(z_size, images, model_width)
+    )
+    row_sums = lax.dot_general(
+        row_weights, column_unit, (((0,), (0,)), ((), ())), preferred_element_type=jnp.float32
+    )
+    sent_back = small_call(
+        back_kernel, row, model_width + part, (row_grad, blocks, row_sums), 2 * row * part * model_width
+    )
+    received = exchange_y(sent_back.reshape(Y_SHARDS, images, model_width + part))
+    text_sum = jnp.sum(received[:, :, :model_width].astype(jnp.float32), axis=0)
     pieces = [
-        (own, at * block_rows + images, at * block_rows + shard_end)
+        (
+            own,
+            model_width + at * block_rows + images,
+            model_width + at * block_rows + shard_end,
+        )
         for at in range(z_size)
         for own in range(Y_SHARDS)
     ]
@@ -283,11 +323,8 @@
         share,
         layernorm_multiplier,
     ).reshape(images, patches, model_width)
-    column_sums, span_grad = lax.optimization_barrier((column_sums, span_grad))
-    text_sums = lax.all_to_all(column_sums, "z", 0, 0)
     prev_grad = from_ahead(span_grad[None], "section", 1)
 
-    text_sum = jnp.sum(text_sums, axis=0)
     text_dir, text_inverse = unit_rows(caption_tower_outputs[0].astype(jnp.float32))
     text_grad = (
         (text_sum - text_dir * jnp.sum(text_dir * text_sum, axis=-1, keepdims=True)) * text_inverse

time: 182 us -> 171 us (0.940)
  the two profiles are of different devices: /device:TPU:6 before, /device:TPU:1 now
where the time goes in v4:
time: 171 us; the launch traced here: 170 us
  starting transfers between devices  58.8 us (34%)
  waiting for transfers between devices  54.7 us (32%)
  between operations  16.3 us (10%)
  Pallas kernels  14.5 us (8%)
  other arithmetic  14 us (8%)
  local copies, waits for them, and re-layouts  7.88 us (5%)
  matrix products  4.01 us (2%)
    ppermute x7, waiting for transfers between devices, from_ahead(): lax.ppermute(array, axis, [((i + by) % peers, i) for i in range(peers)])  35.8 us
    ppermute x7, starting transfers between devices, from_ahead(): lax.ppermute(array, axis, [((i + by) % peers, i) for i in range(peers)])  32.5 us
    all_to_all x4, starting transfers between devices, exchange_y(): return lax.all_to_all(blocks, 'y', 0, 0)  18.8 us
    all_to_all x4, waiting for transfers between devices, exchange_y(): return lax.all_to_all(blocks, 'y', 0, 0)  8.21 us
    pallas_call x1, Pallas kernels, span(): pl.pallas_call(functools.partial(span_kernel, pieces), grid=(count // row...  7.64 us
    all_to_all x1, starting transfers between devices, per_device(): lax.all_to_all(jnp.broadcast_to(image_unit[None], (z_size, images, model_...  7.39 us
    all_gather x1, waiting for transfers between devices, per_device(): up_whole = lax.all_gather(up_y, 'z', axis=0, tiled=True)  4.89 us
    pallas_call x1, Pallas kernels, slopes(): pl.pallas_call(slope_kernel, grid=(tokens // block,), in_specs=[spec], ou...  4.19 us
  transfers between devices with their start and end apart: 14, of which 11 were waited for; matrix products, arithmetic and copies ran while one was open for 12% of the time, Pallas kernels for 4%

profile of v4, /device:TPU:1, one launch (start us, length us, event | category | flops | bytes accessed | tf_op | source)
XLA Modules:
  0.0 170.1 jit_solution(11598088878422527777)
XLA Ops:
  7.2 0.0 all-gather.3.cloned.1.call-start
  7.2 0.1 pad.19.clone
  7.3 1.7 maximum_maximum_fusion
  9.0 0.0 all-gather.5.cloned.1.call-start
  9.1 3.5 %convert_reduce_fusion = f32[16,2176]{1,0:T(8,128)S(1)} fusion(bf16[1,16,32,2176]{3,2,1,0:T(8,128)(2,1)} %param.10), kind=kLoop, calls=%fused_computation.10 | loop fusion | flops 13334528 | bytes 2367488 | tf_op jit(solution)/shard_map/reduce_sum | solution.py:222
  12.6 0.4 div.23
  13.0 0.2 pad_bitcast_fusion
  13.2 0.8 reshape.244
  14.0 5.0 %collective-permute-start.3 = (bf16[36,2176]{1,0:T(8,128)(2,1)S(1)}, bf16[36,2176]{1,0:T(8,128)(2,1)S(1)}, u32[]{:S(2)}, u32[]{:S(2)}) collective-permute-start(bf16[36,2176]{1,0:T(8,128)(2,1)S(1)} %bitcast.63), channel_id=1, source_target_pairs={{3,0},{0,1},{1,2},{2,3},{7,4},{4,5},{5,6},{6,7},{11,8},{8,9},{9,10... | collective-permute-start | bytes 470024 | tf_op jit(solution)/shard_map/ppermute | solution.py:21
  19.1 5.7 %collective-permute-start.4 = (bf16[36,2176]{1,0:T(8,128)(2,1)S(1)}, bf16[36,2176]{1,0:T(8,128)(2,1)S(1)}, u32[]{:S(2)}, u32[]{:S(2)}) collective-permute-start(bf16[36,2176]{1,0:T(8,128)(2,1)S(1)} %bitcast.64), channel_id=1, source_target_pairs={{2,0},{3,1},{0,2},{1,3},{6,4},{7,5},{4,6},{5,7},{10,8},{11,9},{8,1... | collective-permute-start | bytes 470024 | tf_op jit(solution)/shard_map/ppermute | solution.py:21
  24.7 5.0 %collective-permute-start.5 = (bf16[36,2176]{1,0:T(8,128)(2,1)S(1)}, bf16[36,2176]{1,0:T(8,128)(2,1)S(1)}, u32[]{:S(2)}, u32[]{:S(2)}) collective-permute-start(bf16[36,2176]{1,0:T(8,128)(2,1)S(1)} %bitcast.65), channel_id=1, source_target_pairs={{1,0},{2,1},{3,2},{0,3},{5,4},{6,5},{7,6},{4,7},{9,8},{10,9},{11,1... | collective-permute-start | bytes 470024 | tf_op jit(solution)/shard_map/ppermute | solution.py:21
  29.7 4.4 %collective-permute-done.4 = bf16[36,2176]{1,0:T(8,128)(2,1)S(1)} collective-permute-done((bf16[36,2176]{1,0:T(8,128)(2,1)S(1)}, bf16[36,2176]{1,0:T(8,128)(2,1)S(1)}, u32[]{:S(2)}, u32[]{:S(2)}) %collective-permute-start.4) | collective-permute-done | bytes 156704 | tf_op jit(solution)/shard_map/ppermute | solution.py:21
  34.2 7.3 %collective-permute-done.5 = bf16[36,2176]{1,0:T(8,128)(2,1)S(1)} collective-permute-done((bf16[36,2176]{1,0:T(8,128)(2,1)S(1)}, bf16[36,2176]{1,0:T(8,128)(2,1)S(1)}, u32[]{:S(2)}, u32[]{:S(2)}) %collective-permute-start.5) | collective-permute-done | bytes 156704 | tf_op jit(solution)/shard_map/ppermute | solution.py:21
  41.4 0.1 select_select_fusion.3
  41.5 1.0 pad_maximum_fusion.1
  42.5 0.0 all-gather.5.cloned.1.call-update
  42.5 5.9 %all-to-all-start = ((f32[4,16,704]{2,1,0:T(8,128)}), f32[4,16,704]{2,1,0:T(8,128)S(1)}, u32[]{:S(2)}, u32[]{:S(2)}) async-start(f32[4,16,704]{2,1,0:T(8,128)} %reshape.244), calls=%async_computation | async-start | bytes 393216 | tf_op jit(solution)/shard_map/all_to_all | solution.py:174
  48.4 0.1 add_multiply_fusion
  48.5 0.1 iota_add_fusion
  48.6 0.1 add.200
  50.6 0.1 iota_add_fusion.1
  50.7 0.1 add.211
  50.8 0.1 iota_add_fusion.2
  50.9 0.6 add.217
  51.5 0.9 convert_reduce_fusion.1
  52.4 2.9 %all-gather.3.cloned.1.call-done.blocks_ref = bf16[704,1152]{1,0:T(8,128)(2,1)} async-done(((bf16[88,1152]{1,0:T(8,128)(2,1)}), bf16[704,1152]{1,0:T(8,128)(2,1)}) %all-gather.3.cloned.1.call-update) | async-done | bytes 1622032 | tf_op jit(solution)/shard_map/all_gather | solution.py:217
  55.3 1.1 multiply_reduce_fusion
  56.4 0.1 rsqrt.29
  56.5 0.3 all-to-all-done
  56.8 1.4 copy-done
  58.3 1.3 shard_map.104
  59.6 6.2 %all-to-all-start.1 = ((bf16[4,16,1152]{2,1,0:T(8,128)(2,1)}), bf16[4,16,1152]{2,1,0:T(8,128)(2,1)S(1)}, u32[]{:S(2)}, u32[]{:S(2)}) async-start(bf16[4,16,1152]{2,1,0:T(8,128)(2,1)} %bitcast.6), calls=%async_computation.1 | async-start | bytes 294912 | tf_op jit(solution)/shard_map/all_to_all | solution.py:174
  65.8 0.1 fusion.24
  65.9 5.5 %collective-permute-start = (bf16[128,1152]{1,0:T(8,128)(2,1)S(1)}, bf16[128,1152]{1,0:T(8,128)(2,1)S(1)}, u32[]{:S(2)}, u32[]{:S(2)}) collective-permute-start(bf16[128,1152]{1,0:T(8,128)(2,1)S(1)} %fusion.24), channel_id=1, source_target_pairs={{1,0},{2,1},{3,2},{0,3},{5,4},{6,5},{7,6},{4,7},{9,8},{10,9},{11,1... | collective-permute-start | bytes 884744 | tf_op jit(solution)/shard_map/ppermute | solution.py:21
  71.4 4.0 %collective-permute-start.1 = (bf16[128,1152]{1,0:T(8,128)(2,1)S(1)}, bf16[128,1152]{1,0:T(8,128)(2,1)}, u32[]{:S(2)}, u32[]{:S(2)}) collective-permute-start(bf16[128,1152]{1,0:T(8,128)(2,1)S(1)} %fusion.24), channel_id=1, source_target_pairs={{2,0},{3,1},{0,2},{1,3},{6,4},{7,5},{4,6},{5,7},{10,8},{11,9},{8,1... | collective-permute-start | bytes 884744 | tf_op jit(solution)/shard_map/ppermute | solution.py:21
  75.4 4.0 %collective-permute-start.2 = (bf16[128,1152]{1,0:T(8,128)(2,1)S(1)}, bf16[128,1152]{1,0:T(8,128)(2,1)}, u32[]{:S(2)}, u32[]{:S(2)}) collective-permute-start(bf16[128,1152]{1,0:T(8,128)(2,1)S(1)} %fusion.24), channel_id=1, source_target_pairs={{3,0},{0,1},{1,2},{2,3},{7,4},{4,5},{5,6},{6,7},{11,8},{8,9},{9,10... | collective-permute-start | bytes 884744 | tf_op jit(solution)/shard_map/ppermute | solution.py:21
  79.4 1.0 multiply_reduce_fusion.2
  80.5 0.1 multiply_convert_fusion
  80.5 0.7 broadcast_in_dim.21
  81.3 7.4 %all-to-all-start.2 = ((bf16[8,16,1152]{2,1,0:T(8,128)(2,1)}), bf16[8,16,1152]{2,1,0:T(8,128)(2,1)}, u32[]{:S(2)}, u32[]{:S(2)}) async-start(bf16[8,16,1152]{2,1,0:T(8,128)(2,1)} %broadcast_in_dim.21), calls=%async_computation.2 | async-start | bytes 589824 | tf_op jit(solution)/shard_map/all_to_all | solution.py:255
  88.7 0.6 collective-permute-done
  89.3 5.7 %collective-permute-done.2 = bf16[128,1152]{1,0:T(8,128)(2,1)} collective-permute-done((bf16[128,1152]{1,0:T(8,128)(2,1)S(1)}, bf16[128,1152]{1,0:T(8,128)(2,1)}, u32[]{:S(2)}, u32[]{:S(2)}) %collective-permute-start.2) | collective-permute-done | bytes 294944 | tf_op jit(solution)/shard_map/ppermute | solution.py:21
  95.0 2.2 %pad_maximum_fusion = bf16[512,1152]{1,0:T(8,128)(2,1)} fusion(bf16[128,1152]{1,0:T(8,128)(2,1)} %collective-permute-done.2, bf16[128,1152]{1,0:T(8,128)(2,1)} %collective-permute-done.1, bf16[128,1152]{1,0:T(8,128)(2,1)S(1)} %collective-permute-done, bf16[128,1152]{1,0:T(8,128)(2,1)S(1)} %fusion.24), kind=kLoop, calls=%fused_computation.12 | loop fusion | flops 4718592 | bytes 2359296 | tf_op jit(solution)/shard_map/concatenate | solution.py:249
  97.2 2.5 %multiply_reduce_fusion.1 = (f32[16]{0:T(128)S(1)}, f32[16,1152]{1,0:T(8,128)S(1)}) fusion(f32[16,1152]{1,0:T(8,128)S(1)} %get-tuple-element.15, f32[16]{0:T(128)S(1)} %add_rsqrt_fusion.2, bf16[512,1152]{1,0:T(8,128)(2,1)} %pad_maximum_fusion, f32[]{:T(128)} %bitcast.51, f32[]{:T(128)} %bitcast.49, s32[512]{0:T(512)S(1)} %add.200, f32[]{:T(128)S(6)} %mul.194, ...), kind=kOutput, calls=%fused_computation.62 | convolution fusion | flops 37939184 | bytes 1329356 | tf_op jit(solution)/shard_map/dot_general | solution.py:277
  99.6 0.9 select_bitcast_fusion.3
  100.5 0.1 fusion.73
  100.6 2.8 %all-to-all-done.2 = bf16[8,16,1152]{2,1,0:T(8,128)(2,1)} async-done(((bf16[8,16,1152]{2,1,0:T(8,128)(2,1)}), bf16[8,16,1152]{2,1,0:T(8,128)(2,1)}, u32[]{:S(2)}, u32[]{:S(2)}) %all-to-all-start.2) | async-done | bytes 294944 | tf_op jit(solution)/shard_map/all_to_all | solution.py:255
  103.4 0.7 broadcast_in_dim.24
  104.1 3.3 %all-to-all-start.3 = ((bf16[4,16,1152]{2,1,0:T(8,128)(2,1)}), bf16[4,16,1152]{2,1,0:T(8,128)(2,1)S(1)}, u32[]{:S(2)}, u32[]{:S(2)}) async-start(bf16[4,16,1152]{2,1,0:T(8,128)(2,1)} %broadcast_in_dim.24), calls=%async_computation.3 | async-start | bytes 294912 | tf_op jit(solution)/shard_map/all_to_all | solution.py:174
  107.4 1.5 fusion.22.sums_ref
  109.0 5.7 %all-to-all-done.3 = bf16[4,16,1152]{2,1,0:T(8,128)(2,1)S(1)} async-done(((bf16[4,16,1152]{2,1,0:T(8,128)(2,1)}), bf16[4,16,1152]{2,1,0:T(8,128)(2,1)S(1)}, u32[]{:S(2)}, u32[]{:S(2)}) %all-to-all-start.3) | async-done | bytes 147488 | tf_op jit(solution)/shard_map/all_to_all | solution.py:174
  114.7 1.3 shard_map.105
  116.0 3.4 %all-to-all-start.4 = ((bf16[4,16,1856]{2,1,0:T(8,128)(2,1)}), bf16[4,16,1856]{2,1,0:T(8,128)(2,1)S(1)}, u32[]{:S(2)}, u32[]{:S(2)}) async-start(bf16[4,16,1856]{2,1,0:T(8,128)(2,1)} %bitcast.19), calls=%async_computation.4 | async-start | bytes 491520 | tf_op jit(solution)/shard_map/all_to_all | solution.py:174
  119.4 1.6 copy-done.2
  121.1 4.2 %shard_map.106.slope_ref = f32[512,2176]{1,0:T(8,128)} custom-call(bf16[512,2176]{1,0:T(8,128)(2,1)S(1)} %bitcast.56), custom_call_target="tpu_custom_call" | custom-call | flops 22282240 | bytes 6684672 | tf_op jit(solution)/shard_map/pallas_call | solution.py:99
  125.3 2.2 %all-to-all-done.4.grad_ref = bf16[4,16,1856]{2,1,0:T(8,128)(2,1)S(1)} async-done(((bf16[4,16,1856]{2,1,0:T(8,128)(2,1)}), bf16[4,16,1856]{2,1,0:T(8,128)(2,1)S(1)}, u32[]{:S(2)}, u32[]{:S(2)}) %all-to-all-start.4) | async-done | bytes 237600 | tf_op jit(solution)/shard_map/all_to_all | solution.py:174
  127.4 4.9 %all-gather.5.cloned.1.call-done.up_ref = bf16[1152,2176]{1,0:T(8,128)(2,1)} async-done(((bf16[144,2176]{1,0:T(8,128)(2,1)}), bf16[1152,2176]{1,0:T(8,128)(2,1)}) %all-gather.5.cloned.1.call-update) | async-done | bytes 5013520 | tf_op jit(solution)/shard_map/all_gather | solution.py:238
  132.3 7.6 %shard_map.107 = bf16[512,1152]{1,0:T(8,128)(2,1)S(1)} custom-call(bf16[4,16,1856]{2,1,0:T(8,128)(2,1)S(1)} %all-to-all-done.4.grad_ref, f32[512,2176]{1,0:T(8,128)} %shard_map.106.slope_ref, bf16[1152,2176]{1,0:T(8,128)(2,1)} %all-gather.5.cloned.1.call-done.up_ref, bf16[512,1152]{1,0:T(8,128)(2,1)S(1)} %bitcast.57, ...), custom_call_target="tpu_custom_call" | custom-call | flops 2566914048 | bytes 11829248 | tf_op jit(solution)/shard_map/pallas_call | solution.py:150
  140.0 3.4 %collective-permute-start.6 = (bf16[1,16,32,1152]{3,2,1,0:T(8,128)(2,1)S(1)}, bf16[1,16,32,1152]{3,2,1,0:T(8,128)(2,1)S(1)}, u32[]{:S(2)}, u32[]{:S(2)}) collective-permute-start(bf16[1,16,32,1152]{3,2,1,0:T(8,128)(2,1)S(1)} %bitcast.58), channel_id=1, source_target_pairs={{32,0},{64,32},{96,64},{128,96},{160,128},{192,160},{224,192},{256... | collective-permute-start | bytes 3538952 | tf_op jit(solution)/shard_map/ppermute | solution.py:21
  143.4 0.1 fusion.39
  143.6 0.2 fusion.41
  143.8 0.7 fusion.43
  144.5 17.8 %collective-permute-done.6 = bf16[1,16,32,1152]{3,2,1,0:T(8,128)(2,1)S(1)} collective-permute-done((bf16[1,16,32,1152]{3,2,1,0:T(8,128)(2,1)S(1)}, bf16[1,16,32,1152]{3,2,1,0:T(8,128)(2,1)S(1)}, u32[]{:S(2)}, u32[]{:S(2)}) %collective-permute-start.6) | collective-permute-done | bytes 1179680 | tf_op jit(solution)/shard_map/ppermute | solution.py:21
  162.3 1.0 copy.16
  (33 shorter events, 0.2 us)
Async XLA Ops:
  7.2 48.2 %all-gather.3.cloned.1.call-start = ((), (), s32[]{:S(2)}) async-start(), calls=%async_computation.5 | async-start | bytes 1824768 | tf_op jit(solution)/shard_map/all_gather | solution.py:217
  9.0 5.0 %copy-start.6 = (bf16[1,36,2176]{2,1,0:T(8,128)(2,1)S(1)}, bf16[1,36,2176]{2,1,0:T(8,128)(2,1)}, u32[]{:S(2)}) copy-start(bf16[1,36,2176]{2,1,0:T(8,128)(2,1)} %param.12) | copy-start | bytes 470020
  9.0 123.3 %all-gather.5.cloned.1.call-start = ((), (), s32[]{:S(2)}) async-start(), calls=%async_computation.6 | async-start | bytes 5640192 | tf_op jit(solution)/shard_map/all_gather | solution.py:238
  13.2 38.3 %copy-start.3 = (bf16[1,16,32,1152]{3,2,1,0:T(8,128)(2,1)S(1)}, bf16[1,16,32,1152]{3,2,1,0:T(8,128)(2,1)}, u32[]{:S(2)}) copy-start(bf16[1,16,32,1152]{3,2,1,0:T(8,128)(2,1)} %param.9) | copy-start | bytes 3538948
  14.0 15.7 %collective-permute-start.3 = (bf16[36,2176]{1,0:T(8,128)(2,1)S(1)}, bf16[36,2176]{1,0:T(8,128)(2,1)S(1)}, u32[]{:S(2)}, u32[]{:S(2)}) collective-permute-start(bf16[36,2176]{1,0:T(8,128)(2,1)S(1)} %bitcast.63), channel_id=1, source_target_pairs={{3,0},{0,1},{1,2},{2,3},{7,4},{4,5},{5,6},{6,7},{11,8},{8,9},{9,10... | collective-permute-start | bytes 470024 | tf_op jit(solution)/shard_map/ppermute | solution.py:21
  19.1 15.1 %collective-permute-start.4 = (bf16[36,2176]{1,0:T(8,128)(2,1)S(1)}, bf16[36,2176]{1,0:T(8,128)(2,1)S(1)}, u32[]{:S(2)}, u32[]{:S(2)}) collective-permute-start(bf16[36,2176]{1,0:T(8,128)(2,1)S(1)} %bitcast.64), channel_id=1, source_target_pairs={{2,0},{3,1},{0,2},{1,3},{6,4},{7,5},{4,6},{5,7},{10,8},{11,9},{8,1... | collective-permute-start | bytes 470024 | tf_op jit(solution)/shard_map/ppermute | solution.py:21
  24.7 16.7 %collective-permute-start.5 = (bf16[36,2176]{1,0:T(8,128)(2,1)S(1)}, bf16[36,2176]{1,0:T(8,128)(2,1)S(1)}, u32[]{:S(2)}, u32[]{:S(2)}) collective-permute-start(bf16[36,2176]{1,0:T(8,128)(2,1)S(1)} %bitcast.65), channel_id=1, source_target_pairs={{1,0},{2,1},{3,2},{0,3},{5,4},{6,5},{7,6},{4,7},{9,8},{10,9},{11,1... | collective-permute-start | bytes 470024 | tf_op jit(solution)/shard_map/ppermute | solution.py:21
  42.5 14.3 %all-to-all-start = ((f32[4,16,704]{2,1,0:T(8,128)}), f32[4,16,704]{2,1,0:T(8,128)S(1)}, u32[]{:S(2)}, u32[]{:S(2)}) async-start(f32[4,16,704]{2,1,0:T(8,128)} %reshape.244), calls=%async_computation | async-start | bytes 393216 | tf_op jit(solution)/shard_map/all_to_all | solution.py:174
  56.8 1.4 copy-start
  58.3 7.5 %copy-start.1 = (bf16[704,1152]{1,0:T(8,128)(2,1)S(1)}, bf16[704,1152]{1,0:T(8,128)(2,1)}, u32[]{:S(2)}) copy-start(bf16[704,1152]{1,0:T(8,128)(2,1)} %all-gather.3.cloned.1.call-done.blocks_ref) | copy-start | bytes 4866052
  59.6 19.8 %all-to-all-start.1 = ((bf16[4,16,1152]{2,1,0:T(8,128)(2,1)}), bf16[4,16,1152]{2,1,0:T(8,128)(2,1)S(1)}, u32[]{:S(2)}, u32[]{:S(2)}) async-start(bf16[4,16,1152]{2,1,0:T(8,128)(2,1)} %bitcast.6), calls=%async_computation.1 | async-start | bytes 294912 | tf_op jit(solution)/shard_map/all_to_all | solution.py:174
  65.9 23.4 %collective-permute-start = (bf16[128,1152]{1,0:T(8,128)(2,1)S(1)}, bf16[128,1152]{1,0:T(8,128)(2,1)S(1)}, u32[]{:S(2)}, u32[]{:S(2)}) collective-permute-start(bf16[128,1152]{1,0:T(8,128)(2,1)S(1)} %fusion.24), channel_id=1, source_target_pairs={{1,0},{2,1},{3,2},{0,3},{5,4},{6,5},{7,6},{4,7},{9,8},{10,9},{11,1... | collective-permute-start | bytes 884744 | tf_op jit(solution)/shard_map/ppermute | solution.py:21
  71.4 17.9 %collective-permute-start.1 = (bf16[128,1152]{1,0:T(8,128)(2,1)S(1)}, bf16[128,1152]{1,0:T(8,128)(2,1)}, u32[]{:S(2)}, u32[]{:S(2)}) collective-permute-start(bf16[128,1152]{1,0:T(8,128)(2,1)S(1)} %fusion.24), channel_id=1, source_target_pairs={{2,0},{3,1},{0,2},{1,3},{6,4},{7,5},{4,6},{5,7},{10,8},{11,9},{8,1... | collective-permute-start | bytes 884744 | tf_op jit(solution)/shard_map/ppermute | solution.py:21
  75.4 19.6 %collective-permute-start.2 = (bf16[128,1152]{1,0:T(8,128)(2,1)S(1)}, bf16[128,1152]{1,0:T(8,128)(2,1)}, u32[]{:S(2)}, u32[]{:S(2)}) collective-permute-start(bf16[128,1152]{1,0:T(8,128)(2,1)S(1)} %fusion.24), channel_id=1, source_target_pairs={{3,0},{0,1},{1,2},{2,3},{7,4},{4,5},{5,6},{6,7},{11,8},{8,9},{9,10... | collective-permute-start | bytes 884744 | tf_op jit(solution)/shard_map/ppermute | solution.py:21
  81.3 22.1 %all-to-all-start.2 = ((bf16[8,16,1152]{2,1,0:T(8,128)(2,1)}), bf16[8,16,1152]{2,1,0:T(8,128)(2,1)}, u32[]{:S(2)}, u32[]{:S(2)}) async-start(bf16[8,16,1152]{2,1,0:T(8,128)(2,1)} %broadcast_in_dim.21), calls=%async_computation.2 | async-start | bytes 589824 | tf_op jit(solution)/shard_map/all_to_all | solution.py:255
  97.2 10.3 %copy-start.7 = (s32[64]{0:T(128)S(1)}, s32[64]{0:T(128)}, u32[]{:S(2)}) copy-start(s32[64]{0:T(128)} %add.217) | copy-start | bytes 772
  104.1 10.6 %all-to-all-start.3 = ((bf16[4,16,1152]{2,1,0:T(8,128)(2,1)}), bf16[4,16,1152]{2,1,0:T(8,128)(2,1)S(1)}, u32[]{:S(2)}, u32[]{:S(2)}) async-start(bf16[4,16,1152]{2,1,0:T(8,128)(2,1)} %broadcast_in_dim.24), calls=%async_computation.3 | async-start | bytes 294912 | tf_op jit(solution)/shard_map/all_to_all | solution.py:174
  116.0 11.4 %all-to-all-start.4 = ((bf16[4,16,1856]{2,1,0:T(8,128)(2,1)}), bf16[4,16,1856]{2,1,0:T(8,128)(2,1)S(1)}, u32[]{:S(2)}, u32[]{:S(2)}) async-start(bf16[4,16,1856]{2,1,0:T(8,128)(2,1)} %bitcast.19), calls=%async_computation.4 | async-start | bytes 491520 | tf_op jit(solution)/shard_map/all_to_all | solution.py:174
  119.4 1.6 copy-start.2
  121.1 11.2 %copy-start.4 = (f32[1,1152]{1,0:T(1,128)S(1)}, f32[1,1152]{1,0:T(1,128)}, u32[]{:S(2)}) copy-start(f32[1,1152]{1,0:T(1,128)} %multiplier_ref.1) | copy-start | bytes 13828
  132.3 11.1 %copy-start.5 = (bf16[1,16,1152]{2,1,0:T(8,128)(2,1)S(1)}, bf16[1,16,1152]{2,1,0:T(8,128)(2,1)}, u32[]{:S(2)}) copy-start(bf16[1,16,1152]{2,1,0:T(8,128)(2,1)} %param.14) | copy-start | bytes 110596
  140.0 22.3 %collective-permute-start.6 = (bf16[1,16,32,1152]{3,2,1,0:T(8,128)(2,1)S(1)}, bf16[1,16,32,1152]{3,2,1,0:T(8,128)(2,1)S(1)}, u32[]{:S(2)}, u32[]{:S(2)}) collective-permute-start(bf16[1,16,32,1152]{3,2,1,0:T(8,128)(2,1)S(1)} %bitcast.58), channel_id=1, source_target_pairs={{32,0},{64,32},{96,64},{128,96},{160,128},{192,160},{224,192},{256... | collective-permute-start | bytes 3538952 | tf_op jit(solution)/shard_map/ppermute | solution.py:21
Sparse Core Ops, SparseCore 0:
  10.7 44.6 all-gather.2
  57.4 74.8 all-gather.4

commit v5 on v4

--- a/solution.py
+++ b/solution.py
@@ -58,23 +58,21 @@
     )
 
 
-def partial_kernel(means_ref, blocks_ref, sums_ref):
+def partial_kernel(means_ref, blocks_ref, own_ref, sums_ref):
     means = means_ref[...]
     high = means.astype(jnp.bfloat16)
     low = (means - high.astype(jnp.float32)).astype(jnp.bfloat16)
     blocks = blocks_ref[...]
     sums = jnp.dot(high, blocks, preferred_element_type=jnp.float32)
     sums = sums + jnp.dot(low, blocks, preferred_element_type=jnp.float32)
-    sums_ref[...] = sums.astype(jnp.bfloat16)
-
-
-def back_kernel(grads_ref, blocks_ref, sums_ref, sent_ref):
-    width = sums_ref.shape[1]
+    sums_ref[...] = (sums + own_ref[...]).astype(jnp.bfloat16)
+
+
+def back_kernel(grads_ref, blocks_ref, sent_ref):
     hidden = lax.dot_general(
         grads_ref[...], blocks_ref[...], (((1,), (1,)), ((), ())), preferred_element_type=jnp.float32
     )
-    sent_ref[:, :width] = sums_ref[...].astype(jnp.bfloat16)
-    sent_ref[:, width:] = hidden.astype(jnp.bfloat16)
+    sent_ref[...] = hidden.astype(jnp.bfloat16)
 
 
 def small_call(kernel, rows, columns, operands, flops):
@@ -238,10 +236,17 @@
     up_whole = lax.all_gather(up_y, "z", axis=0, tiled=True)
 
     row_mean = exchange_y(mean_sent).reshape(row, part)
+    own_means = jnp.where(
+        jnp.arange(Y_SHARDS, dtype=jnp.int32)[:, None, None] == y, mean_tokens[None], 0.0
+    ).reshape(row, model_width)
     partial = small_call(
-        partial_kernel, row, model_width, (row_mean, blocks), 4 * row * part * model_width
-    )
-    partials = exchange_y(partial.reshape(Y_SHARDS, images, model_width))
+        partial_kernel,
+        row,
+        model_width,
+        (row_mean, blocks, own_means),
+        4 * row * part * model_width,
+    )
+    partials = exchange_y(jnp.broadcast_to(partial[None], (Y_SHARDS, row, model_width)))
     column_text = blocks.reshape(z_size, block_rows, model_width)[:, :images]
     column_text = unit_rows(
         column_text.reshape(z_size * images, model_width).astype(jnp.float32)
@@ -249,12 +254,9 @@
     text_all = jnp.concatenate(
         [column_text] + [from_ahead(column_text, "y", k) for k in range(1, Y_SHARDS)], axis=0
     )
-    pooled = mean_tokens + jnp.sum(partials.astype(jnp.float32), axis=0)
+    pooled = jnp.sum(partials.astype(jnp.float32), axis=0)
     image_dir, image_inverse = unit_rows(pooled)
     image_unit = image_dir.astype(jnp.bfloat16)
-    column_unit = lax.all_to_all(
-        jnp.broadcast_to(image_unit[None], (z_size, images, model_width)), "z", 0, 0
-    ).reshape(z_size * images, model_width)
 
     def index_of(z_index, y_index):
         start = (z_index * Y_SHARDS + y_index) * images
@@ -267,7 +269,7 @@
 
     weights = weigh(
         image_unit,
-        index_of(z, y).reshape(-1),
+        index_of(z, jnp.arange(Y_SHARDS, dtype=jnp.int32)).reshape(-1),
         text_all,
         index_of(
             lax.broadcasted_iota(jnp.int32, (Y_SHARDS, z_size), 1),
@@ -278,38 +280,33 @@
     pooled_grad = (
         image_sum - image_dir * jnp.sum(image_dir * image_sum, axis=-1, keepdims=True)
     ) * image_inverse
-    share = pooled_grad / patches
-    token_grad = share.astype(jnp.bfloat16)
-
-    column_unit, token_grad = lax.optimization_barrier((column_unit, token_grad))
-    row_grad = exchange_y(
-        jnp.broadcast_to(token_grad[None], (Y_SHARDS,) + token_grad.shape)
-    ).reshape(row, model_width)
-    preacts, column_unit = lax.optimization_barrier((stored_hidden_preacts[0], column_unit))
+    row_share = pooled_grad / patches
+    row_grad = row_share.astype(jnp.bfloat16)
+    share = lax.dynamic_slice_in_dim(row_share, y * images, images, axis=0)
+    preacts, row_grad = lax.optimization_barrier((stored_hidden_preacts[0], row_grad))
     slope = slopes(preacts.reshape(images * patches, hidden))
-    row_text = lax.dynamic_index_in_dim(
-        text_all.reshape(Y_SHARDS, z_size, images, model_width), z, axis=1, keepdims=False
-    )
-    row_text = in_order_of_y([row_text[k] for k in range(Y_SHARDS)], y)
-    row_weights = weigh(
-        column_unit,
-        index_of(jnp.arange(z_size, dtype=jnp.int32), y).reshape(-1),
-        row_text,
-        index_of(z, jnp.arange(Y_SHARDS, dtype=jnp.int32)).reshape(-1),
-    )
-    row_sums = lax.dot_general(
-        row_weights, column_unit, (((0,), (0,)), ((), ())), preferred_element_type=jnp.float32
-    )
     sent_back = small_call(
-        back_kernel, row, model_width + part, (row_grad, blocks, row_sums), 2 * row * part * model_width
-    )
-    received = exchange_y(sent_back.reshape(Y_SHARDS, images, model_width + part))
-    text_sum = jnp.sum(received[:, :, :model_width].astype(jnp.float32), axis=0)
+        back_kernel, row, part, (row_grad, blocks), 2 * row * part * model_width
+    )
+    received = exchange_y(sent_back.reshape(Y_SHARDS, images, part))
+    column_sums = lax.dot_general(
+        weights[:, : z_size * images],
+        image_unit,
+        (((0,), (0,)), ((), ())),
+        preferred_element_type=jnp.float32,
+    )
+    column_sums, received = lax.optimization_barrier(
+        (column_sums.astype(jnp.bfloat16), received)
+    )
+    text_sums = lax.all_to_all(
+        column_sums.reshape(z_size, images, model_width), "z", 0, 0
+    )
+    text_sum = jnp.sum(text_sums.astype(jnp.float32), axis=0)
     pieces = [
         (
             own,
-            model_width + at * block_rows + images,
-            model_width + at * block_rows + shard_end,
+            at * block_rows + images,
+            at * block_rows + shard_end,
         )
         for at in range(z_size)
         for own in range(Y_SHARDS)

time: 171 us -> 165 us (0.965)
  the two profiles are of different devices: /device:TPU:1 before, /device:TPU:6 now
where the time goes in v5:
time: 165 us; the launch traced here: 162 us
  starting transfers between devices  59.3 us (36%)
  waiting for transfers between devices  51.2 us (31%)
  between operations  16.3 us (10%)
  Pallas kernels  13.8 us (8%)
  other arithmetic  10.6 us (6%)
  local copies, waits for them, and re-layouts  6.87 us (4%)
  matrix products  4.27 us (3%)
    ppermute x7, waiting for transfers between devices, from_ahead(): lax.ppermute(array, axis, [((i + by) % peers, i) for i in range(peers)])  36.7 us
    ppermute x7, starting transfers between devices, from_ahead(): lax.ppermute(array, axis, [((i + by) % peers, i) for i in range(peers)])  32.2 us
    all_to_all x3, starting transfers between devices, exchange_y(): return lax.all_to_all(blocks, 'y', 0, 0)  20.6 us
    all_gather x1, waiting for transfers between devices, per_device(): blocks = lax.all_gather(block, 'z', axis=0, tiled=True)  7.89 us
    pallas_call x1, Pallas kernels, span(): pl.pallas_call(functools.partial(span_kernel, pieces), grid=(count // row...  7.65 us
    all_to_all x1, starting transfers between devices, per_device(): lax.all_to_all(column_sums.reshape(z_size, images, model_width), 'z', 0, 0)  6.42 us
    all_to_all x3, waiting for transfers between devices, exchange_y(): return lax.all_to_all(blocks, 'y', 0, 0)  5.55 us
    pallas_call x1, Pallas kernels, slopes(): pl.pallas_call(slope_kernel, grid=(tokens // block,), in_specs=[spec], ou...  4.19 us
  transfers between devices with their start and end apart: 13, of which 10 were waited for; matrix products, arithmetic and copies ran while one was open for 10% of the time, Pallas kernels for 8%

profile of v5, /device:TPU:6, one launch (start us, length us, event | category | flops | bytes accessed | tf_op | source)
XLA Modules:
  0.0 162.3 jit_solution(8275912120329473257)
XLA Ops:
  7.2 0.0 all-gather.3.cloned.1.call-start
  7.2 0.1 pad.15.clone
  7.3 1.7 %maximum_maximum_fusion = bf16[88,1152]{1,0:T(8,128)(2,1)} fusion(bf16[68,1152]{1,0:T(8,128)(2,1)} %bitcast.51, bf16[16,1152]{1,0:T(8,128)(2,1)} %bitcast.46, bf16[88]{0:T(256)(128)(2,1)S(1)} %pad.15.clone), kind=kLoop, calls=%fused_computation.36 | loop fusion | flops 608256 | bytes 396464 | tf_op jit(solution)/shard_map/concatenate | solution.py:207
  9.0 0.0 all-gather.3.cloned.1.call-update
  9.0 0.0 all-gather.5.cloned.1.call-start
  9.1 3.5 %convert_reduce_fusion = f32[16,2176]{1,0:T(8,128)S(1)} fusion(bf16[1,16,32,2176]{3,2,1,0:T(8,128)(2,1)} %param.10), kind=kLoop, calls=%fused_computation.10 | loop fusion | flops 13334528 | bytes 2367488 | tf_op jit(solution)/shard_map/reduce_sum | solution.py:220
  12.5 0.4 div.25
  13.0 0.2 pad_bitcast_fusion
  13.2 0.8 reshape.169
  14.0 6.2 %collective-permute-start.5 = (bf16[36,2176]{1,0:T(8,128)(2,1)S(1)}, bf16[36,2176]{1,0:T(8,128)(2,1)S(1)}, u32[]{:S(2)}, u32[]{:S(2)}) collective-permute-start(bf16[36,2176]{1,0:T(8,128)(2,1)S(1)} %bitcast.47), channel_id=1, source_target_pairs={{1,0},{2,1},{3,2},{0,3},{5,4},{6,5},{7,6},{4,7},{9,8},{10,9},{11,1... | collective-permute-start | bytes 470024 | tf_op jit(solution)/shard_map/ppermute | solution.py:21
  20.2 3.8 %collective-permute-start.4 = (bf16[36,2176]{1,0:T(8,128)(2,1)S(1)}, bf16[36,2176]{1,0:T(8,128)(2,1)S(1)}, u32[]{:S(2)}, u32[]{:S(2)}) collective-permute-start(bf16[36,2176]{1,0:T(8,128)(2,1)S(1)} %bitcast.48), channel_id=1, source_target_pairs={{2,0},{3,1},{0,2},{1,3},{6,4},{7,5},{4,6},{5,7},{10,8},{11,9},{8,1... | collective-permute-start | bytes 470024 | tf_op jit(solution)/shard_map/ppermute | solution.py:21
  24.0 4.5 %collective-permute-start.3 = (bf16[36,2176]{1,0:T(8,128)(2,1)S(1)}, bf16[36,2176]{1,0:T(8,128)(2,1)S(1)}, u32[]{:S(2)}, u32[]{:S(2)}) collective-permute-start(bf16[36,2176]{1,0:T(8,128)(2,1)S(1)} %bitcast.49), channel_id=1, source_target_pairs={{3,0},{0,1},{1,2},{2,3},{7,4},{4,5},{5,6},{6,7},{11,8},{8,9},{9,10... | collective-permute-start | bytes 470024 | tf_op jit(solution)/shard_map/ppermute | solution.py:21
  28.5 6.5 %collective-permute-done.5 = bf16[36,2176]{1,0:T(8,128)(2,1)S(1)} collective-permute-done((bf16[36,2176]{1,0:T(8,128)(2,1)S(1)}, bf16[36,2176]{1,0:T(8,128)(2,1)S(1)}, u32[]{:S(2)}, u32[]{:S(2)}) %collective-permute-start.5) | collective-permute-done | bytes 156704 | tf_op jit(solution)/shard_map/ppermute | solution.py:21
  35.0 1.9 %collective-permute-done.4 = bf16[36,2176]{1,0:T(8,128)(2,1)S(1)} collective-permute-done((bf16[36,2176]{1,0:T(8,128)(2,1)S(1)}, bf16[36,2176]{1,0:T(8,128)(2,1)S(1)}, u32[]{:S(2)}, u32[]{:S(2)}) %collective-permute-start.4) | collective-permute-done | bytes 156704 | tf_op jit(solution)/shard_map/ppermute | solution.py:21
  37.0 0.1 select_select_fusion.3
  37.1 0.9 pad_maximum_fusion.1
  38.0 0.0 all-gather.5.cloned.1.call-update
  38.0 9.4 %all-to-all-start = ((f32[4,16,704]{2,1,0:T(8,128)}), f32[4,16,704]{2,1,0:T(8,128)S(1)}, u32[]{:S(2)}, u32[]{:S(2)}) async-start(f32[4,16,704]{2,1,0:T(8,128)} %reshape.169), calls=%async_computation | async-start | bytes 393216 | tf_op jit(solution)/shard_map/all_to_all | solution.py:172
  49.5 0.1 broadcast_in_dim.58
  49.5 0.1 broadcast_in_dim.59
  49.6 0.1 iota_add_fusion.1
  49.7 0.1 add.131
  49.8 0.1 add_multiply_fusion
  49.9 0.1 iota_add_fusion
  50.0 0.1 add.139
  50.0 0.3 convert_reduce_fusion.1
  50.3 0.1 bitcast_select_fusion.own_ref
  50.4 7.9 %all-gather.3.cloned.1.call-done.blocks_ref = bf16[704,1152]{1,0:T(8,128)(2,1)} async-done(((bf16[88,1152]{1,0:T(8,128)(2,1)}), bf16[704,1152]{1,0:T(8,128)(2,1)}) %all-gather.3.cloned.1.call-update) | async-done | bytes 1622032 | tf_op jit(solution)/shard_map/all_gather | solution.py:215
  58.3 1.1 multiply_reduce_fusion
  59.4 0.1 rsqrt.29
  59.5 0.0 all-to-all-done
  59.5 1.4 copy-done
  61.0 0.7 shard_map.104
  61.7 0.8 broadcast_in_dim.64
  62.5 6.7 %all-to-all-start.1 = ((bf16[4,64,1152]{2,1,0:T(8,128)(2,1)}), bf16[4,64,1152]{2,1,0:T(8,128)(2,1)}, u32[]{:S(2)}, u32[]{:S(2)}) async-start(bf16[4,64,1152]{2,1,0:T(8,128)(2,1)} %broadcast_in_dim.64), calls=%async_computation.1 | async-start | bytes 1179648 | tf_op jit(solution)/shard_map/all_to_all | solution.py:172
  69.3 0.1 fusion.14
  69.4 4.8 %collective-permute-start.2 = (bf16[128,1152]{1,0:T(8,128)(2,1)S(1)}, bf16[128,1152]{1,0:T(8,128)(2,1)}, u32[]{:S(2)}, u32[]{:S(2)}) collective-permute-start(bf16[128,1152]{1,0:T(8,128)(2,1)S(1)} %fusion.14), channel_id=1, source_target_pairs={{3,0},{0,1},{1,2},{2,3},{7,4},{4,5},{5,6},{6,7},{11,8},{8,9},{9,10... | collective-permute-start | bytes 884744 | tf_op jit(solution)/shard_map/ppermute | solution.py:21
  74.2 5.5 %collective-permute-start.1 = (bf16[128,1152]{1,0:T(8,128)(2,1)S(1)}, bf16[128,1152]{1,0:T(8,128)(2,1)}, u32[]{:S(2)}, u32[]{:S(2)}) collective-permute-start(bf16[128,1152]{1,0:T(8,128)(2,1)S(1)} %fusion.14), channel_id=1, source_target_pairs={{2,0},{3,1},{0,2},{1,3},{6,4},{7,5},{4,6},{5,7},{10,8},{11,9},{8,1... | collective-permute-start | bytes 884744 | tf_op jit(solution)/shard_map/ppermute | solution.py:21
  79.7 5.5 %collective-permute-start = (bf16[128,1152]{1,0:T(8,128)(2,1)S(1)}, bf16[128,1152]{1,0:T(8,128)(2,1)}, u32[]{:S(2)}, u32[]{:S(2)}) collective-permute-start(bf16[128,1152]{1,0:T(8,128)(2,1)S(1)} %fusion.14), channel_id=1, source_target_pairs={{1,0},{2,1},{3,2},{0,3},{5,4},{6,5},{7,6},{4,7},{9,8},{10,9},{11,1... | collective-permute-start | bytes 884744 | tf_op jit(solution)/shard_map/ppermute | solution.py:21
  85.2 3.9 %all-to-all-done.1 = bf16[4,64,1152]{2,1,0:T(8,128)(2,1)} async-done(((bf16[4,64,1152]{2,1,0:T(8,128)(2,1)}), bf16[4,64,1152]{2,1,0:T(8,128)(2,1)}, u32[]{:S(2)}, u32[]{:S(2)}) %all-to-all-start.1) | async-done | bytes 589856 | tf_op jit(solution)/shard_map/all_to_all | solution.py:172
  89.1 1.2 convert_reduce_fusion.2
  90.3 0.1 multiply_reduce_fusion.2
  90.4 10.0 %collective-permute-done.2 = bf16[128,1152]{1,0:T(8,128)(2,1)} collective-permute-done((bf16[128,1152]{1,0:T(8,128)(2,1)S(1)}, bf16[128,1152]{1,0:T(8,128)(2,1)}, u32[]{:S(2)}, u32[]{:S(2)}) %collective-permute-start.2) | collective-permute-done | bytes 294944 | tf_op jit(solution)/shard_map/ppermute | solution.py:21
  100.4 4.7 %collective-permute-done.1 = bf16[128,1152]{1,0:T(8,128)(2,1)} collective-permute-done((bf16[128,1152]{1,0:T(8,128)(2,1)S(1)}, bf16[128,1152]{1,0:T(8,128)(2,1)}, u32[]{:S(2)}, u32[]{:S(2)}) %collective-permute-start.1) | collective-permute-done | bytes 294944 | tf_op jit(solution)/shard_map/ppermute | solution.py:21
  105.1 2.0 %collective-permute-done = bf16[128,1152]{1,0:T(8,128)(2,1)} collective-permute-done((bf16[128,1152]{1,0:T(8,128)(2,1)S(1)}, bf16[128,1152]{1,0:T(8,128)(2,1)}, u32[]{:S(2)}, u32[]{:S(2)}) %collective-permute-start) | collective-permute-done | bytes 294944 | tf_op jit(solution)/shard_map/ppermute | solution.py:21
  107.1 1.7 %fusion.13 = bf16[64,512]{1,0:T(8,128)(2,1)S(1)} fusion(bf16[128,1152]{1,0:T(8,128)(2,1)} %collective-permute-done.2, bf16[128,1152]{1,0:T(8,128)(2,1)} %collective-permute-done.1, bf16[128,1152]{1,0:T(8,128)(2,1)} %collective-permute-done, bf16[128,1152]{1,0:T(8,128)(2,1)S(1)} %fusion.14, f32[]{:T(128)} %bitcast.38, f32[]{:T(128)} %bitcast.37, ...), kind=kOutput, calls=%fused_computation.23 | convolution fusion | flops 80756736 | bytes 1542668 | tf_op jit(solution)/shard_map/dot_general | solution.py:40
  108.7 1.6 multiply_reduce_fusion.1
  110.3 0.1 fusion.25
  110.5 1.3 shard_map.105
  111.7 4.5 %all-to-all-start.2 = ((bf16[4,16,704]{2,1,0:T(8,128)(2,1)}), bf16[4,16,704]{2,1,0:T(8,128)(2,1)S(1)}, u32[]{:S(2)}, u32[]{:S(2)}) async-start(bf16[4,16,704]{2,1,0:T(8,128)(2,1)} %bitcast.12), calls=%async_computation.2 | async-start | bytes 196608 | tf_op jit(solution)/shard_map/all_to_all | solution.py:172
  116.2 1.6 %copy-done.2 = bf16[1,16,32,2176]{3,2,1,0:T(8,128)(2,1)S(1)} copy-done((bf16[1,16,32,2176]{3,2,1,0:T(8,128)(2,1)S(1)}, bf16[1,16,32,2176]{3,2,1,0:T(8,128)(2,1)}, u32[]{:S(2)}) %copy-start.2) | copy-done | bytes 2228248
  117.8 4.2 %shard_map.106.slope_ref = f32[512,2176]{1,0:T(8,128)} custom-call(bf16[512,2176]{1,0:T(8,128)(2,1)S(1)} %bitcast.42), custom_call_target="tpu_custom_call" | custom-call | flops 22282240 | bytes 6684672 | tf_op jit(solution)/shard_map/pallas_call | solution.py:97
  122.0 1.0 convolution_convert_fusion
  123.0 1.6 all-to-all-done.2.grad_ref
  124.7 6.4 %all-to-all-start.3 = ((bf16[8,16,1152]{2,1,0:T(8,128)(2,1)}), bf16[8,16,1152]{2,1,0:T(8,128)(2,1)S(1)}, u32[]{:S(2)}, u32[]{:S(2)}) async-start(bf16[8,16,1152]{2,1,0:T(8,128)(2,1)} %bitcast.17), calls=%async_computation.3 | async-start | bytes 589824 | tf_op jit(solution)/shard_map/all_to_all | solution.py:301
  131.1 0.0 all-gather.5.cloned.1.call-done.up_ref
  131.1 7.6 %shard_map.107 = bf16[512,1152]{1,0:T(8,128)(2,1)S(1)} custom-call(bf16[4,16,704]{2,1,0:T(8,128)(2,1)S(1)} %all-to-all-done.2.grad_ref, f32[512,2176]{1,0:T(8,128)} %shard_map.106.slope_ref, bf16[1152,2176]{1,0:T(8,128)(2,1)} %all-gather.5.cloned.1.call-done.up_ref, bf16[512,1152]{1,0:T(8,128)(2,1)S(1)} %bitcast.43, ...), custom_call_target="tpu_custom_call" | custom-call | flops 2566914048 | bytes 11829248 | tf_op jit(solution)/shard_map/pallas_call | solution.py:148
  138.8 1.9 %collective-permute-start.6 = (bf16[1,16,32,1152]{3,2,1,0:T(8,128)(2,1)S(1)}, bf16[1,16,32,1152]{3,2,1,0:T(8,128)(2,1)S(1)}, u32[]{:S(2)}, u32[]{:S(2)}) collective-permute-start(bf16[1,16,32,1152]{3,2,1,0:T(8,128)(2,1)S(1)} %bitcast.44), channel_id=1, source_target_pairs={{32,0},{64,32},{96,64},{128,96},{160,128},{192,160},{224,192},{256... | collective-permute-start | bytes 3538952 | tf_op jit(solution)/shard_map/ppermute | solution.py:21
  140.7 0.1 fusion.16
  140.8 1.1 all-to-all-done.3
  142.0 0.2 fusion.18
  142.2 0.7 fusion.20
  142.9 11.5 %collective-permute-done.6 = bf16[1,16,32,1152]{3,2,1,0:T(8,128)(2,1)S(1)} collective-permute-done((bf16[1,16,32,1152]{3,2,1,0:T(8,128)(2,1)S(1)}, bf16[1,16,32,1152]{3,2,1,0:T(8,128)(2,1)S(1)}, u32[]{:S(2)}, u32[]{:S(2)}) %collective-permute-start.6) | collective-permute-done | bytes 1179680 | tf_op jit(solution)/shard_map/ppermute | solution.py:21
  154.4 1.0 copy.17
  (27 shorter events, 0.2 us)
Async XLA Ops:
  7.2 51.2 %all-gather.3.cloned.1.call-start = ((), (), s32[]{:S(2)}) async-start(), calls=%async_computation.4 | async-start | bytes 1824768 | tf_op jit(solution)/shard_map/all_gather | solution.py:215
  9.0 5.0 %copy-start.6 = (bf16[1,36,2176]{2,1,0:T(8,128)(2,1)S(1)}, bf16[1,36,2176]{2,1,0:T(8,128)(2,1)}, u32[]{:S(2)}) copy-start(bf16[1,36,2176]{2,1,0:T(8,128)(2,1)} %param.12) | copy-start | bytes 470020
  9.0 122.1 %all-gather.5.cloned.1.call-start = ((), (), s32[]{:S(2)}) async-start(), calls=%async_computation.5 | async-start | bytes 5640192 | tf_op jit(solution)/shard_map/all_gather | solution.py:236
  13.2 36.9 %copy-start.3 = (bf16[1,16,32,1152]{3,2,1,0:T(8,128)(2,1)S(1)}, bf16[1,16,32,1152]{3,2,1,0:T(8,128)(2,1)}, u32[]{:S(2)}) copy-start(bf16[1,16,32,1152]{3,2,1,0:T(8,128)(2,1)} %param.9) | copy-start | bytes 3538948
  14.0 21.0 %collective-permute-start.5 = (bf16[36,2176]{1,0:T(8,128)(2,1)S(1)}, bf16[36,2176]{1,0:T(8,128)(2,1)S(1)}, u32[]{:S(2)}, u32[]{:S(2)}) collective-permute-start(bf16[36,2176]{1,0:T(8,128)(2,1)S(1)} %bitcast.47), channel_id=1, source_target_pairs={{1,0},{2,1},{3,2},{0,3},{5,4},{6,5},{7,6},{4,7},{9,8},{10,9},{11,1... | collective-permute-start | bytes 470024 | tf_op jit(solution)/shard_map/ppermute | solution.py:21
  20.2 16.8 %collective-permute-start.4 = (bf16[36,2176]{1,0:T(8,128)(2,1)S(1)}, bf16[36,2176]{1,0:T(8,128)(2,1)S(1)}, u32[]{:S(2)}, u32[]{:S(2)}) collective-permute-start(bf16[36,2176]{1,0:T(8,128)(2,1)S(1)} %bitcast.48), channel_id=1, source_target_pairs={{2,0},{3,1},{0,2},{1,3},{6,4},{7,5},{4,6},{5,7},{10,8},{11,9},{8,1... | collective-permute-start | bytes 470024 | tf_op jit(solution)/shard_map/ppermute | solution.py:21
  24.0 13.0 %collective-permute-start.3 = (bf16[36,2176]{1,0:T(8,128)(2,1)S(1)}, bf16[36,2176]{1,0:T(8,128)(2,1)S(1)}, u32[]{:S(2)}, u32[]{:S(2)}) collective-permute-start(bf16[36,2176]{1,0:T(8,128)(2,1)S(1)} %bitcast.49), channel_id=1, source_target_pairs={{3,0},{0,1},{1,2},{2,3},{7,4},{4,5},{5,6},{6,7},{11,8},{8,9},{9,10... | collective-permute-start | bytes 470024 | tf_op jit(solution)/shard_map/ppermute | solution.py:21
  38.0 21.5 %all-to-all-start = ((f32[4,16,704]{2,1,0:T(8,128)}), f32[4,16,704]{2,1,0:T(8,128)S(1)}, u32[]{:S(2)}, u32[]{:S(2)}) async-start(f32[4,16,704]{2,1,0:T(8,128)} %reshape.169), calls=%async_computation | async-start | bytes 393216 | tf_op jit(solution)/shard_map/all_to_all | solution.py:172
  59.5 1.4 copy-start
  61.0 8.3 %copy-start.1 = (bf16[704,1152]{1,0:T(8,128)(2,1)S(1)}, bf16[704,1152]{1,0:T(8,128)(2,1)}, u32[]{:S(2)}) copy-start(bf16[704,1152]{1,0:T(8,128)(2,1)} %all-gather.3.cloned.1.call-done.blocks_ref) | copy-start | bytes 4866052
  62.5 26.6 %all-to-all-start.1 = ((bf16[4,64,1152]{2,1,0:T(8,128)(2,1)}), bf16[4,64,1152]{2,1,0:T(8,128)(2,1)}, u32[]{:S(2)}, u32[]{:S(2)}) async-start(bf16[4,64,1152]{2,1,0:T(8,128)(2,1)} %broadcast_in_dim.64), calls=%async_computation.1 | async-start | bytes 1179648 | tf_op jit(solution)/shard_map/all_to_all | solution.py:172
  69.4 31.0 %collective-permute-start.2 = (bf16[128,1152]{1,0:T(8,128)(2,1)S(1)}, bf16[128,1152]{1,0:T(8,128)(2,1)}, u32[]{:S(2)}, u32[]{:S(2)}) collective-permute-start(bf16[128,1152]{1,0:T(8,128)(2,1)S(1)} %fusion.14), channel_id=1, source_target_pairs={{3,0},{0,1},{1,2},{2,3},{7,4},{4,5},{5,6},{6,7},{11,8},{8,9},{9,10... | collective-permute-start | bytes 884744 | tf_op jit(solution)/shard_map/ppermute | solution.py:21
  74.2 30.9 %collective-permute-start.1 = (bf16[128,1152]{1,0:T(8,128)(2,1)S(1)}, bf16[128,1152]{1,0:T(8,128)(2,1)}, u32[]{:S(2)}, u32[]{:S(2)}) collective-permute-start(bf16[128,1152]{1,0:T(8,128)(2,1)S(1)} %fusion.14), channel_id=1, source_target_pairs={{2,0},{3,1},{0,2},{1,3},{6,4},{7,5},{4,6},{5,7},{10,8},{11,9},{8,1... | collective-permute-start | bytes 884744 | tf_op jit(solution)/shard_map/ppermute | solution.py:21
  79.7 27.4 %collective-permute-start = (bf16[128,1152]{1,0:T(8,128)(2,1)S(1)}, bf16[128,1152]{1,0:T(8,128)(2,1)}, u32[]{:S(2)}, u32[]{:S(2)}) collective-permute-start(bf16[128,1152]{1,0:T(8,128)(2,1)S(1)} %fusion.14), channel_id=1, source_target_pairs={{1,0},{2,1},{3,2},{0,3},{5,4},{6,5},{7,6},{4,7},{9,8},{10,9},{11,1... | collective-permute-start | bytes 884744 | tf_op jit(solution)/shard_map/ppermute | solution.py:21
  111.7 12.9 %all-to-all-start.2 = ((bf16[4,16,704]{2,1,0:T(8,128)(2,1)}), bf16[4,16,704]{2,1,0:T(8,128)(2,1)S(1)}, u32[]{:S(2)}, u32[]{:S(2)}) async-start(bf16[4,16,704]{2,1,0:T(8,128)(2,1)} %bitcast.12), calls=%async_computation.2 | async-start | bytes 196608 | tf_op jit(solution)/shard_map/all_to_all | solution.py:172
  116.2 1.6 %copy-start.2 = (bf16[1,16,32,2176]{3,2,1,0:T(8,128)(2,1)S(1)}, bf16[1,16,32,2176]{3,2,1,0:T(8,128)(2,1)}, u32[]{:S(2)}) copy-start(bf16[1,16,32,2176]{3,2,1,0:T(8,128)(2,1)} %param.10) | copy-start | bytes 6684676
  117.8 13.3 %copy-start.4 = (f32[1,1152]{1,0:T(1,128)S(1)}, f32[1,1152]{1,0:T(1,128)}, u32[]{:S(2)}) copy-start(f32[1,1152]{1,0:T(1,128)} %multiplier_ref.1) | copy-start | bytes 13828
  124.7 17.3 %all-to-all-start.3 = ((bf16[8,16,1152]{2,1,0:T(8,128)(2,1)}), bf16[8,16,1152]{2,1,0:T(8,128)(2,1)S(1)}, u32[]{:S(2)}, u32[]{:S(2)}) async-start(bf16[8,16,1152]{2,1,0:T(8,128)(2,1)} %bitcast.17), calls=%async_computation.3 | async-start | bytes 589824 | tf_op jit(solution)/shard_map/all_to_all | solution.py:301
  131.1 9.6 %copy-start.5 = (bf16[1,16,1152]{2,1,0:T(8,128)(2,1)S(1)}, bf16[1,16,1152]{2,1,0:T(8,128)(2,1)}, u32[]{:S(2)}) copy-start(bf16[1,16,1152]{2,1,0:T(8,128)(2,1)} %param.14) | copy-start | bytes 110596
  138.8 15.6 %collective-permute-start.6 = (bf16[1,16,32,1152]{3,2,1,0:T(8,128)(2,1)S(1)}, bf16[1,16,32,1152]{3,2,1,0:T(8,128)(2,1)S(1)}, u32[]{:S(2)}, u32[]{:S(2)}) collective-permute-start(bf16[1,16,32,1152]{3,2,1,0:T(8,128)(2,1)S(1)} %bitcast.44), channel_id=1, source_target_pairs={{32,0},{64,32},{96,64},{128,96},{160,128},{192,160},{224,192},{256... | collective-permute-start | bytes 3538952 | tf_op jit(solution)/shard_map/ppermute | solution.py:21
Sparse Core Ops, SparseCore 0:
  10.1 48.1 all-gather.2
  61.0 63.9 all-gather.4

commit v6 on v5

--- a/solution.py
+++ b/solution.py
@@ -58,14 +58,25 @@
     )
 
 
-def partial_kernel(means_ref, blocks_ref, own_ref, sums_ref):
+def partial_kernel(images, means_ref, blocks_ref, own_ref, sent_ref):
     means = means_ref[...]
     high = means.astype(jnp.bfloat16)
     low = (means - high.astype(jnp.float32)).astype(jnp.bfloat16)
     blocks = blocks_ref[...]
     sums = jnp.dot(high, blocks, preferred_element_type=jnp.float32)
     sums = sums + jnp.dot(low, blocks, preferred_element_type=jnp.float32)
-    sums_ref[...] = (sums + own_ref[...]).astype(jnp.bfloat16)
+    sums = (sums + own_ref[...]).astype(jnp.bfloat16)
+    rows, width = sums.shape
+    blocks_z = sent_ref.shape[1] // images - rows // images
+    block_rows = blocks.shape[0] // blocks_z
+    for at in range(blocks_z):
+        text = blocks[at * block_rows : at * block_rows + images].astype(jnp.float32)
+        inverse = lax.rsqrt(jnp.sum(text * text, axis=-1, keepdims=True) + EPSILON)
+        unit = (text * inverse).astype(jnp.bfloat16)
+        for peer in range(sent_ref.shape[0]):
+            sent_ref[peer, rows + at * images : rows + (at + 1) * images] = unit
+    for peer in range(sent_ref.shape[0]):
+        sent_ref[peer, :rows] = sums
 
 
 def back_kernel(grads_ref, blocks_ref, sent_ref):
@@ -75,10 +86,10 @@
     sent_ref[...] = hidden.astype(jnp.bfloat16)
 
 
-def small_call(kernel, rows, columns, operands, flops):
+def small_call(kernel, shape, operands, flops):
     return pl.pallas_call(
         kernel,
-        out_shape=jax.ShapeDtypeStruct((rows, columns), jnp.bfloat16),
+        out_shape=jax.ShapeDtypeStruct(shape, jnp.bfloat16),
         in_specs=[pl.BlockSpec(memory_space=pltpu.VMEM)] * len(operands),
         out_specs=pl.BlockSpec(memory_space=pltpu.VMEM),
         compiler_params=pltpu.CompilerParams(vmem_limit_bytes=VMEM_BYTES),
@@ -239,22 +250,16 @@
     own_means = jnp.where(
         jnp.arange(Y_SHARDS, dtype=jnp.int32)[:, None, None] == y, mean_tokens[None], 0.0
     ).reshape(row, model_width)
-    partial = small_call(
-        partial_kernel,
-        row,
-        model_width,
-        (row_mean, blocks, own_means),
-        4 * row * part * model_width,
-    )
-    partials = exchange_y(jnp.broadcast_to(partial[None], (Y_SHARDS, row, model_width)))
-    column_text = blocks.reshape(z_size, block_rows, model_width)[:, :images]
-    column_text = unit_rows(
-        column_text.reshape(z_size * images, model_width).astype(jnp.float32)
-    )[0].astype(jnp.bfloat16)
-    text_all = jnp.concatenate(
-        [column_text] + [from_ahead(column_text, "y", k) for k in range(1, Y_SHARDS)], axis=0
-    )
-    pooled = jnp.sum(partials.astype(jnp.float32), axis=0)
+    shared = exchange_y(
+        small_call(
+            functools.partial(partial_kernel, images),
+            (Y_SHARDS, row + z_size * images, model_width),
+            (row_mean, blocks, own_means),
+            4 * row * part * model_width,
+        )
+    )
+    text_all = shared[:, row:].reshape(-1, model_width)
+    pooled = jnp.sum(shared[:, :row].astype(jnp.float32), axis=0)
     image_dir, image_inverse = unit_rows(pooled)
     image_unit = image_dir.astype(jnp.bfloat16)
 
@@ -273,7 +278,7 @@
         text_all,
         index_of(
             lax.broadcasted_iota(jnp.int32, (Y_SHARDS, z_size), 1),
-            (y + lax.broadcasted_iota(jnp.int32, (Y_SHARDS, z_size), 0)) % Y_SHARDS,
+            lax.broadcasted_iota(jnp.int32, (Y_SHARDS, z_size), 0),
         ).reshape(-1),
     )
     image_sum = jnp.dot(weights, text_all, preferred_element_type=jnp.float32)
@@ -286,22 +291,15 @@
     preacts, row_grad = lax.optimization_barrier((stored_hidden_preacts[0], row_grad))
     slope = slopes(preacts.reshape(images * patches, hidden))
     sent_back = small_call(
-        back_kernel, row, part, (row_grad, blocks), 2 * row * part * model_width
+        back_kernel, (row, part), (row_grad, blocks), 2 * row * part * model_width
     )
     received = exchange_y(sent_back.reshape(Y_SHARDS, images, part))
     column_sums = lax.dot_general(
-        weights[:, : z_size * images],
+        lax.dynamic_slice_in_dim(weights, y * z_size * images, z_size * images, axis=1),
         image_unit,
         (((0,), (0,)), ((), ())),
         preferred_element_type=jnp.float32,
     )
-    column_sums, received = lax.optimization_barrier(
-        (column_sums.astype(jnp.bfloat16), received)
-    )
-    text_sums = lax.all_to_all(
-        column_sums.reshape(z_size, images, model_width), "z", 0, 0
-    )
-    text_sum = jnp.sum(text_sums.astype(jnp.float32), axis=0)
     pieces = [
         (
             own,
@@ -320,7 +318,15 @@
         share,
         layernorm_multiplier,
     ).reshape(images, patches, model_width)
+    column_sums, span_grad = lax.optimization_barrier(
+        (column_sums.astype(jnp.bfloat16), span_grad)
+    )
     prev_grad = from_ahead(span_grad[None], "section", 1)
+    text_sums = lax.all_to_all(
+        column_sums.reshape(z_size, images, model_width), "z", 0, 0
+    )
+    text_sums, prev_grad = lax.optimization_barrier((text_sums, prev_grad))
+    text_sum = jnp.sum(text_sums.astype(jnp.float32), axis=0)
 
     text_dir, text_inverse = unit_rows(caption_tower_outputs[0].astype(jnp.float32))
     text_grad = (

time: 165 us -> 162 us (0.982)
  waiting for transfers between devices: 51.2 us -> 76.3 us
  starting transfers between devices: 59.3 us -> 36.1 us
  other arithmetic: 10.6 us -> 8.87 us
    all_to_all x3, waiting for transfers between devices: 5.55 us -> 48.2 us  [exchange_y(): return lax.all_to_all(blocks, 'y', 0, 0)]
    ppermute x7 -> x4, waiting for transfers between devices: 36.7 us -> 9.52 us  [from_ahead(): lax.ppermute(array, axis, [((i + by) % peers, i) for i in range(peers)])]
    ppermute x7 -> x4, starting transfers between devices: 32.2 us -> 17.6 us  [from_ahead(): lax.ppermute(array, axis, [((i + by) % peers, i) for i in range(peers)])]
    all_to_all x1, waiting for transfers between devices: 1.07 us -> 11.9 us  [per_device(): lax.all_to_all(column_sums.reshape(z_size, images, model_width), 'z', 0, 0)]
    all_to_all x3, starting transfers between devices: 20.6 us -> 14.3 us  [exchange_y(): return lax.all_to_all(blocks, 'y', 0, 0)]
    all_gather x1, waiting for transfers between devices: 7.89 us -> 4.57 us  [per_device(): blocks = lax.all_gather(block, 'z', axis=0, tiled=True)]
    all_to_all x1, starting transfers between devices: 6.42 us -> 4.15 us  [per_device(): lax.all_to_all(column_sums.reshape(z_size, images, model_width), 'z', 0, 0)]
    all_gather x1, waiting for transfers between devices: 0.01 us -> 2.08 us  [per_device(): up_whole = lax.all_gather(up_y, 'z', axis=0, tiled=True)]
  transfers between devices with their start and end apart: 13 -> 10, of which waited for: 10 -> 8; matrix products, arithmetic and copies ran while one was open for 10% -> 7% of each run, Pallas kernels for 8% -> 4%
where the time goes in v6:
time: 162 us; the launch traced here: 161 us
  waiting for transfers between devices  76.3 us (47%)
  starting transfers between devices  36.1 us (22%)
  between operations  16.3 us (10%)
  Pallas kernels  14.5 us (9%)
  other arithmetic  8.87 us (5%)
  local copies, waits for them, and re-layouts  6.11 us (4%)
  matrix products  2.69 us (2%)
    all_to_all x3, waiting for transfers between devices, exchange_y(): return lax.all_to_all(blocks, 'y', 0, 0)  48.2 us
    ppermute x4, starting transfers between devices, from_ahead(): lax.ppermute(array, axis, [((i + by) % peers, i) for i in range(peers)])  17.6 us
    all_to_all x3, starting transfers between devices, exchange_y(): return lax.all_to_all(blocks, 'y', 0, 0)  14.3 us
    all_to_all x1, waiting for transfers between devices, per_device(): lax.all_to_all(column_sums.reshape(z_size, images, model_width), 'z', 0, 0)  11.9 us
    ppermute x4, waiting for transfers between devices, from_ahead(): lax.ppermute(array, axis, [((i + by) % peers, i) for i in range(peers)])  9.52 us
    pallas_call x1, Pallas kernels, span(): pl.pallas_call(functools.partial(span_kernel, pieces), grid=(count // row...  7.63 us
    all_gather x1, waiting for transfers between devices, per_device(): blocks = lax.all_gather(block, 'z', axis=0, tiled=True)  4.57 us
    pallas_call x1, Pallas kernels, slopes(): pl.pallas_call(slope_kernel, grid=(tokens // block,), in_specs=[spec], ou...  4.22 us
  transfers between devices with their start and end apart: 10, of which 8 were waited for; matrix products, arithmetic and copies ran while one was open for 7% of the time, Pallas kernels for 4%

profile of v6, /device:TPU:6, one launch (start us, length us, event | category | flops | bytes accessed | tf_op | source)
XLA Modules:
  0.0 160.8 jit_solution(4220822524566955336)
XLA Ops:
  7.2 0.0 all-gather.3.cloned.1.call-start
  7.2 0.1 pad.11.clone
  7.3 1.7 %maximum_maximum_fusion = bf16[88,1152]{1,0:T(8,128)(2,1)} fusion(bf16[68,1152]{1,0:T(8,128)(2,1)} %bitcast.51, bf16[16,1152]{1,0:T(8,128)(2,1)} %bitcast.46, bf16[88]{0:T(256)(128)(2,1)S(1)} %pad.11.clone), kind=kLoop, calls=%fused_computation.31 | loop fusion | flops 608256 | bytes 396464 | tf_op jit(solution)/shard_map/concatenate | solution.py:218
  9.0 0.0 all-gather.3.cloned.1.call-update
  9.0 0.0 copy-start.9
  9.0 0.0 all-gather.5.cloned.1.call-start
  9.1 3.5 %convert_reduce_fusion = f32[16,2176]{1,0:T(8,128)S(1)} fusion(bf16[1,16,32,2176]{3,2,1,0:T(8,128)(2,1)} %param.10), kind=kLoop, calls=%fused_computation.10 | loop fusion | flops 13334528 | bytes 2367488 | tf_op jit(solution)/shard_map/reduce_sum | solution.py:231
  12.6 0.4 div.25
  13.0 0.2 pad_bitcast_fusion
  13.2 0.8 reshape.128
  14.0 7.7 %collective-permute-start.1 = (bf16[36,2176]{1,0:T(8,128)(2,1)S(1)}, bf16[36,2176]{1,0:T(8,128)(2,1)S(1)}, u32[]{:S(2)}, u32[]{:S(2)}) collective-permute-start(bf16[36,2176]{1,0:T(8,128)(2,1)S(1)} %bitcast.47), channel_id=1, source_target_pairs={{2,0},{3,1},{0,2},{1,3},{6,4},{7,5},{4,6},{5,7},{10,8},{11,9},{8,1... | collective-permute-start | bytes 470024 | tf_op jit(solution)/shard_map/ppermute | solution.py:21
  21.8 2.2 %collective-permute-start.2 = (bf16[36,2176]{1,0:T(8,128)(2,1)S(1)}, bf16[36,2176]{1,0:T(8,128)(2,1)S(1)}, u32[]{:S(2)}, u32[]{:S(2)}) collective-permute-start(bf16[36,2176]{1,0:T(8,128)(2,1)S(1)} %bitcast.48), channel_id=1, source_target_pairs={{1,0},{2,1},{3,2},{0,3},{5,4},{6,5},{7,6},{4,7},{9,8},{10,9},{11,1... | collective-permute-start | bytes 470024 | tf_op jit(solution)/shard_map/ppermute | solution.py:21
  24.0 4.5 %collective-permute-start = (bf16[36,2176]{1,0:T(8,128)(2,1)S(1)}, bf16[36,2176]{1,0:T(8,128)(2,1)S(1)}, u32[]{:S(2)}, u32[]{:S(2)}) collective-permute-start(bf16[36,2176]{1,0:T(8,128)(2,1)S(1)} %bitcast.49), channel_id=1, source_target_pairs={{3,0},{0,1},{1,2},{2,3},{7,4},{4,5},{5,6},{6,7},{11,8},{8,9},{9,10... | collective-permute-start | bytes 470024 | tf_op jit(solution)/shard_map/ppermute | solution.py:21
  28.5 0.0 copy-start.3
  28.5 0.1 collective-permute-done.1
  28.6 9.4 %collective-permute-done.2 = bf16[36,2176]{1,0:T(8,128)(2,1)S(1)} collective-permute-done((bf16[36,2176]{1,0:T(8,128)(2,1)S(1)}, bf16[36,2176]{1,0:T(8,128)(2,1)S(1)}, u32[]{:S(2)}, u32[]{:S(2)}) %collective-permute-start.2) | collective-permute-done | bytes 156704 | tf_op jit(solution)/shard_map/ppermute | solution.py:21
  38.0 0.0 collective-permute-done
  38.1 0.1 select_select_fusion.3
  38.1 0.9 pad_maximum_fusion
  39.1 0.0 all-gather.5.cloned.1.call-update
  39.1 4.5 %all-to-all-start = ((f32[4,16,704]{2,1,0:T(8,128)}), f32[4,16,704]{2,1,0:T(8,128)S(1)}, u32[]{:S(2)}, u32[]{:S(2)}) async-start(f32[4,16,704]{2,1,0:T(8,128)} %reshape.128), calls=%async_computation | async-start | bytes 393216 | tf_op jit(solution)/shard_map/all_to_all | solution.py:183
  43.7 0.1 broadcast_in_dim.54
  43.7 0.1 broadcast_in_dim.55
  43.8 0.0 copy-done.3
  43.8 0.3 convert_reduce_fusion.1
  44.1 0.1 bitcast_select_fusion.own_ref
  44.2 9.5 %all-to-all-done = f32[4,16,704]{2,1,0:T(8,128)S(1)} async-done(((f32[4,16,704]{2,1,0:T(8,128)}), f32[4,16,704]{2,1,0:T(8,128)S(1)}, u32[]{:S(2)}, u32[]{:S(2)}) %all-to-all-start) | async-done | bytes 180256 | tf_op jit(solution)/shard_map/all_to_all | solution.py:183
  53.7 4.6 %all-gather.3.cloned.1.call-done.blocks_ref = bf16[704,1152]{1,0:T(8,128)(2,1)} async-done(((bf16[88,1152]{1,0:T(8,128)(2,1)}), bf16[704,1152]{1,0:T(8,128)(2,1)}) %all-gather.3.cloned.1.call-update) | async-done | bytes 1622032 | tf_op jit(solution)/shard_map/all_gather | solution.py:226
  58.3 1.4 copy-done.1
  59.7 2.0 %shard_map.104 = bf16[4,192,1152]{2,1,0:T(8,128)(2,1)} custom-call(f32[64,704]{1,0:T(8,128)S(1)} %bitcast.42, bf16[704,1152]{1,0:T(8,128)(2,1)S(1)} %copy-done.1, f32[64,1152]{1,0:T(8,128)S(1)} %bitcast_select_fusion.own_ref), custom_call_target="tpu_custom_call" | custom-call | flops 207618048 | bytes 2000000 | tf_op jit(solution)/shard_map/pallas_call | solution.py:90
  61.7 6.5 %all-to-all-start.1 = ((bf16[4,192,1152]{2,1,0:T(8,128)(2,1)}), bf16[4,192,1152]{2,1,0:T(8,128)(2,1)S(1)}, u32[]{:S(2)}, u32[]{:S(2)}) async-start(bf16[4,192,1152]{2,1,0:T(8,128)(2,1)} %shard_map.104), calls=%async_computation.1 | async-start | bytes 3538944 | tf_op jit(solution)/shard_map/all_to_all | solution.py:183
  69.5 0.1 iota_add_fusion
  69.6 0.1 add.112
  70.3 0.1 iota_add_fusion.1
  70.4 0.1 add.107
  70.5 37.1 %all-to-all-done.1 = bf16[4,192,1152]{2,1,0:T(8,128)(2,1)S(1)} async-done(((bf16[4,192,1152]{2,1,0:T(8,128)(2,1)}), bf16[4,192,1152]{2,1,0:T(8,128)(2,1)S(1)}, u32[]{:S(2)}, u32[]{:S(2)}) %all-to-all-start.1) | async-done | bytes 1769504 | tf_op jit(solution)/shard_map/all_to_all | solution.py:183
  107.6 0.1 slice.9
  107.7 0.1 convert_reduce_fusion.2
  107.8 0.1 multiply_reduce_fusion.1
  107.9 0.5 fusion.13
  108.5 0.4 multiply_reduce_fusion
  108.9 0.0 copy-start
  108.9 0.2 copy-done.10
  109.1 0.8 fusion.21
  110.0 0.0 copy-done.2
  110.0 0.6 shard_map.105
  110.6 0.0 copy-start.4
  110.6 0.6 copy-done.4
  111.2 3.3 %all-to-all-start.2 = ((bf16[4,16,704]{2,1,0:T(8,128)(2,1)}), bf16[4,16,704]{2,1,0:T(8,128)(2,1)S(1)}, u32[]{:S(2)}, u32[]{:S(2)}) async-start(bf16[4,16,704]{2,1,0:T(8,128)(2,1)} %bitcast.43), calls=%async_computation.2 | async-start | bytes 196608 | tf_op jit(solution)/shard_map/all_to_all | solution.py:183
  114.6 0.0 copy-start.5
  114.6 4.2 %shard_map.106.slope_ref = f32[512,2176]{1,0:T(8,128)} custom-call(bf16[512,2176]{1,0:T(8,128)(2,1)S(1)} %bitcast.39), custom_call_target="tpu_custom_call" | custom-call | flops 22282240 | bytes 6684672 | tf_op jit(solution)/shard_map/pallas_call | solution.py:108
  118.8 1.7 %convolution_convert_fusion = bf16[128,1152]{1,0:T(8,128)(2,1)} fusion(bf16[64,512]{1,0:T(8,128)(2,1)} %copy-done.10, s32[]{:T(128)S(6)} %select_n.89, f32[64,1152]{1,0:T(8,128)S(1)} %copy-done.7, f32[64]{0:T(128)S(1)} %add_rsqrt_fusion.1), kind=kOutput, calls=%fused_computation.11 | convolution fusion | flops 19169280 | bytes 606468 | tf_op jit(solution)/shard_map/dot_general | solution.py:297
  120.5 0.9 dynamic-slice_bitcast_fusion.share_ref
  121.4 1.6 all-to-all-done.2.grad_ref
  123.0 2.1 %all-gather.5.cloned.1.call-done.up_ref = bf16[1152,2176]{1,0:T(8,128)(2,1)} async-done(((bf16[144,2176]{1,0:T(8,128)(2,1)}), bf16[1152,2176]{1,0:T(8,128)(2,1)}) %all-gather.5.cloned.1.call-update) | async-done | bytes 5013520 | tf_op jit(solution)/shard_map/all_gather | solution.py:247
  125.1 7.6 %shard_map.107 = bf16[512,1152]{1,0:T(8,128)(2,1)S(1)} custom-call(bf16[4,16,704]{2,1,0:T(8,128)(2,1)S(1)} %all-to-all-done.2.grad_ref, f32[512,2176]{1,0:T(8,128)} %shard_map.106.slope_ref, bf16[1152,2176]{1,0:T(8,128)(2,1)} %all-gather.5.cloned.1.call-done.up_ref, bf16[512,1152]{1,0:T(8,128)(2,1)S(1)} %bitcast.40, ...), custom_call_target="tpu_custom_call" | custom-call | flops 2566914048 | bytes 11829248 | tf_op jit(solution)/shard_map/pallas_call | solution.py:159
  132.7 3.1 %collective-permute-start.3 = (bf16[1,16,32,1152]{3,2,1,0:T(8,128)(2,1)S(1)}, bf16[1,16,32,1152]{3,2,1,0:T(8,128)(2,1)S(1)}, u32[]{:S(2)}, u32[]{:S(2)}) collective-permute-start(bf16[1,16,32,1152]{3,2,1,0:T(8,128)(2,1)S(1)} %bitcast.41), channel_id=1, source_target_pairs={{32,0},{64,32},{96,64},{128,96},{160,128},{192,160},{224,192},{256... | collective-permute-start | bytes 3538952 | tf_op jit(solution)/shard_map/ppermute | solution.py:21
  135.8 4.2 %all-to-all-start.3 = ((bf16[8,16,1152]{2,1,0:T(8,128)(2,1)}), bf16[8,16,1152]{2,1,0:T(8,128)(2,1)S(1)}, u32[]{:S(2)}, u32[]{:S(2)}) async-start(bf16[8,16,1152]{2,1,0:T(8,128)(2,1)} %bitcast.16), calls=%async_computation.3 | async-start | bytes 589824 | tf_op jit(solution)/shard_map/all_to_all | solution.py:325
  140.0 0.1 fusion.14
  140.1 11.9 %all-to-all-done.3 = bf16[8,16,1152]{2,1,0:T(8,128)(2,1)S(1)} async-done(((bf16[8,16,1152]{2,1,0:T(8,128)(2,1)}), bf16[8,16,1152]{2,1,0:T(8,128)(2,1)S(1)}, u32[]{:S(2)}, u32[]{:S(2)}) %all-to-all-start.3) | async-done | bytes 294944 | tf_op jit(solution)/shard_map/all_to_all | solution.py:325
  152.0 0.0 collective-permute-done.3
  152.1 0.2 fusion.16
  152.3 0.7 fusion.18
  153.0 1.0 copy.16
  (23 shorter events, 0.1 us)
Async XLA Ops:
  7.2 51.1 %all-gather.3.cloned.1.call-start = ((), (), s32[]{:S(2)}) async-start(), calls=%async_computation.4 | async-start | bytes 1824768 | tf_op jit(solution)/shard_map/all_gather | solution.py:226
  9.0 5.0 %copy-start.9 = (bf16[1,36,2176]{2,1,0:T(8,128)(2,1)S(1)}, bf16[1,36,2176]{2,1,0:T(8,128)(2,1)}, u32[]{:S(2)}) copy-start(bf16[1,36,2176]{2,1,0:T(8,128)(2,1)} %param.12) | copy-start | bytes 470020
  9.0 116.0 %all-gather.5.cloned.1.call-start = ((), (), s32[]{:S(2)}) async-start(), calls=%async_computation.5 | async-start | bytes 5640192 | tf_op jit(solution)/shard_map/all_gather | solution.py:247
  14.0 14.6 %collective-permute-start.1 = (bf16[36,2176]{1,0:T(8,128)(2,1)S(1)}, bf16[36,2176]{1,0:T(8,128)(2,1)S(1)}, u32[]{:S(2)}, u32[]{:S(2)}) collective-permute-start(bf16[36,2176]{1,0:T(8,128)(2,1)S(1)} %bitcast.47), channel_id=1, source_target_pairs={{2,0},{3,1},{0,2},{1,3},{6,4},{7,5},{4,6},{5,7},{10,8},{11,9},{8,1... | collective-permute-start | bytes 470024 | tf_op jit(solution)/shard_map/ppermute | solution.py:21
  21.8 16.3 %collective-permute-start.2 = (bf16[36,2176]{1,0:T(8,128)(2,1)S(1)}, bf16[36,2176]{1,0:T(8,128)(2,1)S(1)}, u32[]{:S(2)}, u32[]{:S(2)}) collective-permute-start(bf16[36,2176]{1,0:T(8,128)(2,1)S(1)} %bitcast.48), channel_id=1, source_target_pairs={{1,0},{2,1},{3,2},{0,3},{5,4},{6,5},{7,6},{4,7},{9,8},{10,9},{11,1... | collective-permute-start | bytes 470024 | tf_op jit(solution)/shard_map/ppermute | solution.py:21
  24.0 14.0 %collective-permute-start = (bf16[36,2176]{1,0:T(8,128)(2,1)S(1)}, bf16[36,2176]{1,0:T(8,128)(2,1)S(1)}, u32[]{:S(2)}, u32[]{:S(2)}) collective-permute-start(bf16[36,2176]{1,0:T(8,128)(2,1)S(1)} %bitcast.49), channel_id=1, source_target_pairs={{3,0},{0,1},{1,2},{2,3},{7,4},{4,5},{5,6},{6,7},{11,8},{8,9},{9,10... | collective-permute-start | bytes 470024 | tf_op jit(solution)/shard_map/ppermute | solution.py:21
  28.5 15.3 %copy-start.3 = (bf16[1,16,32,1152]{3,2,1,0:T(8,128)(2,1)S(1)}, bf16[1,16,32,1152]{3,2,1,0:T(8,128)(2,1)}, u32[]{:S(2)}) copy-start(bf16[1,16,32,1152]{3,2,1,0:T(8,128)(2,1)} %param.9) | copy-start | bytes 3538948
  39.1 14.6 %all-to-all-start = ((f32[4,16,704]{2,1,0:T(8,128)}), f32[4,16,704]{2,1,0:T(8,128)S(1)}, u32[]{:S(2)}, u32[]{:S(2)}) async-start(f32[4,16,704]{2,1,0:T(8,128)} %reshape.128), calls=%async_computation | async-start | bytes 393216 | tf_op jit(solution)/shard_map/all_to_all | solution.py:183
  58.3 1.4 copy-start.1
  61.7 45.9 %all-to-all-start.1 = ((bf16[4,192,1152]{2,1,0:T(8,128)(2,1)}), bf16[4,192,1152]{2,1,0:T(8,128)(2,1)S(1)}, u32[]{:S(2)}, u32[]{:S(2)}) async-start(bf16[4,192,1152]{2,1,0:T(8,128)(2,1)} %shard_map.104), calls=%async_computation.1 | async-start | bytes 3538944 | tf_op jit(solution)/shard_map/all_to_all | solution.py:183
  107.8 1.3 copy-start.6
  108.5 0.6 copy-start.10
  108.5 1.5 copy-start.2
  108.9 5.6 %copy-start = (bf16[1,16,32,2176]{3,2,1,0:T(8,128)(2,1)S(1)}, bf16[1,16,32,2176]{3,2,1,0:T(8,128)(2,1)}, u32[]{:S(2)}) copy-start(bf16[1,16,32,2176]{3,2,1,0:T(8,128)(2,1)} %param.10) | copy-start | bytes 6684676
  110.6 0.6 copy-start.4
  111.2 11.7 %all-to-all-start.2 = ((bf16[4,16,704]{2,1,0:T(8,128)(2,1)}), bf16[4,16,704]{2,1,0:T(8,128)(2,1)S(1)}, u32[]{:S(2)}, u32[]{:S(2)}) async-start(bf16[4,16,704]{2,1,0:T(8,128)(2,1)} %bitcast.43), calls=%async_computation.2 | async-start | bytes 196608 | tf_op jit(solution)/shard_map/all_to_all | solution.py:183
  114.5 4.2 %copy-start.7 = (f32[64,1152]{1,0:T(8,128)S(1)}, f32[64,1152]{1,0:T(8,128)}, u32[]{:S(2)}) copy-start(f32[64,1152]{1,0:T(8,128)} %copy-done.6) | copy-start | bytes 884740
  114.6 10.5 %copy-start.5 = (f32[1,1152]{1,0:T(1,128)S(1)}, f32[1,1152]{1,0:T(1,128)}, u32[]{:S(2)}) copy-start(f32[1,1152]{1,0:T(1,128)} %multiplier_ref.1) | copy-start | bytes 13828
  125.1 14.9 %copy-start.8 = (bf16[1,16,1152]{2,1,0:T(8,128)(2,1)S(1)}, bf16[1,16,1152]{2,1,0:T(8,128)(2,1)}, u32[]{:S(2)}) copy-start(bf16[1,16,1152]{2,1,0:T(8,128)(2,1)} %param.14) | copy-start | bytes 110596
  132.7 19.3 %collective-permute-start.3 = (bf16[1,16,32,1152]{3,2,1,0:T(8,128)(2,1)S(1)}, bf16[1,16,32,1152]{3,2,1,0:T(8,128)(2,1)S(1)}, u32[]{:S(2)}, u32[]{:S(2)}) collective-permute-start(bf16[1,16,32,1152]{3,2,1,0:T(8,128)(2,1)S(1)} %bitcast.41), channel_id=1, source_target_pairs={{32,0},{64,32},{96,64},{128,96},{160,128},{192,160},{224,192},{256... | collective-permute-start | bytes 3538952 | tf_op jit(solution)/shard_map/ppermute | solution.py:21
  135.8 16.2 %all-to-all-start.3 = ((bf16[8,16,1152]{2,1,0:T(8,128)(2,1)}), bf16[8,16,1152]{2,1,0:T(8,128)(2,1)S(1)}, u32[]{:S(2)}, u32[]{:S(2)}) async-start(bf16[8,16,1152]{2,1,0:T(8,128)(2,1)} %bitcast.16), calls=%async_computation.3 | async-start | bytes 589824 | tf_op jit(solution)/shard_map/all_to_all | solution.py:325
Sparse Core Ops, SparseCore 0:
  10.1 48.1 all-gather.2
  61.0 64.0 all-gather.4

commit v7 on v6

--- a/solution.py
+++ b/solution.py
@@ -70,7 +70,10 @@
     blocks_z = sent_ref.shape[1] // images - rows // images
     block_rows = blocks.shape[0] // blocks_z
     for at in range(blocks_z):
-        text = blocks[at * block_rows : at * block_rows + images].astype(jnp.float32)
+        first = at * block_rows // 16 * 16
+        skipped = at * block_rows - first
+        last = -(-(skipped + images) // 16) * 16
+        text = blocks_ref[first : first + last].astype(jnp.float32)[skipped : skipped + images]
         inverse = lax.rsqrt(jnp.sum(text * text, axis=-1, keepdims=True) + EPSILON)
         unit = (text * inverse).astype(jnp.bfloat16)
         for peer in range(sent_ref.shape[0]):

time: 162 us -> 162 us (level)
  no operation moved by 1% of the time
where the time goes in v7:
time: 162 us; the launch traced here: 161 us
  waiting for transfers between devices  76.3 us (47%)
  starting transfers between devices  36.1 us (22%)
  between operations  16.3 us (10%)
  Pallas kernels  14.5 us (9%)
  other arithmetic  8.87 us (5%)
  local copies, waits for them, and re-layouts  6.1 us (4%)
  matrix products  2.69 us (2%)
    all_to_all x3, waiting for transfers between devices, exchange_y(): return lax.all_to_all(blocks, 'y', 0, 0)  48.2 us
    ppermute x4, starting transfers between devices, from_ahead(): lax.ppermute(array, axis, [((i + by) % peers, i) for i in range(peers)])  17.6 us
    all_to_all x3, starting transfers between devices, exchange_y(): return lax.all_to_all(blocks, 'y', 0, 0)  14.3 us
    all_to_all x1, waiting for transfers between devices, per_device(): lax.all_to_all(column_sums.reshape(z_size, images, model_width), 'z', 0, 0)  11.9 us
    ppermute x4, waiting for transfers between devices, from_ahead(): lax.ppermute(array, axis, [((i + by) % peers, i) for i in range(peers)])  9.52 us
    pallas_call x1, Pallas kernels, span(): pl.pallas_call(functools.partial(span_kernel, pieces), grid=(count // row...  7.63 us
    all_gather x1, waiting for transfers between devices, per_device(): blocks = lax.all_gather(block, 'z', axis=0, tiled=True)  4.57 us
    pallas_call x1, Pallas kernels, slopes(): pl.pallas_call(slope_kernel, grid=(tokens // block,), in_specs=[spec], ou...  4.22 us
  transfers between devices with their start and end apart: 10, of which 8 were waited for; matrix products, arithmetic and copies ran while one was open for 7% of the time, Pallas kernels for 4%

profile of v7, /device:TPU:6, one launch (start us, length us, event | category | flops | bytes accessed | tf_op | source)
XLA Modules:
  0.0 160.8 jit_solution(11051761676269911528)
XLA Ops:
  7.2 0.0 all-gather.3.cloned.1.call-start
  7.2 0.1 pad.11.clone
  7.3 1.7 %maximum_maximum_fusion = bf16[88,1152]{1,0:T(8,128)(2,1)} fusion(bf16[68,1152]{1,0:T(8,128)(2,1)} %bitcast.51, bf16[16,1152]{1,0:T(8,128)(2,1)} %bitcast.46, bf16[88]{0:T(256)(128)(2,1)S(1)} %pad.11.clone), kind=kLoop, calls=%fused_computation.31 | loop fusion | flops 608256 | bytes 396464 | tf_op jit(solution)/shard_map/concatenate | solution.py:221
  9.0 0.0 all-gather.3.cloned.1.call-update
  9.0 0.0 copy-start.9
  9.0 0.0 all-gather.5.cloned.1.call-start
  9.1 3.5 %convert_reduce_fusion = f32[16,2176]{1,0:T(8,128)S(1)} fusion(bf16[1,16,32,2176]{3,2,1,0:T(8,128)(2,1)} %param.10), kind=kLoop, calls=%fused_computation.10 | loop fusion | flops 13334528 | bytes 2367488 | tf_op jit(solution)/shard_map/reduce_sum | solution.py:234
  12.6 0.4 div.25
  13.0 0.2 pad_bitcast_fusion
  13.2 0.8 reshape.128
  14.0 7.7 %collective-permute-start.1 = (bf16[36,2176]{1,0:T(8,128)(2,1)S(1)}, bf16[36,2176]{1,0:T(8,128)(2,1)S(1)}, u32[]{:S(2)}, u32[]{:S(2)}) collective-permute-start(bf16[36,2176]{1,0:T(8,128)(2,1)S(1)} %bitcast.47), channel_id=1, source_target_pairs={{2,0},{3,1},{0,2},{1,3},{6,4},{7,5},{4,6},{5,7},{10,8},{11,9},{8,1... | collective-permute-start | bytes 470024 | tf_op jit(solution)/shard_map/ppermute | solution.py:21
  21.8 2.2 %collective-permute-start.2 = (bf16[36,2176]{1,0:T(8,128)(2,1)S(1)}, bf16[36,2176]{1,0:T(8,128)(2,1)S(1)}, u32[]{:S(2)}, u32[]{:S(2)}) collective-permute-start(bf16[36,2176]{1,0:T(8,128)(2,1)S(1)} %bitcast.48), channel_id=1, source_target_pairs={{1,0},{2,1},{3,2},{0,3},{5,4},{6,5},{7,6},{4,7},{9,8},{10,9},{11,1... | collective-permute-start | bytes 470024 | tf_op jit(solution)/shard_map/ppermute | solution.py:21
  24.0 4.5 %collective-permute-start = (bf16[36,2176]{1,0:T(8,128)(2,1)S(1)}, bf16[36,2176]{1,0:T(8,128)(2,1)S(1)}, u32[]{:S(2)}, u32[]{:S(2)}) collective-permute-start(bf16[36,2176]{1,0:T(8,128)(2,1)S(1)} %bitcast.49), channel_id=1, source_target_pairs={{3,0},{0,1},{1,2},{2,3},{7,4},{4,5},{5,6},{6,7},{11,8},{8,9},{9,10... | collective-permute-start | bytes 470024 | tf_op jit(solution)/shard_map/ppermute | solution.py:21
  28.5 0.0 copy-start.3
  28.5 0.1 collective-permute-done.1
  28.6 9.4 %collective-permute-done.2 = bf16[36,2176]{1,0:T(8,128)(2,1)S(1)} collective-permute-done((bf16[36,2176]{1,0:T(8,128)(2,1)S(1)}, bf16[36,2176]{1,0:T(8,128)(2,1)S(1)}, u32[]{:S(2)}, u32[]{:S(2)}) %collective-permute-start.2) | collective-permute-done | bytes 156704 | tf_op jit(solution)/shard_map/ppermute | solution.py:21
  38.0 0.0 collective-permute-done
  38.1 0.1 select_select_fusion.3
  38.1 0.9 pad_maximum_fusion
  39.1 0.0 all-gather.5.cloned.1.call-update
  39.1 4.5 %all-to-all-start = ((f32[4,16,704]{2,1,0:T(8,128)}), f32[4,16,704]{2,1,0:T(8,128)S(1)}, u32[]{:S(2)}, u32[]{:S(2)}) async-start(f32[4,16,704]{2,1,0:T(8,128)} %reshape.128), calls=%async_computation | async-start | bytes 393216 | tf_op jit(solution)/shard_map/all_to_all | solution.py:186
  43.7 0.1 broadcast_in_dim.54
  43.7 0.1 broadcast_in_dim.55
  43.8 0.3 convert_reduce_fusion.1
  44.1 0.1 bitcast_select_fusion.own_ref
  44.2 9.5 %all-to-all-done = f32[4,16,704]{2,1,0:T(8,128)S(1)} async-done(((f32[4,16,704]{2,1,0:T(8,128)}), f32[4,16,704]{2,1,0:T(8,128)S(1)}, u32[]{:S(2)}, u32[]{:S(2)}) %all-to-all-start) | async-done | bytes 180256 | tf_op jit(solution)/shard_map/all_to_all | solution.py:186
  53.7 4.6 %all-gather.3.cloned.1.call-done.blocks_ref = bf16[704,1152]{1,0:T(8,128)(2,1)} async-done(((bf16[88,1152]{1,0:T(8,128)(2,1)}), bf16[704,1152]{1,0:T(8,128)(2,1)}) %all-gather.3.cloned.1.call-update) | async-done | bytes 1622032 | tf_op jit(solution)/shard_map/all_gather | solution.py:229
  58.3 1.4 copy-done.1
  59.7 2.0 %shard_map.104 = bf16[4,192,1152]{2,1,0:T(8,128)(2,1)} custom-call(f32[64,704]{1,0:T(8,128)S(1)} %bitcast.42, bf16[704,1152]{1,0:T(8,128)(2,1)S(1)} %copy-done.1, f32[64,1152]{1,0:T(8,128)S(1)} %bitcast_select_fusion.own_ref), custom_call_target="tpu_custom_call" | custom-call | flops 207618048 | bytes 2000000 | tf_op jit(solution)/shard_map/pallas_call | solution.py:93
  61.7 6.5 %all-to-all-start.1 = ((bf16[4,192,1152]{2,1,0:T(8,128)(2,1)}), bf16[4,192,1152]{2,1,0:T(8,128)(2,1)S(1)}, u32[]{:S(2)}, u32[]{:S(2)}) async-start(bf16[4,192,1152]{2,1,0:T(8,128)(2,1)} %shard_map.104), calls=%async_computation.1 | async-start | bytes 3538944 | tf_op jit(solution)/shard_map/all_to_all | solution.py:186
  69.5 0.1 iota_add_fusion
  69.6 0.1 add.112
  70.3 0.1 iota_add_fusion.1
  70.4 0.1 add.107
  70.5 37.1 %all-to-all-done.1 = bf16[4,192,1152]{2,1,0:T(8,128)(2,1)S(1)} async-done(((bf16[4,192,1152]{2,1,0:T(8,128)(2,1)}), bf16[4,192,1152]{2,1,0:T(8,128)(2,1)S(1)}, u32[]{:S(2)}, u32[]{:S(2)}) %all-to-all-start.1) | async-done | bytes 1769504 | tf_op jit(solution)/shard_map/all_to_all | solution.py:186
  107.6 0.1 slice.9
  107.7 0.1 convert_reduce_fusion.2
  107.8 0.1 multiply_reduce_fusion.1
  107.9 0.5 fusion.13
  108.5 0.4 multiply_reduce_fusion
  108.9 0.0 copy-start
  108.9 0.2 copy-done.10
  109.1 0.8 fusion.21
  110.0 0.0 copy-done.2
  110.0 0.6 shard_map.105
  110.6 0.0 copy-start.4
  110.6 0.6 copy-done.4
  111.2 3.3 %all-to-all-start.2 = ((bf16[4,16,704]{2,1,0:T(8,128)(2,1)}), bf16[4,16,704]{2,1,0:T(8,128)(2,1)S(1)}, u32[]{:S(2)}, u32[]{:S(2)}) async-start(bf16[4,16,704]{2,1,0:T(8,128)(2,1)} %bitcast.43), calls=%async_computation.2 | async-start | bytes 196608 | tf_op jit(solution)/shard_map/all_to_all | solution.py:186
  114.6 0.0 copy-start.5
  114.6 4.2 %shard_map.106.slope_ref = f32[512,2176]{1,0:T(8,128)} custom-call(bf16[512,2176]{1,0:T(8,128)(2,1)S(1)} %bitcast.39), custom_call_target="tpu_custom_call" | custom-call | flops 22282240 | bytes 6684672 | tf_op jit(solution)/shard_map/pallas_call | solution.py:111
  118.8 0.0 copy-done.7
  118.8 1.7 %convolution_convert_fusion = bf16[128,1152]{1,0:T(8,128)(2,1)} fusion(bf16[64,512]{1,0:T(8,128)(2,1)} %copy-done.10, s32[]{:T(128)S(6)} %select_n.89, f32[64,1152]{1,0:T(8,128)S(1)} %copy-done.7, f32[64]{0:T(128)S(1)} %add_rsqrt_fusion.1), kind=kOutput, calls=%fused_computation.11 | convolution fusion | flops 19169280 | bytes 606468 | tf_op jit(solution)/shard_map/dot_general | solution.py:300
  120.5 0.9 dynamic-slice_bitcast_fusion.share_ref
  121.4 1.6 all-to-all-done.2.grad_ref
  123.0 2.1 %all-gather.5.cloned.1.call-done.up_ref = bf16[1152,2176]{1,0:T(8,128)(2,1)} async-done(((bf16[144,2176]{1,0:T(8,128)(2,1)}), bf16[1152,2176]{1,0:T(8,128)(2,1)}) %all-gather.5.cloned.1.call-update) | async-done | bytes 5013520 | tf_op jit(solution)/shard_map/all_gather | solution.py:250
  125.1 7.6 %shard_map.107 = bf16[512,1152]{1,0:T(8,128)(2,1)S(1)} custom-call(bf16[4,16,704]{2,1,0:T(8,128)(2,1)S(1)} %all-to-all-done.2.grad_ref, f32[512,2176]{1,0:T(8,128)} %shard_map.106.slope_ref, bf16[1152,2176]{1,0:T(8,128)(2,1)} %all-gather.5.cloned.1.call-done.up_ref, bf16[512,1152]{1,0:T(8,128)(2,1)S(1)} %bitcast.40, ...), custom_call_target="tpu_custom_call" | custom-call | flops 2566914048 | bytes 11829248 | tf_op jit(solution)/shard_map/pallas_call | solution.py:162
  132.7 3.1 %collective-permute-start.3 = (bf16[1,16,32,1152]{3,2,1,0:T(8,128)(2,1)S(1)}, bf16[1,16,32,1152]{3,2,1,0:T(8,128)(2,1)S(1)}, u32[]{:S(2)}, u32[]{:S(2)}) collective-permute-start(bf16[1,16,32,1152]{3,2,1,0:T(8,128)(2,1)S(1)} %bitcast.41), channel_id=1, source_target_pairs={{32,0},{64,32},{96,64},{128,96},{160,128},{192,160},{224,192},{256... | collective-permute-start | bytes 3538952 | tf_op jit(solution)/shard_map/ppermute | solution.py:21
  135.8 4.2 %all-to-all-start.3 = ((bf16[8,16,1152]{2,1,0:T(8,128)(2,1)}), bf16[8,16,1152]{2,1,0:T(8,128)(2,1)S(1)}, u32[]{:S(2)}, u32[]{:S(2)}) async-start(bf16[8,16,1152]{2,1,0:T(8,128)(2,1)} %bitcast.16), calls=%async_computation.3 | async-start | bytes 589824 | tf_op jit(solution)/shard_map/all_to_all | solution.py:328
  140.0 0.1 fusion.14
  140.1 11.9 %all-to-all-done.3 = bf16[8,16,1152]{2,1,0:T(8,128)(2,1)S(1)} async-done(((bf16[8,16,1152]{2,1,0:T(8,128)(2,1)}), bf16[8,16,1152]{2,1,0:T(8,128)(2,1)S(1)}, u32[]{:S(2)}, u32[]{:S(2)}) %all-to-all-start.3) | async-done | bytes 294944 | tf_op jit(solution)/shard_map/all_to_all | solution.py:328
  152.0 0.0 collective-permute-done.3
  152.1 0.2 fusion.16
  152.3 0.7 fusion.18
  153.0 1.0 copy.16
  (23 shorter events, 0.1 us)
Async XLA Ops:
  7.2 51.1 %all-gather.3.cloned.1.call-start = ((), (), s32[]{:S(2)}) async-start(), calls=%async_computation.4 | async-start | bytes 1824768 | tf_op jit(solution)/shard_map/all_gather | solution.py:229
  9.0 5.0 %copy-start.9 = (bf16[1,36,2176]{2,1,0:T(8,128)(2,1)S(1)}, bf16[1,36,2176]{2,1,0:T(8,128)(2,1)}, u32[]{:S(2)}) copy-start(bf16[1,36,2176]{2,1,0:T(8,128)(2,1)} %param.12) | copy-start | bytes 470020
  9.0 116.0 %all-gather.5.cloned.1.call-start = ((), (), s32[]{:S(2)}) async-start(), calls=%async_computation.5 | async-start | bytes 5640192 | tf_op jit(solution)/shard_map/all_gather | solution.py:250
  14.0 14.6 %collective-permute-start.1 = (bf16[36,2176]{1,0:T(8,128)(2,1)S(1)}, bf16[36,2176]{1,0:T(8,128)(2,1)S(1)}, u32[]{:S(2)}, u32[]{:S(2)}) collective-permute-start(bf16[36,2176]{1,0:T(8,128)(2,1)S(1)} %bitcast.47), channel_id=1, source_target_pairs={{2,0},{3,1},{0,2},{1,3},{6,4},{7,5},{4,6},{5,7},{10,8},{11,9},{8,1... | collective-permute-start | bytes 470024 | tf_op jit(solution)/shard_map/ppermute | solution.py:21
  21.8 16.3 %collective-permute-start.2 = (bf16[36,2176]{1,0:T(8,128)(2,1)S(1)}, bf16[36,2176]{1,0:T(8,128)(2,1)S(1)}, u32[]{:S(2)}, u32[]{:S(2)}) collective-permute-start(bf16[36,2176]{1,0:T(8,128)(2,1)S(1)} %bitcast.48), channel_id=1, source_target_pairs={{1,0},{2,1},{3,2},{0,3},{5,4},{6,5},{7,6},{4,7},{9,8},{10,9},{11,1... | collective-permute-start | bytes 470024 | tf_op jit(solution)/shard_map/ppermute | solution.py:21
  24.0 14.0 %collective-permute-start = (bf16[36,2176]{1,0:T(8,128)(2,1)S(1)}, bf16[36,2176]{1,0:T(8,128)(2,1)S(1)}, u32[]{:S(2)}, u32[]{:S(2)}) collective-permute-start(bf16[36,2176]{1,0:T(8,128)(2,1)S(1)} %bitcast.49), channel_id=1, source_target_pairs={{3,0},{0,1},{1,2},{2,3},{7,4},{4,5},{5,6},{6,7},{11,8},{8,9},{9,10... | collective-permute-start | bytes 470024 | tf_op jit(solution)/shard_map/ppermute | solution.py:21
  28.5 15.3 %copy-start.3 = (bf16[1,16,32,1152]{3,2,1,0:T(8,128)(2,1)S(1)}, bf16[1,16,32,1152]{3,2,1,0:T(8,128)(2,1)}, u32[]{:S(2)}) copy-start(bf16[1,16,32,1152]{3,2,1,0:T(8,128)(2,1)} %param.9) | copy-start | bytes 3538948
  39.1 14.6 %all-to-all-start = ((f32[4,16,704]{2,1,0:T(8,128)}), f32[4,16,704]{2,1,0:T(8,128)S(1)}, u32[]{:S(2)}, u32[]{:S(2)}) async-start(f32[4,16,704]{2,1,0:T(8,128)} %reshape.128), calls=%async_computation | async-start | bytes 393216 | tf_op jit(solution)/shard_map/all_to_all | solution.py:186
  58.3 1.4 copy-start.1
  61.7 45.9 %all-to-all-start.1 = ((bf16[4,192,1152]{2,1,0:T(8,128)(2,1)}), bf16[4,192,1152]{2,1,0:T(8,128)(2,1)S(1)}, u32[]{:S(2)}, u32[]{:S(2)}) async-start(bf16[4,192,1152]{2,1,0:T(8,128)(2,1)} %shard_map.104), calls=%async_computation.1 | async-start | bytes 3538944 | tf_op jit(solution)/shard_map/all_to_all | solution.py:186
  107.8 1.3 copy-start.6
  108.5 0.6 copy-start.10
  108.5 1.5 copy-start.2
  108.9 5.6 %copy-start = (bf16[1,16,32,2176]{3,2,1,0:T(8,128)(2,1)S(1)}, bf16[1,16,32,2176]{3,2,1,0:T(8,128)(2,1)}, u32[]{:S(2)}) copy-start(bf16[1,16,32,2176]{3,2,1,0:T(8,128)(2,1)} %param.10) | copy-start | bytes 6684676
  110.6 0.6 copy-start.4
  111.2 11.7 %all-to-all-start.2 = ((bf16[4,16,704]{2,1,0:T(8,128)(2,1)}), bf16[4,16,704]{2,1,0:T(8,128)(2,1)S(1)}, u32[]{:S(2)}, u32[]{:S(2)}) async-start(bf16[4,16,704]{2,1,0:T(8,128)(2,1)} %bitcast.43), calls=%async_computation.2 | async-start | bytes 196608 | tf_op jit(solution)/shard_map/all_to_all | solution.py:186
  114.5 4.2 %copy-start.7 = (f32[64,1152]{1,0:T(8,128)S(1)}, f32[64,1152]{1,0:T(8,128)}, u32[]{:S(2)}) copy-start(f32[64,1152]{1,0:T(8,128)} %copy-done.6) | copy-start | bytes 884740
  114.6 10.5 %copy-start.5 = (f32[1,1152]{1,0:T(1,128)S(1)}, f32[1,1152]{1,0:T(1,128)}, u32[]{:S(2)}) copy-start(f32[1,1152]{1,0:T(1,128)} %multiplier_ref.1) | copy-start | bytes 13828
  125.1 14.9 %copy-start.8 = (bf16[1,16,1152]{2,1,0:T(8,128)(2,1)S(1)}, bf16[1,16,1152]{2,1,0:T(8,128)(2,1)}, u32[]{:S(2)}) copy-start(bf16[1,16,1152]{2,1,0:T(8,128)(2,1)} %param.14) | copy-start | bytes 110596
  132.7 19.3 %collective-permute-start.3 = (bf16[1,16,32,1152]{3,2,1,0:T(8,128)(2,1)S(1)}, bf16[1,16,32,1152]{3,2,1,0:T(8,128)(2,1)S(1)}, u32[]{:S(2)}, u32[]{:S(2)}) collective-permute-start(bf16[1,16,32,1152]{3,2,1,0:T(8,128)(2,1)S(1)} %bitcast.41), channel_id=1, source_target_pairs={{32,0},{64,32},{96,64},{128,96},{160,128},{192,160},{224,192},{256... | collective-permute-start | bytes 3538952 | tf_op jit(solution)/shard_map/ppermute | solution.py:21
  135.8 16.2 %all-to-all-start.3 = ((bf16[8,16,1152]{2,1,0:T(8,128)(2,1)}), bf16[8,16,1152]{2,1,0:T(8,128)(2,1)S(1)}, u32[]{:S(2)}, u32[]{:S(2)}) async-start(bf16[8,16,1152]{2,1,0:T(8,128)(2,1)} %bitcast.16), calls=%async_computation.3 | async-start | bytes 589824 | tf_op jit(solution)/shard_map/all_to_all | solution.py:328
Sparse Core Ops, SparseCore 0:
  10.1 48.1 all-gather.2
  61.0 64.0 all-gather.4

commit v8 on v7

--- a/solution.py
+++ b/solution.py
@@ -121,49 +121,69 @@
     )(preact)
 
 
-def span_kernel(
-    pieces, grad_ref, slope_ref, up_ref, tokens_ref, share_ref, multiplier_ref, span_ref, hidden_ref
-):
-    @pl.when(pl.program_id(0) == 0)
+def preact_kernel(pieces, grad_ref, slope_ref, preact_grad_ref, hidden_ref):
+    step = pl.program_id(0)
+
+    @pl.when(step == 0)
     def _():
         hidden_ref[...] = jnp.concatenate(
             [grad_ref[y, :, start:end].astype(jnp.float32) for y, start, end in pieces], axis=1
         ).reshape(hidden_ref.shape)
 
-    step = pl.program_id(0)
+    rows = preact_grad_ref.shape[0]
+    _, count, hidden = hidden_ref.shape
+    slope = slope_ref[...].reshape(count, rows // count, hidden)
+    preact_grad_ref[...] = (
+        (hidden_ref[step][:, None, :] * slope).astype(jnp.bfloat16).reshape(rows, hidden)
+    )
+
+
+def preact_grads(received, pieces, slope, images):
+    count, hidden = slope.shape
+    rows = IMAGE_BLOCK * (count // images)
+    block = pl.BlockSpec((rows, hidden), lambda i: (i, 0))
+    return pl.pallas_call(
+        functools.partial(preact_kernel, pieces),
+        grid=(count // rows,),
+        in_specs=[pl.BlockSpec(received.shape, lambda i: (0, 0, 0)), block],
+        out_specs=block,
+        out_shape=jax.ShapeDtypeStruct((count, hidden), jnp.bfloat16),
+        scratch_shapes=[pltpu.VMEM((images // IMAGE_BLOCK, IMAGE_BLOCK, hidden), jnp.float32)],
+        compiler_params=pltpu.CompilerParams(vmem_limit_bytes=VMEM_BYTES),
+        cost_estimate=pl.CostEstimate(
+            flops=2 * count * hidden, bytes_accessed=6 * count * hidden, transcendentals=0
+        ),
+    )(received, slope)
+
+
+def span_kernel(grads_ref, up_ref, tokens_ref, share_ref, multiplier_ref, span_ref):
     tokens = tokens_ref[...].astype(jnp.float32)
     rows, width = tokens.shape
-    count = IMAGE_BLOCK
-    patches = rows // count
-    hidden = hidden_ref.shape[2]
-    grads = hidden_ref[step]
-    slope = slope_ref[...].reshape(count, patches, hidden)
-    preact_grad = (grads[:, None, :] * slope).astype(jnp.bfloat16).reshape(rows, hidden)
+    patches = rows // IMAGE_BLOCK
     normed = lax.dot_general(
-        preact_grad, up_ref[...], (((1,), (1,)), ((), ())), preferred_element_type=jnp.float32
+        grads_ref[...], up_ref[...], (((1,), (1,)), ((), ())), preferred_element_type=jnp.float32
     )
     inner = norm_backward(tokens, normed, multiplier_ref[...])
-    share = share_ref[step]
+    share = share_ref[pl.program_id(0)]
     span_ref[...] = (
-        (share[:, None, :] + inner.reshape(count, patches, width))
+        (share[:, None, :] + inner.reshape(IMAGE_BLOCK, patches, width))
         .astype(jnp.bfloat16)
         .reshape(rows, width)
     )
 
 
-def span(received, pieces, slope, up_whole, tokens, share, multiplier):
+def span(preact_grad, up_whole, tokens, share, multiplier):
     count, width = tokens.shape
     images = share.shape[0]
     share = share.reshape(images // IMAGE_BLOCK, IMAGE_BLOCK, width)
-    hidden = slope.shape[1]
+    hidden = preact_grad.shape[1]
     rows = IMAGE_BLOCK * (count // images)
     whole = lambda array: pl.BlockSpec(array.shape, lambda i: (0,) * array.ndim)
     block = lambda columns: pl.BlockSpec((rows, columns), lambda i: (i, 0))
     return pl.pallas_call(
-        functools.partial(span_kernel, pieces),
+        span_kernel,
         grid=(count // rows,),
         in_specs=[
-            whole(received),
             block(hidden),
             whole(up_whole),
             block(width),
@@ -172,14 +192,13 @@
         ],
         out_specs=block(width),
         out_shape=jax.ShapeDtypeStruct((count, width), jnp.bfloat16),
-        scratch_shapes=[pltpu.VMEM((images // IMAGE_BLOCK, IMAGE_BLOCK, hidden), jnp.float32)],
         compiler_params=pltpu.CompilerParams(vmem_limit_bytes=VMEM_BYTES),
         cost_estimate=pl.CostEstimate(
             flops=2 * count * hidden * width,
-            bytes_accessed=4 * count * hidden + 2 * hidden * width + 4 * count * width,
+            bytes_accessed=2 * count * hidden + 2 * hidden * width + 4 * count * width,
             transcendentals=0,
         ),
-    )(received, slope, up_whole, tokens, share, multiplier)
+    )(preact_grad, up_whole, tokens, share, multiplier)
 
 
 def exchange_y(blocks):
@@ -313,9 +332,7 @@
         for own in range(Y_SHARDS)
     ]
     span_grad = span(
-        received,
-        pieces,
-        slope,
+        preact_grads(received, pieces, slope, images),
         up_whole,
         feedforward_entry_states.reshape(images * patches, model_width),
         share,

time: 162 us -> 164 us (1.012)
  Pallas kernels: 14.5 us -> 17.1 us
    all_gather x1, waiting for transfers between devices: 2.08 us -> 0.01 us  [per_device(): up_whole = lax.all_gather(up_y, 'z', axis=0, tiled=True)]
    pallas_call x1 -> x2, Pallas kernels: 7.63 us -> 9.59 us  [the longest x1 7.12 us: span(): pl.pallas_call(span_kernel, grid=(count // rows,), in_specs=[block(hidden...]
  transfers between devices with their start and end apart: 10 -> 10, of which waited for: 8 -> 7; matrix products, arithmetic and copies ran while one was open for 7% -> 7% of each run, Pallas kernels for 4% -> 6%
where the time goes in v8:
time: 164 us; the launch traced here: 162 us
  waiting for transfers between devices  75.4 us (46%)
  starting transfers between devices  35.3 us (22%)
  Pallas kernels  17.1 us (10%)
  between operations  16.3 us (10%)
  other arithmetic  8.87 us (5%)
  local copies, waits for them, and re-layouts  6.87 us (4%)
  matrix products  2.69 us (2%)
    all_to_all x3, waiting for transfers between devices, exchange_y(): return lax.all_to_all(blocks, 'y', 0, 0)  48.2 us
    ppermute x4, starting transfers between devices, from_ahead(): lax.ppermute(array, axis, [((i + by) % peers, i) for i in range(peers)])  16.4 us
    all_to_all x3, starting transfers between devices, exchange_y(): return lax.all_to_all(blocks, 'y', 0, 0)  14.3 us
    all_to_all x1, waiting for transfers between devices, per_device(): lax.all_to_all(column_sums.reshape(z_size, images, model_width), 'z', 0, 0)  13.1 us
    ppermute x4, waiting for transfers between devices, from_ahead(): lax.ppermute(array, axis, [((i + by) % peers, i) for i in range(peers)])  9.52 us
    pallas_call x1, Pallas kernels, span(): pl.pallas_call(span_kernel, grid=(count // rows,), in_specs=[block(hidden...  7.12 us
    all_gather x1, waiting for transfers between devices, per_device(): blocks = lax.all_gather(block, 'z', axis=0, tiled=True)  4.57 us
    all_to_all x1, starting transfers between devices, per_device(): lax.all_to_all(column_sums.reshape(z_size, images, model_width), 'z', 0, 0)  4.51 us
  transfers between devices with their start and end apart: 10, of which 7 were waited for; matrix products, arithmetic and copies ran while one was open for 7% of the time, Pallas kernels for 6%

profile of v8, /device:TPU:6, one launch (start us, length us, event | category | flops | bytes accessed | tf_op | source)
XLA Modules:
  0.0 162.5 jit_solution(321371336540217417)
XLA Ops:
  7.2 0.0 all-gather.3.cloned.1.call-start
  7.2 0.1 pad.11.clone
  7.3 1.7 %maximum_maximum_fusion = bf16[88,1152]{1,0:T(8,128)(2,1)} fusion(bf16[68,1152]{1,0:T(8,128)(2,1)} %bitcast.50, bf16[16,1152]{1,0:T(8,128)(2,1)} %bitcast.45, bf16[88]{0:T(256)(128)(2,1)S(1)} %pad.11.clone), kind=kLoop, calls=%fused_computation.31 | loop fusion | flops 608256 | bytes 396464 | tf_op jit(solution)/shard_map/concatenate | solution.py:240
  9.0 0.0 all-gather.3.cloned.1.call-update
  9.0 0.0 copy-start.9
  9.0 0.0 all-gather.5.cloned.1.call-start
  9.1 3.5 %convert_reduce_fusion = f32[16,2176]{1,0:T(8,128)S(1)} fusion(bf16[1,16,32,2176]{3,2,1,0:T(8,128)(2,1)} %param.10), kind=kLoop, calls=%fused_computation.10 | loop fusion | flops 13334528 | bytes 2367488 | tf_op jit(solution)/shard_map/reduce_sum | solution.py:253
  12.6 0.4 div.25
  13.0 0.2 pad_bitcast_fusion
  13.2 0.8 reshape.128
  14.0 0.0 copy-done.9
  14.0 7.7 %collective-permute-start.1 = (bf16[36,2176]{1,0:T(8,128)(2,1)S(1)}, bf16[36,2176]{1,0:T(8,128)(2,1)S(1)}, u32[]{:S(2)}, u32[]{:S(2)}) collective-permute-start(bf16[36,2176]{1,0:T(8,128)(2,1)S(1)} %bitcast.46), channel_id=1, source_target_pairs={{2,0},{3,1},{0,2},{1,3},{6,4},{7,5},{4,6},{5,7},{10,8},{11,9},{8,1... | collective-permute-start | bytes 470024 | tf_op jit(solution)/shard_map/ppermute | solution.py:21
  21.8 2.2 %collective-permute-start.2 = (bf16[36,2176]{1,0:T(8,128)(2,1)S(1)}, bf16[36,2176]{1,0:T(8,128)(2,1)S(1)}, u32[]{:S(2)}, u32[]{:S(2)}) collective-permute-start(bf16[36,2176]{1,0:T(8,128)(2,1)S(1)} %bitcast.47), channel_id=1, source_target_pairs={{1,0},{2,1},{3,2},{0,3},{5,4},{6,5},{7,6},{4,7},{9,8},{10,9},{11,1... | collective-permute-start | bytes 470024 | tf_op jit(solution)/shard_map/ppermute | solution.py:21
  24.0 4.5 %collective-permute-start = (bf16[36,2176]{1,0:T(8,128)(2,1)S(1)}, bf16[36,2176]{1,0:T(8,128)(2,1)S(1)}, u32[]{:S(2)}, u32[]{:S(2)}) collective-permute-start(bf16[36,2176]{1,0:T(8,128)(2,1)S(1)} %bitcast.48), channel_id=1, source_target_pairs={{3,0},{0,1},{1,2},{2,3},{7,4},{4,5},{5,6},{6,7},{11,8},{8,9},{9,10... | collective-permute-start | bytes 470024 | tf_op jit(solution)/shard_map/ppermute | solution.py:21
  28.5 0.0 copy-start.4
  28.5 0.1 collective-permute-done.1
  28.6 9.4 %collective-permute-done.2 = bf16[36,2176]{1,0:T(8,128)(2,1)S(1)} collective-permute-done((bf16[36,2176]{1,0:T(8,128)(2,1)S(1)}, bf16[36,2176]{1,0:T(8,128)(2,1)S(1)}, u32[]{:S(2)}, u32[]{:S(2)}) %collective-permute-start.2) | collective-permute-done | bytes 156704 | tf_op jit(solution)/shard_map/ppermute | solution.py:21
  38.0 0.0 collective-permute-done
  38.1 0.1 select_select_fusion.3
  38.1 0.9 pad_maximum_fusion
  39.1 0.0 all-gather.5.cloned.1.call-update
  39.1 4.5 %all-to-all-start = ((f32[4,16,704]{2,1,0:T(8,128)}), f32[4,16,704]{2,1,0:T(8,128)S(1)}, u32[]{:S(2)}, u32[]{:S(2)}) async-start(f32[4,16,704]{2,1,0:T(8,128)} %reshape.128), calls=%async_computation | async-start | bytes 393216 | tf_op jit(solution)/shard_map/all_to_all | solution.py:205
  43.7 0.1 broadcast_in_dim.54
  43.7 0.1 broadcast_in_dim.55
  43.8 0.0 copy-done.4
  43.8 0.3 convert_reduce_fusion.1
  44.1 0.1 bitcast_select_fusion.own_ref
  44.2 9.5 %all-to-all-done = f32[4,16,704]{2,1,0:T(8,128)S(1)} async-done(((f32[4,16,704]{2,1,0:T(8,128)}), f32[4,16,704]{2,1,0:T(8,128)S(1)}, u32[]{:S(2)}, u32[]{:S(2)}) %all-to-all-start) | async-done | bytes 180256 | tf_op jit(solution)/shard_map/all_to_all | solution.py:205
  53.7 4.6 %all-gather.3.cloned.1.call-done.blocks_ref = bf16[704,1152]{1,0:T(8,128)(2,1)} async-done(((bf16[88,1152]{1,0:T(8,128)(2,1)}), bf16[704,1152]{1,0:T(8,128)(2,1)}) %all-gather.3.cloned.1.call-update) | async-done | bytes 1622032 | tf_op jit(solution)/shard_map/all_gather | solution.py:248
  58.3 1.4 copy-done.2
  59.7 2.0 %shard_map.104 = bf16[4,192,1152]{2,1,0:T(8,128)(2,1)} custom-call(f32[64,704]{1,0:T(8,128)S(1)} %bitcast.42, bf16[704,1152]{1,0:T(8,128)(2,1)S(1)} %copy-done.2, f32[64,1152]{1,0:T(8,128)S(1)} %bitcast_select_fusion.own_ref), custom_call_target="tpu_custom_call" | custom-call | flops 207618048 | bytes 2000000 | tf_op jit(solution)/shard_map/pallas_call | solution.py:93
  61.7 6.5 %all-to-all-start.1 = ((bf16[4,192,1152]{2,1,0:T(8,128)(2,1)}), bf16[4,192,1152]{2,1,0:T(8,128)(2,1)S(1)}, u32[]{:S(2)}, u32[]{:S(2)}) async-start(bf16[4,192,1152]{2,1,0:T(8,128)(2,1)} %shard_map.104), calls=%async_computation.1 | async-start | bytes 3538944 | tf_op jit(solution)/shard_map/all_to_all | solution.py:205
  69.5 0.1 iota_add_fusion
  69.6 0.1 add.112
  70.3 0.1 iota_add_fusion.1
  70.4 0.1 add.107
  70.5 37.1 %all-to-all-done.1 = bf16[4,192,1152]{2,1,0:T(8,128)(2,1)S(1)} async-done(((bf16[4,192,1152]{2,1,0:T(8,128)(2,1)}), bf16[4,192,1152]{2,1,0:T(8,128)(2,1)S(1)}, u32[]{:S(2)}, u32[]{:S(2)}) %all-to-all-start.1) | async-done | bytes 1769504 | tf_op jit(solution)/shard_map/all_to_all | solution.py:205
  107.6 0.1 slice.9
  107.7 0.1 convert_reduce_fusion.2
  107.8 0.0 copy-start.6
  107.8 0.1 multiply_reduce_fusion.1
  107.9 0.5 fusion.13
  108.5 0.4 multiply_reduce_fusion
  108.9 0.0 copy-start
  109.0 0.8 fusion.21
  109.8 0.2 copy-done.3
  110.0 1.2 shard_map.105
  111.2 3.3 %all-to-all-start.2 = ((bf16[4,16,704]{2,1,0:T(8,128)(2,1)}), bf16[4,16,704]{2,1,0:T(8,128)(2,1)S(1)}, u32[]{:S(2)}, u32[]{:S(2)}) async-start(bf16[4,16,704]{2,1,0:T(8,128)(2,1)} %bitcast.11), calls=%async_computation.2 | async-start | bytes 196608 | tf_op jit(solution)/shard_map/all_to_all | solution.py:205
  114.6 4.2 %shard_map.106.slope_ref = f32[512,2176]{1,0:T(8,128)} custom-call(bf16[512,2176]{1,0:T(8,128)(2,1)S(1)} %bitcast.39), custom_call_target="tpu_custom_call" | custom-call | flops 22282240 | bytes 6684672 | tf_op jit(solution)/shard_map/pallas_call | solution.py:111
  118.8 1.7 %convolution_convert_fusion = bf16[128,1152]{1,0:T(8,128)(2,1)} fusion(bf16[64,512]{1,0:T(8,128)(2,1)} %copy-done.10, s32[]{:T(128)S(6)} %select_n.89, f32[64,1152]{1,0:T(8,128)S(1)} %copy-done.7, f32[64]{0:T(128)S(1)} %add_rsqrt_fusion.1), kind=kOutput, calls=%fused_computation.11 | convolution fusion | flops 19169280 | bytes 606468 | tf_op jit(solution)/shard_map/dot_general | solution.py:319
  120.5 0.9 dynamic-slice_bitcast_fusion.share_ref
  121.4 1.6 all-to-all-done.2.grad_ref
  123.0 2.5 %shard_map.107.grads_ref = bf16[512,2176]{1,0:T(8,128)(2,1)S(1)} custom-call(bf16[4,16,704]{2,1,0:T(8,128)(2,1)S(1)} %all-to-all-done.2.grad_ref, f32[512,2176]{1,0:T(8,128)} %shard_map.106.slope_ref), custom_call_target="tpu_custom_call" | custom-call | flops 2228224 | bytes 6684672 | tf_op jit(solution)/shard_map/pallas_call | solution.py:145
  125.5 1.4 copy-done.1
  126.9 0.0 copy-done.5
  126.9 7.1 %shard_map.108 = bf16[512,1152]{1,0:T(8,128)(2,1)S(1)} custom-call(bf16[512,2176]{1,0:T(8,128)(2,1)} %copy-done.1, bf16[1152,2176]{1,0:T(8,128)(2,1)} %all-gather.5.cloned.1.call-done.up_ref, bf16[512,1152]{1,0:T(8,128)(2,1)S(1)} %bitcast.40, f32[2,8,1152]{2,1,0:T(8,128)S(1)} %dynamic-slice_bitcast_fusion.share_ref, f32[1,1152]{1,0:T(1,128)S(1)} %copy-done.5), custom_call_target="tpu_custom_call" | custom-call | flops 2566914048 | bytes 9601024 | tf_op jit(solution)/shard_map/pallas_call | solution.py:183
  134.0 1.9 %collective-permute-start.3 = (bf16[1,16,32,1152]{3,2,1,0:T(8,128)(2,1)S(1)}, bf16[1,16,32,1152]{3,2,1,0:T(8,128)(2,1)S(1)}, u32[]{:S(2)}, u32[]{:S(2)}) collective-permute-start(bf16[1,16,32,1152]{3,2,1,0:T(8,128)(2,1)S(1)} %bitcast.41), channel_id=1, source_target_pairs={{32,0},{64,32},{96,64},{128,96},{160,128},{192,160},{224,192},{256... | collective-permute-start | bytes 3538952 | tf_op jit(solution)/shard_map/ppermute | solution.py:21
  135.9 4.5 %all-to-all-start.3 = ((bf16[8,16,1152]{2,1,0:T(8,128)(2,1)}), bf16[8,16,1152]{2,1,0:T(8,128)(2,1)S(1)}, u32[]{:S(2)}, u32[]{:S(2)}) async-start(bf16[8,16,1152]{2,1,0:T(8,128)(2,1)} %bitcast.16), calls=%async_computation.3 | async-start | bytes 589824 | tf_op jit(solution)/shard_map/all_to_all | solution.py:345
  140.4 0.1 fusion.14
  140.6 13.1 %all-to-all-done.3 = bf16[8,16,1152]{2,1,0:T(8,128)(2,1)S(1)} async-done(((bf16[8,16,1152]{2,1,0:T(8,128)(2,1)}), bf16[8,16,1152]{2,1,0:T(8,128)(2,1)S(1)}, u32[]{:S(2)}, u32[]{:S(2)}) %all-to-all-start.3) | async-done | bytes 294944 | tf_op jit(solution)/shard_map/all_to_all | solution.py:345
  153.7 0.0 collective-permute-done.3
  153.7 0.2 fusion.16
  153.9 0.7 fusion.18
  154.6 1.0 copy.16
  (24 shorter events, 0.1 us)
Async XLA Ops:
  7.2 51.1 %all-gather.3.cloned.1.call-start = ((), (), s32[]{:S(2)}) async-start(), calls=%async_computation.4 | async-start | bytes 1824768 | tf_op jit(solution)/shard_map/all_gather | solution.py:248
  9.0 5.0 %copy-start.9 = (bf16[1,36,2176]{2,1,0:T(8,128)(2,1)S(1)}, bf16[1,36,2176]{2,1,0:T(8,128)(2,1)}, u32[]{:S(2)}) copy-start(bf16[1,36,2176]{2,1,0:T(8,128)(2,1)} %param.12) | copy-start | bytes 470020
  9.0 117.8 %all-gather.5.cloned.1.call-start = ((), (), s32[]{:S(2)}) async-start(), calls=%async_computation.5 | async-start | bytes 5640192 | tf_op jit(solution)/shard_map/all_gather | solution.py:269
  14.0 14.6 %collective-permute-start.1 = (bf16[36,2176]{1,0:T(8,128)(2,1)S(1)}, bf16[36,2176]{1,0:T(8,128)(2,1)S(1)}, u32[]{:S(2)}, u32[]{:S(2)}) collective-permute-start(bf16[36,2176]{1,0:T(8,128)(2,1)S(1)} %bitcast.46), channel_id=1, source_target_pairs={{2,0},{3,1},{0,2},{1,3},{6,4},{7,5},{4,6},{5,7},{10,8},{11,9},{8,1... | collective-permute-start | bytes 470024 | tf_op jit(solution)/shard_map/ppermute | solution.py:21
  21.8 16.3 %collective-permute-start.2 = (bf16[36,2176]{1,0:T(8,128)(2,1)S(1)}, bf16[36,2176]{1,0:T(8,128)(2,1)S(1)}, u32[]{:S(2)}, u32[]{:S(2)}) collective-permute-start(bf16[36,2176]{1,0:T(8,128)(2,1)S(1)} %bitcast.47), channel_id=1, source_target_pairs={{1,0},{2,1},{3,2},{0,3},{5,4},{6,5},{7,6},{4,7},{9,8},{10,9},{11,1... | collective-permute-start | bytes 470024 | tf_op jit(solution)/shard_map/ppermute | solution.py:21
  24.0 14.0 %collective-permute-start = (bf16[36,2176]{1,0:T(8,128)(2,1)S(1)}, bf16[36,2176]{1,0:T(8,128)(2,1)S(1)}, u32[]{:S(2)}, u32[]{:S(2)}) collective-permute-start(bf16[36,2176]{1,0:T(8,128)(2,1)S(1)} %bitcast.48), channel_id=1, source_target_pairs={{3,0},{0,1},{1,2},{2,3},{7,4},{4,5},{5,6},{6,7},{11,8},{8,9},{9,10... | collective-permute-start | bytes 470024 | tf_op jit(solution)/shard_map/ppermute | solution.py:21
  28.5 15.3 %copy-start.4 = (bf16[1,16,32,1152]{3,2,1,0:T(8,128)(2,1)S(1)}, bf16[1,16,32,1152]{3,2,1,0:T(8,128)(2,1)}, u32[]{:S(2)}) copy-start(bf16[1,16,32,1152]{3,2,1,0:T(8,128)(2,1)} %param.9) | copy-start | bytes 3538948
  39.1 14.6 %all-to-all-start = ((f32[4,16,704]{2,1,0:T(8,128)}), f32[4,16,704]{2,1,0:T(8,128)S(1)}, u32[]{:S(2)}, u32[]{:S(2)}) async-start(f32[4,16,704]{2,1,0:T(8,128)} %reshape.128), calls=%async_computation | async-start | bytes 393216 | tf_op jit(solution)/shard_map/all_to_all | solution.py:205
  58.3 1.4 copy-start.2
  61.7 45.9 %all-to-all-start.1 = ((bf16[4,192,1152]{2,1,0:T(8,128)(2,1)}), bf16[4,192,1152]{2,1,0:T(8,128)(2,1)S(1)}, u32[]{:S(2)}, u32[]{:S(2)}) async-start(bf16[4,192,1152]{2,1,0:T(8,128)(2,1)} %shard_map.104), calls=%async_computation.1 | async-start | bytes 3538944 | tf_op jit(solution)/shard_map/all_to_all | solution.py:205
  107.8 1.1 copy-start.6
  108.5 1.3 copy-start.10
  108.5 1.5 copy-start.3
  108.9 5.6 %copy-start = (bf16[1,16,32,2176]{3,2,1,0:T(8,128)(2,1)S(1)}, bf16[1,16,32,2176]{3,2,1,0:T(8,128)(2,1)}, u32[]{:S(2)}) copy-start(bf16[1,16,32,2176]{3,2,1,0:T(8,128)(2,1)} %param.10) | copy-start | bytes 6684676
  111.2 11.7 %all-to-all-start.2 = ((bf16[4,16,704]{2,1,0:T(8,128)(2,1)}), bf16[4,16,704]{2,1,0:T(8,128)(2,1)S(1)}, u32[]{:S(2)}, u32[]{:S(2)}) async-start(bf16[4,16,704]{2,1,0:T(8,128)(2,1)} %bitcast.11), calls=%async_computation.2 | async-start | bytes 196608 | tf_op jit(solution)/shard_map/all_to_all | solution.py:205
  114.5 4.2 %copy-start.7 = (f32[64,1152]{1,0:T(8,128)S(1)}, f32[64,1152]{1,0:T(8,128)}, u32[]{:S(2)}) copy-start(f32[64,1152]{1,0:T(8,128)} %copy-done.6) | copy-start | bytes 884740
  121.4 5.5 %copy-start.5 = (f32[1,1152]{1,0:T(1,128)S(1)}, f32[1,1152]{1,0:T(1,128)}, u32[]{:S(2)}) copy-start(f32[1,1152]{1,0:T(1,128)} %multiplier_ref.1) | copy-start | bytes 13828
  125.4 1.4 copy-start.1
  126.9 13.6 %copy-start.8 = (bf16[1,16,1152]{2,1,0:T(8,128)(2,1)S(1)}, bf16[1,16,1152]{2,1,0:T(8,128)(2,1)}, u32[]{:S(2)}) copy-start(bf16[1,16,1152]{2,1,0:T(8,128)(2,1)} %param.14) | copy-start | bytes 110596
  134.0 19.7 %collective-permute-start.3 = (bf16[1,16,32,1152]{3,2,1,0:T(8,128)(2,1)S(1)}, bf16[1,16,32,1152]{3,2,1,0:T(8,128)(2,1)S(1)}, u32[]{:S(2)}, u32[]{:S(2)}) collective-permute-start(bf16[1,16,32,1152]{3,2,1,0:T(8,128)(2,1)S(1)} %bitcast.41), channel_id=1, source_target_pairs={{32,0},{64,32},{96,64},{128,96},{160,128},{192,160},{224,192},{256... | collective-permute-start | bytes 3538952 | tf_op jit(solution)/shard_map/ppermute | solution.py:21
  135.9 17.8 %all-to-all-start.3 = ((bf16[8,16,1152]{2,1,0:T(8,128)(2,1)}), bf16[8,16,1152]{2,1,0:T(8,128)(2,1)S(1)}, u32[]{:S(2)}, u32[]{:S(2)}) async-start(bf16[8,16,1152]{2,1,0:T(8,128)(2,1)} %bitcast.16), calls=%async_computation.3 | async-start | bytes 589824 | tf_op jit(solution)/shard_map/all_to_all | solution.py:345
Sparse Core Ops, SparseCore 0:
  10.1 48.1 all-gather.2
  61.0 64.0 all-gather.4

commit v9 on v7

--- a/solution.py
+++ b/solution.py
@@ -49,13 +49,9 @@
 def norm_backward(tokens, normed_grad, layernorm_multiplier):
     centered = tokens - jnp.mean(tokens, axis=-1, keepdims=True)
     inverse = lax.rsqrt(jnp.mean(centered * centered, axis=-1, keepdims=True) + EPSILON)
-    normal = centered * inverse
     scaled = normed_grad * layernorm_multiplier
-    return inverse * (
-        scaled
-        - jnp.mean(scaled, axis=-1, keepdims=True)
-        - normal * jnp.mean(scaled * normal, axis=-1, keepdims=True)
-    )
+    along = jnp.mean(scaled * centered, axis=-1, keepdims=True) * inverse * inverse
+    return inverse * (scaled - jnp.mean(scaled, axis=-1, keepdims=True) - centered * along)
 
 
 def partial_kernel(images, means_ref, blocks_ref, own_ref, sent_ref):
@@ -101,7 +97,7 @@
 
 
 def slope_kernel(preact_ref, slope_ref):
-    slope_ref[...] = gelu_slope(preact_ref[...].astype(jnp.float32))
+    slope_ref[...] = gelu_slope(preact_ref[...].astype(jnp.float32)).astype(jnp.bfloat16)
 
 
 def slopes(preact):
@@ -113,10 +109,10 @@
         grid=(tokens // block,),
         in_specs=[spec],
         out_specs=spec,
-        out_shape=jax.ShapeDtypeStruct((tokens, hidden), jnp.float32),
+        out_shape=jax.ShapeDtypeStruct((tokens, hidden), jnp.bfloat16),
         compiler_params=pltpu.CompilerParams(vmem_limit_bytes=VMEM_BYTES),
         cost_estimate=pl.CostEstimate(
-            flops=20 * tokens * hidden, bytes_accessed=6 * tokens * hidden, transcendentals=0
+            flops=20 * tokens * hidden, bytes_accessed=4 * tokens * hidden, transcendentals=0
         ),
     )(preact)
 
@@ -137,7 +133,7 @@
     patches = rows // count
     hidden = hidden_ref.shape[2]
     grads = hidden_ref[step]
-    slope = slope_ref[...].reshape(count, patches, hidden)
+    slope = slope_ref[...].astype(jnp.float32).reshape(count, patches, hidden)
     preact_grad = (grads[:, None, :] * slope).astype(jnp.bfloat16).reshape(rows, hidden)
     normed = lax.dot_general(
         preact_grad, up_ref[...], (((1,), (1,)), ((), ())), preferred_element_type=jnp.float32

time: 162 us -> 162 us (level)
    unnamed x23 -> x15, local copies, waits for them, and re-layouts: 3.28 us -> 4.74 us
  transfers between devices with their start and end apart: 10 -> 10, of which waited for: 8 -> 8; matrix products, arithmetic and copies ran while one was open for 7% -> 6% of each run, Pallas kernels for 4% -> 5%
where the time goes in v9:
time: 162 us; the launch traced here: 161 us
  waiting for transfers between devices  76.1 us (47%)
  starting transfers between devices  36.4 us (22%)
  between operations  16.2 us (10%)
  Pallas kernels  14.9 us (9%)
  other arithmetic  8.17 us (5%)
  local copies, waits for them, and re-layouts  6.68 us (4%)
  matrix products  1.97 us (1%)
    all_to_all x3, waiting for transfers between devices, exchange_y(): return lax.all_to_all(blocks, 'y', 0, 0)  48 us
    ppermute x4, starting transfers between devices, from_ahead(): lax.ppermute(array, axis, [((i + by) % peers, i) for i in range(peers)])  17.6 us
    all_to_all x3, starting transfers between devices, exchange_y(): return lax.all_to_all(blocks, 'y', 0, 0)  14.6 us
    all_to_all x1, waiting for transfers between devices, per_device(): lax.all_to_all(column_sums.reshape(z_size, images, model_width), 'z', 0, 0)  11.9 us
    ppermute x4, waiting for transfers between devices, from_ahead(): lax.ppermute(array, axis, [((i + by) % peers, i) for i in range(peers)])  9.52 us
    pallas_call x1, Pallas kernels, span(): pl.pallas_call(functools.partial(span_kernel, pieces), grid=(count // row...  7.36 us
    unnamed x15, local copies, waits for them, and re-layouts  4.74 us
    all_gather x1, waiting for transfers between devices, per_device(): blocks = lax.all_gather(block, 'z', axis=0, tiled=True)  4.56 us
  transfers between devices with their start and end apart: 10, of which 8 were waited for; matrix products, arithmetic and copies ran while one was open for 6% of the time, Pallas kernels for 5%

profile of v9, /device:TPU:6, one launch (start us, length us, event | category | flops | bytes accessed | tf_op | source)
XLA Modules:
  0.0 160.5 jit_solution(17659663899140760483)
XLA Ops:
  7.2 0.0 all-gather.3.cloned.1.call-start
  7.2 0.1 pad.11.clone
  7.3 1.7 %maximum_maximum_fusion = bf16[88,1152]{1,0:T(8,128)(2,1)} fusion(bf16[68,1152]{1,0:T(8,128)(2,1)} %bitcast.50, bf16[16,1152]{1,0:T(8,128)(2,1)} %bitcast.45, bf16[88]{0:T(256)(128)(2,1)S(1)} %pad.11.clone), kind=kLoop, calls=%fused_computation.31 | loop fusion | flops 608256 | bytes 396464 | tf_op jit(solution)/shard_map/concatenate | solution.py:217
  9.0 0.0 all-gather.3.cloned.1.call-update
  9.0 0.0 copy-start.6
  9.0 0.0 all-gather.5.cloned.1.call-start
  9.1 3.5 %convert_reduce_fusion = f32[16,2176]{1,0:T(8,128)S(1)} fusion(bf16[1,16,32,2176]{3,2,1,0:T(8,128)(2,1)} %param.10), kind=kLoop, calls=%fused_computation.10 | loop fusion | flops 13334528 | bytes 2367488 | tf_op jit(solution)/shard_map/reduce_sum | solution.py:230
  12.6 0.4 div.25
  13.0 0.2 pad_bitcast_fusion
  13.2 0.8 reshape.128
  14.0 0.0 copy-done.6
  14.0 7.7 %collective-permute-start.1 = (bf16[36,2176]{1,0:T(8,128)(2,1)S(1)}, bf16[36,2176]{1,0:T(8,128)(2,1)S(1)}, u32[]{:S(2)}, u32[]{:S(2)}) collective-permute-start(bf16[36,2176]{1,0:T(8,128)(2,1)S(1)} %bitcast.46), channel_id=1, source_target_pairs={{2,0},{3,1},{0,2},{1,3},{6,4},{7,5},{4,6},{5,7},{10,8},{11,9},{8,1... | collective-permute-start | bytes 470024 | tf_op jit(solution)/shard_map/ppermute | solution.py:21
  21.8 2.2 %collective-permute-start.2 = (bf16[36,2176]{1,0:T(8,128)(2,1)S(1)}, bf16[36,2176]{1,0:T(8,128)(2,1)S(1)}, u32[]{:S(2)}, u32[]{:S(2)}) collective-permute-start(bf16[36,2176]{1,0:T(8,128)(2,1)S(1)} %bitcast.47), channel_id=1, source_target_pairs={{1,0},{2,1},{3,2},{0,3},{5,4},{6,5},{7,6},{4,7},{9,8},{10,9},{11,1... | collective-permute-start | bytes 470024 | tf_op jit(solution)/shard_map/ppermute | solution.py:21
  24.0 4.5 %collective-permute-start = (bf16[36,2176]{1,0:T(8,128)(2,1)S(1)}, bf16[36,2176]{1,0:T(8,128)(2,1)S(1)}, u32[]{:S(2)}, u32[]{:S(2)}) collective-permute-start(bf16[36,2176]{1,0:T(8,128)(2,1)S(1)} %bitcast.48), channel_id=1, source_target_pairs={{3,0},{0,1},{1,2},{2,3},{7,4},{4,5},{5,6},{6,7},{11,8},{8,9},{9,10... | collective-permute-start | bytes 470024 | tf_op jit(solution)/shard_map/ppermute | solution.py:21
  28.5 0.0 copy-start.3
  28.6 0.1 collective-permute-done.1
  28.7 9.4 %collective-permute-done.2 = bf16[36,2176]{1,0:T(8,128)(2,1)S(1)} collective-permute-done((bf16[36,2176]{1,0:T(8,128)(2,1)S(1)}, bf16[36,2176]{1,0:T(8,128)(2,1)S(1)}, u32[]{:S(2)}, u32[]{:S(2)}) %collective-permute-start.2) | collective-permute-done | bytes 156704 | tf_op jit(solution)/shard_map/ppermute | solution.py:21
  38.1 0.0 collective-permute-done
  38.1 0.1 select_select_fusion.3
  38.2 0.9 pad_maximum_fusion
  39.1 0.0 all-gather.5.cloned.1.call-update
  39.1 4.5 %all-to-all-start = ((f32[4,16,704]{2,1,0:T(8,128)}), f32[4,16,704]{2,1,0:T(8,128)S(1)}, u32[]{:S(2)}, u32[]{:S(2)}) async-start(f32[4,16,704]{2,1,0:T(8,128)} %reshape.128), calls=%async_computation | async-start | bytes 393216 | tf_op jit(solution)/shard_map/all_to_all | solution.py:182
  43.7 0.1 broadcast_in_dim.54
  43.8 0.1 broadcast_in_dim.55
  43.8 0.0 copy-done.3
  43.8 0.3 convert_reduce_fusion.1
  44.1 0.1 bitcast_select_fusion.own_ref
  44.2 9.5 %all-to-all-done = f32[4,16,704]{2,1,0:T(8,128)S(1)} async-done(((f32[4,16,704]{2,1,0:T(8,128)}), f32[4,16,704]{2,1,0:T(8,128)S(1)}, u32[]{:S(2)}, u32[]{:S(2)}) %all-to-all-start) | async-done | bytes 180256 | tf_op jit(solution)/shard_map/all_to_all | solution.py:182
  53.8 4.6 %all-gather.3.cloned.1.call-done.blocks_ref = bf16[704,1152]{1,0:T(8,128)(2,1)} async-done(((bf16[88,1152]{1,0:T(8,128)(2,1)}), bf16[704,1152]{1,0:T(8,128)(2,1)}) %all-gather.3.cloned.1.call-update) | async-done | bytes 1622032 | tf_op jit(solution)/shard_map/all_gather | solution.py:225
  58.3 1.4 copy-done.1
  59.7 2.0 %shard_map.104 = bf16[4,192,1152]{2,1,0:T(8,128)(2,1)} custom-call(f32[64,704]{1,0:T(8,128)S(1)} %bitcast.41, bf16[704,1152]{1,0:T(8,128)(2,1)S(1)} %copy-done.1, f32[64,1152]{1,0:T(8,128)S(1)} %bitcast_select_fusion.own_ref), custom_call_target="tpu_custom_call" | custom-call | flops 207618048 | bytes 2000000 | tf_op jit(solution)/shard_map/pallas_call | solution.py:89
  61.7 6.7 %all-to-all-start.1 = ((bf16[4,192,1152]{2,1,0:T(8,128)(2,1)}), bf16[4,192,1152]{2,1,0:T(8,128)(2,1)S(1)}, u32[]{:S(2)}, u32[]{:S(2)}) async-start(bf16[4,192,1152]{2,1,0:T(8,128)(2,1)} %shard_map.104), calls=%async_computation.1 | async-start | bytes 3538944 | tf_op jit(solution)/shard_map/all_to_all | solution.py:182
  69.8 0.1 iota_add_fusion
  69.9 0.1 add.112
  70.6 0.1 iota_add_fusion.1
  70.7 0.1 add.107
  70.8 36.9 %all-to-all-done.1 = bf16[4,192,1152]{2,1,0:T(8,128)(2,1)S(1)} async-done(((bf16[4,192,1152]{2,1,0:T(8,128)(2,1)}), bf16[4,192,1152]{2,1,0:T(8,128)(2,1)S(1)}, u32[]{:S(2)}, u32[]{:S(2)}) %all-to-all-start.1) | async-done | bytes 1769504 | tf_op jit(solution)/shard_map/all_to_all | solution.py:182
  107.6 0.1 slice.9
  107.7 0.1 convert_reduce_fusion.2
  107.8 0.1 multiply_reduce_fusion.1
  107.9 0.5 fusion.13
  108.5 0.0 copy-start.2
  108.5 0.4 multiply_reduce_fusion
  108.9 0.1 fusion.21
  109.1 0.9 copy-done.2
  109.9 1.3 shard_map.105
  111.2 3.3 %all-to-all-start.2 = ((bf16[4,16,704]{2,1,0:T(8,128)(2,1)}), bf16[4,16,704]{2,1,0:T(8,128)(2,1)S(1)}, u32[]{:S(2)}, u32[]{:S(2)}) async-start(bf16[4,16,704]{2,1,0:T(8,128)(2,1)} %bitcast.11), calls=%async_computation.2 | async-start | bytes 196608 | tf_op jit(solution)/shard_map/all_to_all | solution.py:182
  114.5 0.0 copy-start.4
  114.5 4.3 %shard_map.106.slope_ref = bf16[512,2176]{1,0:T(8,128)(2,1)S(1)} custom-call(bf16[512,2176]{1,0:T(8,128)(2,1)} %bitcast.42), custom_call_target="tpu_custom_call" | custom-call | flops 22282240 | bytes 4456448 | tf_op jit(solution)/shard_map/pallas_call | solution.py:107
  118.8 0.0 copy-start
  118.9 1.4 copy-done
  120.3 1.0 convolution_convert_fusion
  121.3 1.7 %all-to-all-done.2.grad_ref = bf16[4,16,704]{2,1,0:T(8,128)(2,1)S(1)} async-done(((bf16[4,16,704]{2,1,0:T(8,128)(2,1)}), bf16[4,16,704]{2,1,0:T(8,128)(2,1)S(1)}, u32[]{:S(2)}, u32[]{:S(2)}) %all-to-all-start.2) | async-done | bytes 90144 | tf_op jit(solution)/shard_map/all_to_all | solution.py:182
  122.9 2.1 %all-gather.5.cloned.1.call-done.up_ref = bf16[1152,2176]{1,0:T(8,128)(2,1)} async-done(((bf16[144,2176]{1,0:T(8,128)(2,1)}), bf16[1152,2176]{1,0:T(8,128)(2,1)}) %all-gather.5.cloned.1.call-update) | async-done | bytes 5013520 | tf_op jit(solution)/shard_map/all_gather | solution.py:246
  125.0 7.4 %shard_map.107 = bf16[512,1152]{1,0:T(8,128)(2,1)S(1)} custom-call(bf16[4,16,704]{2,1,0:T(8,128)(2,1)S(1)} %all-to-all-done.2.grad_ref, bf16[512,2176]{1,0:T(8,128)(2,1)} %copy-done, bf16[1152,2176]{1,0:T(8,128)(2,1)} %all-gather.5.cloned.1.call-done.up_ref, bf16[512,1152]{1,0:T(8,128)(2,1)S(1)} %bitcast.39, ...), custom_call_target="tpu_custom_call" | custom-call | flops 2566914048 | bytes 11829248 | tf_op jit(solution)/shard_map/pallas_call | solution.py:158
  132.4 3.1 %collective-permute-start.3 = (bf16[1,16,32,1152]{3,2,1,0:T(8,128)(2,1)S(1)}, bf16[1,16,32,1152]{3,2,1,0:T(8,128)(2,1)S(1)}, u32[]{:S(2)}, u32[]{:S(2)}) collective-permute-start(bf16[1,16,32,1152]{3,2,1,0:T(8,128)(2,1)S(1)} %bitcast.40), channel_id=1, source_target_pairs={{32,0},{64,32},{96,64},{128,96},{160,128},{192,160},{224,192},{256... | collective-permute-start | bytes 3538952 | tf_op jit(solution)/shard_map/ppermute | solution.py:21
  135.5 4.2 %all-to-all-start.3 = ((bf16[8,16,1152]{2,1,0:T(8,128)(2,1)}), bf16[8,16,1152]{2,1,0:T(8,128)(2,1)S(1)}, u32[]{:S(2)}, u32[]{:S(2)}) async-start(bf16[8,16,1152]{2,1,0:T(8,128)(2,1)} %bitcast.16), calls=%async_computation.3 | async-start | bytes 589824 | tf_op jit(solution)/shard_map/all_to_all | solution.py:324
  139.7 0.0 copy-done.5
  139.7 0.1 fusion.14
  139.8 11.9 %all-to-all-done.3 = bf16[8,16,1152]{2,1,0:T(8,128)(2,1)S(1)} async-done(((bf16[8,16,1152]{2,1,0:T(8,128)(2,1)}), bf16[8,16,1152]{2,1,0:T(8,128)(2,1)S(1)}, u32[]{:S(2)}, u32[]{:S(2)}) %all-to-all-start.3) | async-done | bytes 294944 | tf_op jit(solution)/shard_map/all_to_all | solution.py:324
  151.7 0.0 collective-permute-done.3
  151.8 0.2 fusion.16
  152.0 0.7 fusion.18
  152.7 1.0 copy.16
  (15 shorter events, 0.1 us)
Async XLA Ops:
  7.2 51.1 %all-gather.3.cloned.1.call-start = ((), (), s32[]{:S(2)}) async-start(), calls=%async_computation.4 | async-start | bytes 1824768 | tf_op jit(solution)/shard_map/all_gather | solution.py:225
  9.0 5.0 %copy-start.6 = (bf16[1,36,2176]{2,1,0:T(8,128)(2,1)S(1)}, bf16[1,36,2176]{2,1,0:T(8,128)(2,1)}, u32[]{:S(2)}) copy-start(bf16[1,36,2176]{2,1,0:T(8,128)(2,1)} %param.12) | copy-start | bytes 470020
  9.0 116.0 %all-gather.5.cloned.1.call-start = ((), (), s32[]{:S(2)}) async-start(), calls=%async_computation.5 | async-start | bytes 5640192 | tf_op jit(solution)/shard_map/all_gather | solution.py:246
  14.0 14.6 %collective-permute-start.1 = (bf16[36,2176]{1,0:T(8,128)(2,1)S(1)}, bf16[36,2176]{1,0:T(8,128)(2,1)S(1)}, u32[]{:S(2)}, u32[]{:S(2)}) collective-permute-start(bf16[36,2176]{1,0:T(8,128)(2,1)S(1)} %bitcast.46), channel_id=1, source_target_pairs={{2,0},{3,1},{0,2},{1,3},{6,4},{7,5},{4,6},{5,7},{10,8},{11,9},{8,1... | collective-permute-start | bytes 470024 | tf_op jit(solution)/shard_map/ppermute | solution.py:21
  21.8 16.3 %collective-permute-start.2 = (bf16[36,2176]{1,0:T(8,128)(2,1)S(1)}, bf16[36,2176]{1,0:T(8,128)(2,1)S(1)}, u32[]{:S(2)}, u32[]{:S(2)}) collective-permute-start(bf16[36,2176]{1,0:T(8,128)(2,1)S(1)} %bitcast.47), channel_id=1, source_target_pairs={{1,0},{2,1},{3,2},{0,3},{5,4},{6,5},{7,6},{4,7},{9,8},{10,9},{11,1... | collective-permute-start | bytes 470024 | tf_op jit(solution)/shard_map/ppermute | solution.py:21
  24.0 14.0 %collective-permute-start = (bf16[36,2176]{1,0:T(8,128)(2,1)S(1)}, bf16[36,2176]{1,0:T(8,128)(2,1)S(1)}, u32[]{:S(2)}, u32[]{:S(2)}) collective-permute-start(bf16[36,2176]{1,0:T(8,128)(2,1)S(1)} %bitcast.48), channel_id=1, source_target_pairs={{3,0},{0,1},{1,2},{2,3},{7,4},{4,5},{5,6},{6,7},{11,8},{8,9},{9,10... | collective-permute-start | bytes 470024 | tf_op jit(solution)/shard_map/ppermute | solution.py:21
  28.5 15.3 %copy-start.3 = (bf16[1,16,32,1152]{3,2,1,0:T(8,128)(2,1)S(1)}, bf16[1,16,32,1152]{3,2,1,0:T(8,128)(2,1)}, u32[]{:S(2)}) copy-start(bf16[1,16,32,1152]{3,2,1,0:T(8,128)(2,1)} %param.9) | copy-start | bytes 3538948
  39.1 14.6 %all-to-all-start = ((f32[4,16,704]{2,1,0:T(8,128)}), f32[4,16,704]{2,1,0:T(8,128)S(1)}, u32[]{:S(2)}, u32[]{:S(2)}) async-start(f32[4,16,704]{2,1,0:T(8,128)} %reshape.128), calls=%async_computation | async-start | bytes 393216 | tf_op jit(solution)/shard_map/all_to_all | solution.py:182
  58.3 1.4 copy-start.1
  61.7 45.9 %all-to-all-start.1 = ((bf16[4,192,1152]{2,1,0:T(8,128)(2,1)}), bf16[4,192,1152]{2,1,0:T(8,128)(2,1)S(1)}, u32[]{:S(2)}, u32[]{:S(2)}) async-start(bf16[4,192,1152]{2,1,0:T(8,128)(2,1)} %shard_map.104), calls=%async_computation.1 | async-start | bytes 3538944 | tf_op jit(solution)/shard_map/all_to_all | solution.py:182
  108.5 1.5 copy-start.2
  111.2 11.7 %all-to-all-start.2 = ((bf16[4,16,704]{2,1,0:T(8,128)(2,1)}), bf16[4,16,704]{2,1,0:T(8,128)(2,1)S(1)}, u32[]{:S(2)}, u32[]{:S(2)}) async-start(bf16[4,16,704]{2,1,0:T(8,128)(2,1)} %bitcast.11), calls=%async_computation.2 | async-start | bytes 196608 | tf_op jit(solution)/shard_map/all_to_all | solution.py:182
  114.5 10.5 %copy-start.4 = (f32[1,1152]{1,0:T(1,128)S(1)}, f32[1,1152]{1,0:T(1,128)}, u32[]{:S(2)}) copy-start(f32[1,1152]{1,0:T(1,128)} %multiplier_ref.1) | copy-start | bytes 13828
  118.8 1.4 copy-start
  125.0 14.6 %copy-start.5 = (bf16[1,16,1152]{2,1,0:T(8,128)(2,1)S(1)}, bf16[1,16,1152]{2,1,0:T(8,128)(2,1)}, u32[]{:S(2)}) copy-start(bf16[1,16,1152]{2,1,0:T(8,128)(2,1)} %param.14) | copy-start | bytes 110596
  132.4 19.3 %collective-permute-start.3 = (bf16[1,16,32,1152]{3,2,1,0:T(8,128)(2,1)S(1)}, bf16[1,16,32,1152]{3,2,1,0:T(8,128)(2,1)S(1)}, u32[]{:S(2)}, u32[]{:S(2)}) collective-permute-start(bf16[1,16,32,1152]{3,2,1,0:T(8,128)(2,1)S(1)} %bitcast.40), channel_id=1, source_target_pairs={{32,0},{64,32},{96,64},{128,96},{160,128},{192,160},{224,192},{256... | collective-permute-start | bytes 3538952 | tf_op jit(solution)/shard_map/ppermute | solution.py:21
  135.5 16.2 %all-to-all-start.3 = ((bf16[8,16,1152]{2,1,0:T(8,128)(2,1)}), bf16[8,16,1152]{2,1,0:T(8,128)(2,1)S(1)}, u32[]{:S(2)}, u32[]{:S(2)}) async-start(bf16[8,16,1152]{2,1,0:T(8,128)(2,1)} %bitcast.16), calls=%async_computation.3 | async-start | bytes 589824 | tf_op jit(solution)/shard_map/all_to_all | solution.py:324
Sparse Core Ops, SparseCore 0:
  10.1 48.1 all-gather.2
  61.0 64.0 all-gather.4
